TPU v7x, 32 devices: a whole 2x2x4 slice. The times are simulated.
32 devices in a mesh: ctx: 4 (over z), exp: 4 (over y, x), tp: 2 (over core).
Axes of the slice: x: 2, y: 2, z: 4, core: 2. Of those that a mesh axis runs over, the one named last changes fastest.
Arguments:
- queries: bfloat16 [16, 2, 4, 8, 128], P('ctx', 'tp', None, 'exp'), may hold values from -6 to 6
- keys: bfloat16 [128, 4, 128], P('ctx'), may hold values from -6 to 6
- values: bfloat16 [128, 4, 128], P('ctx'), may hold values from -6 to 6
- out_weight: bfloat16 [1024, 4096], P('exp'), may hold values from -0.1875 to 0.1875
- norm_gain: float32 [4096], replicated, may hold values from 0.5 to 1.5
- routes: int32 [128, 8], P(('ctx', 'exp', 'tp')), may hold values from 0 to 127, as said below
- route_weight: float32 [128, 8], P(('ctx', 'exp', 'tp')), may hold values from 0.05 to 1
- w_gate: bfloat16 [4, 4096, 384], P('exp', None, 'tp'), may hold values from -0.09375 to 0.09375
- w_up: bfloat16 [4, 4096, 384], P('exp', None, 'tp'), may hold values from -0.09375 to 0.09375
- w_down: bfloat16 [4, 384, 4096], P('exp', 'tp'), may hold values from -0.21875 to 0.21875
Outputs:
- layer_out: bfloat16 [128, 4096], P(('ctx', 'exp', 'tp'))
Inputs may be any that keep to these rules, and one draw needn't show every extreme that they name: `routes`: each row names 8 different experts. In each aligned block of 4 rows no expert is named by more than 2 rows, and some expert is named by exactly 2 rows.
All inputs are finite; a program needn't handle non-finite values.
Results may differ from a plain program's by a relative error of at most 0.025.
Values may be sent and summed in bfloat16 or wider, within the bound.
No kernel may reach another device: no remote copies, remote signals or barrier semaphores. Data moves between devices by JAX's collectives and lax.ppermute only.
A program may use at most 64 MiB of HBM per device.

v0:
```python
import jax
import jax.numpy as jnp
from jax import lax
from jax.sharding import PartitionSpec as P

CAP = 2


def silu_mul(gate, up):
    return gate / (1.0 + jnp.exp(-gate)) * up


def on_device(
    queries, keys, values, out_weight, norm_gain, routes, route_weight, w_gate, w_up, w_down
):
    blocks, lanes, rows, local_heads, head_dim = queries.shape
    width = out_weight.shape[1]
    n_exp = lax.axis_size("exp")
    n_tp = lax.axis_size("tp")
    live_count = n_exp // 2
    ctx_index = lax.axis_index("ctx")
    exp_index = lax.axis_index("exp")
    tp_index = lax.axis_index("tp")
    group = local_heads * n_exp // keys.shape[1]
    kv_head = exp_index * local_heads // group
    key_mine = lax.dynamic_index_in_dim(keys, kv_head, 1, keepdims=False)
    value_mine = lax.dynamic_index_in_dim(values, kv_head, 1, keepdims=False)
    query_rows = blocks * rows
    query_vector = queries.reshape(query_rows, local_heads, head_dim).transpose(1, 0, 2)
    block_ids = jnp.arange(blocks, dtype=jnp.int32)[:, None]
    inner = jnp.arange(rows, dtype=jnp.int32)[None, :]
    query_pos = (((ctx_index * blocks + block_ids) * n_tp + tp_index) * rows + inner).reshape(-1)
    score_scale = head_dim ** (-0.5)
    highest = jnp.full((local_heads, query_rows), -1e30, jnp.float32)
    key_portion = lax.all_gather(key_mine, "ctx", axis=0, tiled=True)
    value_portion = lax.all_gather(value_mine, "ctx", axis=0, tiled=True)
    logit_score = (
        jnp.einsum("qbr,zr->qbz", query_vector, key_portion, preferred_element_type=jnp.float32)
        * score_scale
    )
    key_pos = jnp.arange(key_portion.shape[0], dtype=jnp.int32)
    allowed = (key_pos[None, :] <= query_pos[:, None])[None, :, :]
    logit_score = jnp.where(allowed, logit_score, -1e30)
    new_high = jnp.maximum(highest, jnp.max(logit_score, axis=2))
    attention_probability = jnp.where(allowed, jnp.exp(logit_score - new_high[:, :, None]), 0.0)
    total = jnp.sum(attention_probability, axis=2)
    accum = jnp.einsum(
        "axt,ty->axy",
        attention_probability.astype(jnp.bfloat16),
        value_portion,
        preferred_element_type=jnp.float32,
    )
    highest, total, accum = (new_high, total, accum)
    mixed = (accum / total[:, :, None]).astype(jnp.bfloat16)
    mixed_rows = mixed.transpose(1, 0, 2).reshape(query_rows, local_heads * head_dim)
    summed = lax.psum_scatter(
        jnp.dot(mixed_rows, out_weight, preferred_element_type=jnp.float32).astype(jnp.bfloat16),
        "exp",
        scatter_dimension=0,
        tiled=True,
    )
    state_wide = summed.astype(jnp.float32)
    inverse = lax.rsqrt(jnp.mean(state_wide * state_wide, axis=1, keepdims=True) + 1e-06)
    normed = (state_wide * inverse * norm_gain[None, :]).astype(jnp.bfloat16)
    picks = routes.shape[1]
    flat = routes.reshape(-1)
    order = jnp.arange(flat.shape[0], dtype=jnp.int32)
    same = (flat[:, None] == flat[None, :]) & (order[None, :] < order[:, None])
    slot = jnp.sum(same.astype(jnp.int32), axis=1)
    target = jnp.where(flat < live_count, flat * CAP + slot, -1)
    slots = jnp.arange(live_count * CAP, dtype=jnp.int32)
    hit = (
        (target[None, :] == slots[:, None])
        .astype(jnp.float32)
        .reshape(live_count * CAP, rows, picks)
    )
    pick = jnp.sum(hit, axis=2).astype(jnp.bfloat16)
    buffer = (
        jnp.dot(pick, normed, preferred_element_type=jnp.float32)
        .astype(jnp.bfloat16)
        .reshape(live_count, CAP, width)
    )
    share = route_weight / jnp.sum(route_weight, axis=1, keepdims=True)
    mix = jnp.sum(hit * share[None, :, :], axis=2).T
    outgoing = jnp.broadcast_to(buffer[None, :, None], (2, live_count, n_tp, CAP, width)).reshape(
        n_exp * n_tp, CAP, width
    )
    received = lax.all_to_all(outgoing, ("exp", "tp"), split_axis=0, concat_axis=0, tiled=True)
    flat_rows = received.reshape(-1, width)
    gate = jnp.dot(flat_rows, w_gate[0], preferred_element_type=jnp.float32)
    up = jnp.dot(flat_rows, w_up[0], preferred_element_type=jnp.float32)
    hidden = silu_mul(gate, up).astype(jnp.bfloat16)
    result = jnp.dot(hidden, w_down[0], preferred_element_type=jnp.float32).astype(jnp.bfloat16)
    returned = lax.all_to_all(
        result.reshape(received.shape), ("exp", "tp"), split_axis=0, concat_axis=0, tiled=True
    )
    expert_output_rows = jnp.sum(
        returned.astype(jnp.float32).reshape(2, live_count, n_tp, CAP, width), axis=(0, 2)
    )
    moe = jnp.dot(
        mix,
        expert_output_rows.reshape(live_count * CAP, width),
        precision=lax.Precision.HIGHEST,
        preferred_element_type=jnp.float32,
    )
    return (state_wide + moe).astype(jnp.bfloat16)


def solution(mesh):
    in_specs = (
        P("ctx", "tp", None, "exp", None),
        P("ctx", None, None),
        P("ctx", None, None),
        P("exp", None),
        P(),
        P(("ctx", "exp", "tp"), None),
        P(("ctx", "exp", "tp"), None),
        P("exp", None, "tp"),
        P("exp", None, "tp"),
        P("exp", "tp", None),
    )
    out_specs = P(("ctx", "exp", "tp"), None)
    return jax.shard_map(
        on_device, mesh=mesh, in_specs=in_specs, out_specs=out_specs, check_vma=False
    )
```

profile of v0, /device:TPU:0, one launch (start us, length us, event | category | flops | bytes accessed | tf_op | source)
XLA Modules:
  0.0 114.3 jit_solution(9184538001288642870)
XLA Ops:
  6.5 0.0 all-reduce.3.cloned.1.call-start
  6.6 0.1 iota_add_fusion
  6.7 0.1 add.81
  6.8 0.1 iota_compare_fusion.2
  6.9 1.0 constant_dynamic-slice_fusion.1
  7.8 0.8 constant_dynamic-slice_fusion
  8.6 14.8 %all-gather.1 = bf16[128,1,128]{2,0,1:T(8,128)(2,1)S(1)} all-gather(bf16[32,1,128]{2,0,1:T(8,128)(2,1)S(1)} %copy.27), channel_id=3, replica_groups=mesh['ctx'=4,'exp'=4,'tp'=2] {'ctx'}, dimensions={0}, use_global_device_ids=true | all-gather | bytes 40960 | tf_op jit(solution)/shard_map/all_gather | solution.py:36
  23.4 13.1 %all-gather = bf16[128,1,128]{2,0,1:T(8,128)(2,1)S(1)} all-gather(bf16[32,1,128]{2,0,1:T(8,128)(2,1)S(1)} %copy.26), channel_id=2, replica_groups=mesh['ctx'=4,'exp'=4,'tp'=2] {'ctx'}, dimensions={0}, use_global_device_ids=true | all-gather | bytes 40960 | tf_op jit(solution)/shard_map/all_gather | solution.py:35
  36.6 0.9 fusion.48
  37.5 0.2 fusion.33
  37.7 0.2 fusion.18
  37.9 1.0 convolution_convert_fusion.1
  39.0 0.1 eq.29
  39.1 0.2 convert_reduce_fusion.1
  39.2 0.1 reduce_sum.67
  39.3 0.1 reduce_sum.68
  39.5 0.1 broadcast_divide_fusion
  39.5 0.6 dynamic-slice
  40.8 0.1 convert_reduce_fusion.2
  40.9 41.2 %all-reduce.3.cloned.1.call-done = bf16[16,4096]{1,0:T(8,128)(2,1)} async-done(((bf16[16,4096]{1,0:T(8,128)(2,1)}), bf16[16,4096]{1,0:T(8,128)(2,1)}) %all-reduce.3.cloned.1.call-update) | async-done | bytes 131088
  82.1 1.0 fusion.19
  83.1 1.1 convolution_convert_fusion.2
  84.2 0.1 broadcast_in_dim.52
  84.3 8.1 %all_to_all.10 = bf16[8,2,4096]{2,1,0:T(2,128)(2,1)S(1)} all-to-all(bf16[8,2,4096]{2,1,0:T(2,128)(2,1)S(1)} %bitcast.59), channel_id=1, replica_groups=mesh['ctx'=4,'exp'=4,'tp'=2] {'exp','tp'}, dimensions={0} | all-to-all | bytes 262144 | tf_op jit(solution)/shard_map/all_to_all | solution.py:88
  92.3 0.1 reshape.111
  92.4 1.9 %fusion.4 = f32[16,192]{1,0:T(8,128)S(1)} fusion(bf16[16,4096]{1,0:T(8,128)(2,1)S(1)} %reshape.111, bf16[1,4096,192]{1,2,0:T(8,128)(2,1)} %param.17), kind=kOutput, calls=%fused_computation.8 | convolution fusion | flops 25165824 | bytes 1716224 | tf_op jit(solution)/shard_map/dot_general | solution.py:90
  94.3 3.1 %convolution_convert_fusion = bf16[16,4096]{1,0:T(8,128)(2,1)S(1)} fusion(bf16[1,192,4096]{2,1,0:T(8,128)(2,1)} %param.19, bf16[16,4096]{1,0:T(8,128)(2,1)S(1)} %reshape.111, bf16[1,4096,192]{1,2,0:T(8,128)(2,1)} %param.18, f32[16,192]{1,0:T(8,128)S(1)} %fusion.4), kind=kOutput, calls=%fused_computation | convolution fusion | flops 50412544 | bytes 3420160 | tf_op jit(solution)/shard_map/dot_general | solution.py:93
  97.4 0.1 reshape.112
  97.6 7.9 %all_to_all.11 = bf16[8,2,4096]{2,1,0:T(2,128)(2,1)S(1)} all-to-all(bf16[8,2,4096]{2,1,0:T(2,128)(2,1)S(1)} %reshape.112), channel_id=1, replica_groups=mesh['ctx'=4,'exp'=4,'tp'=2] {'exp','tp'}, dimensions={0} | all-to-all | bytes 262144 | tf_op jit(solution)/shard_map/all_to_all | solution.py:94
  105.5 0.1 convert_reduce_fusion
  105.6 0.1 reshape.115
  105.7 1.8 %fusion = bf16[4,4096]{1,0:T(4,128)(2,1)} fusion(f32[4,4]{1,0:T(4,128)S(1)} %get-tuple-element.6, f32[4,4096]{1,0:T(4,128)S(1)} %reshape.115, bf16[16,4096]{1,0:T(8,128)(2,1)} %all-reduce.3.cloned.1.call-done, u32[]{:T(128)S(6)} %multiply.7), kind=kOutput, calls=%fused_computation.3 | convolution fusion | flops 835584 | bytes 131140 | tf_op jit(solution)/shard_map/dot_general | solution.py:100
  (18 shorter events, 0.1 us)
Async XLA Ops:
  6.5 31.4 %copy-start = (bf16[256,4096]{1,0:T(8,128)(2,1)S(1)}, bf16[256,4096]{1,0:T(8,128)(2,1)}, u32[]{:S(2)}) copy-start(bf16[256,4096]{1,0:T(8,128)(2,1)} %param.13) | copy-start | bytes 6291460
  6.5 33.0 %copy-start.4 = (u32[32]{0:T(128)S(1)}, u32[32]{0:T(128)}, u32[]{:S(2)}) copy-start(u32[32]{0:T(128)} %constant.64) | copy-start | bytes 388
  6.5 32.4 %copy-start.1 = (s32[4,8]{1,0:T(4,128)S(1)}, s32[4,8]{1,0:T(4,128)}, u32[]{:S(2)}) copy-start(s32[4,8]{1,0:T(4,128)} %param.15) | copy-start | bytes 388
  6.5 32.8 %copy-start.2 = (f32[4,8]{1,0:T(4,128)S(1)}, f32[4,8]{1,0:T(4,128)}, u32[]{:S(2)}) copy-start(f32[4,8]{1,0:T(4,128)} %param.16) | copy-start | bytes 388
  6.5 76.6 %copy-start.3 = (f32[4096]{0:T(1024)S(1)}, f32[4096]{0:T(1024)}, u32[]{:S(2)}) copy-start(f32[4096]{0:T(1024)} %param.14) | copy-start | bytes 49156
  6.5 75.6 %all-reduce.3.cloned.1.call-start = ((), (), s32[]{:S(2)}) async-start(), calls=%async_computation.2 | async-start | bytes 262144
Sparse Core Ops, SparseCore 0:
  39.1 42.9 all-reduce.2
where the time goes:
time: 115 us; the launch traced here: 114 us
  blocking collectives  43.9 us (38%)
  waiting for transfers between devices  41.2 us (36%)
  between operations  14.2 us (12%)
  matrix products  10 us (9%)
  local copies, waits for them, and re-layouts  2.97 us (3%)
  other arithmetic  1.92 us (2%)
    unnamed x2, waiting for transfers between devices  41.2 us
    all_gather x1, blocking collectives, on_device(): value_portion = lax.all_gather(value_mine, 'ctx', axis=0, tiled=True)  14.8 us
    all_gather x1, blocking collectives, on_device(): key_portion = lax.all_gather(key_mine, 'ctx', axis=0, tiled=True)  13.1 us
    all_to_all x1, blocking collectives, on_device(): lax.all_to_all(outgoing, ('exp', 'tp'), split_axis=0, concat_axis=0, tile...  8.07 us
    all_to_all x1, blocking collectives, on_device(): lax.all_to_all(result.reshape(received.shape), ('exp', 'tp'), split_axis=...  7.92 us
    dot_general x1, matrix products, on_device(): jnp.dot(hidden, w_down[0], preferred_element_type=jnp.float32)  3.11 us
  transfers between devices with their start and end apart: 1, of which 1 were waited for; matrix products, arithmetic and copies ran while one was open for 1% of the time, Pallas kernels for 0%

commit v1 on v0

v1 whole, which is shorter than its diff:
```python
import jax
import jax.numpy as jnp
from jax import lax
from jax.sharding import PartitionSpec as P

CAP = 2


def silu_mul(gate, up):
    return gate / (1.0 + jnp.exp(-gate)) * up


def swap(x, axis, mask):
    size = lax.axis_size(axis)
    return lax.ppermute(x, axis, [(i, i ^ mask) for i in range(size)])


def swap_by_core(x, axis, masks):
    size, cores = lax.axis_size(axis), lax.axis_size("tp")
    pairs = [
        (i * cores + t, (i ^ masks[t % len(masks)]) * cores + t)
        for i in range(size)
        for t in range(cores)
    ]
    return lax.ppermute(x, (axis, "tp"), pairs)


def gather_ctx(x):
    size = lax.axis_size("ctx")
    first = lax.axis_index("tp") == 0
    got = [(0, x)]
    for low in range(1, size // 2):
        high = size - low
        mine = swap_by_core(x, "ctx", (low, high))
        got.append((jnp.where(first, low, high), mine))
        got.append((jnp.where(first, high, low), swap(mine, "tp", 1)))
    got.append((size // 2, swap(x, "ctx", size // 2)))
    return got


def on_device(
    queries, keys, values, out_weight, norm_gain, routes, route_weight, w_gate, w_up, w_down
):
    blocks, lanes, rows, local_heads, head_dim = queries.shape
    width = out_weight.shape[1]
    n_exp = lax.axis_size("exp")
    n_tp = lax.axis_size("tp")
    live_count = n_exp // 2
    ctx_index = lax.axis_index("ctx")
    exp_index = lax.axis_index("exp")
    tp_index = lax.axis_index("tp")
    group = local_heads * n_exp // keys.shape[1]
    kv_head = exp_index * local_heads // group
    span = keys.shape[0]
    key_mine = lax.dynamic_index_in_dim(keys, kv_head, 1, keepdims=False)
    value_mine = lax.dynamic_index_in_dim(values, kv_head, 1, keepdims=False)
    query_rows = blocks * rows
    query_vector = queries.reshape(query_rows, local_heads, head_dim).transpose(1, 0, 2)
    block_ids = jnp.arange(blocks, dtype=jnp.int32)[:, None]
    inner = jnp.arange(rows, dtype=jnp.int32)[None, :]
    query_pos = (((ctx_index * blocks + block_ids) * n_tp + tp_index) * rows + inner).reshape(-1)
    score_scale = head_dim ** (-0.5)

    got = gather_ctx(jnp.concatenate([key_mine, value_mine], axis=0))
    key_portion = jnp.concatenate([b[:span] for _, b in got], axis=0)
    value_portion = jnp.concatenate([b[span:] for _, b in got], axis=0)
    key_pos = jnp.concatenate(
        [(ctx_index ^ m) * span + jnp.arange(span, dtype=jnp.int32) for m, _ in got]
    )
    logit_score = (
        jnp.einsum("qbr,zr->qbz", query_vector, key_portion, preferred_element_type=jnp.float32)
        * score_scale
    )
    allowed = (key_pos[None, :] <= query_pos[:, None])[None, :, :]
    logit_score = jnp.where(allowed, logit_score, -1e30)
    high = jnp.max(logit_score, axis=2, keepdims=True)
    prob = jnp.where(allowed, jnp.exp(logit_score - high), 0.0)
    total = jnp.sum(prob, axis=2)
    accum = jnp.einsum(
        "axt,ty->axy",
        prob.astype(jnp.bfloat16),
        value_portion,
        preferred_element_type=jnp.float32,
    )
    mixed = (accum / total[:, :, None]).astype(jnp.bfloat16)
    mixed_rows = mixed.transpose(1, 0, 2).reshape(query_rows, local_heads * head_dim)
    term = jnp.dot(mixed_rows, out_weight, preferred_element_type=jnp.float32).astype(jnp.bfloat16)

    picks = routes.shape[1]
    flat = routes.reshape(-1)
    order = jnp.arange(flat.shape[0], dtype=jnp.int32)
    same = (flat[:, None] == flat[None, :]) & (order[None, :] < order[:, None])
    slot = jnp.sum(same.astype(jnp.int32), axis=1)
    target = jnp.where(flat < live_count, flat * CAP + slot, -1)
    slots = jnp.arange(live_count * CAP, dtype=jnp.int32)
    hit = (
        (target[None, :] == slots[:, None])
        .astype(jnp.float32)
        .reshape(live_count * CAP, rows, picks)
    )
    pick = jnp.sum(hit, axis=2).astype(jnp.bfloat16)
    share = route_weight / jnp.sum(route_weight, axis=1, keepdims=True)
    mix = jnp.sum(hit * share[None, :, :], axis=2).T

    pad = -(live_count * CAP) % 128
    note = jnp.pad(pick.T, ((0, 0), (0, pad)))
    note = jnp.where(
        (jnp.arange(blocks) == exp_index)[:, None, None], note[None], 0
    ).reshape(query_rows, -1)
    summed = jnp.concatenate([term, note], axis=1)
    steps = [1 << i for i in range(n_exp.bit_length() - 1)]
    for i, step in enumerate(steps):
        other = swap_by_core(summed, "exp", (step, steps[-1 - i]))
        summed = (summed.astype(jnp.float32) + other.astype(jnp.float32)).astype(jnp.bfloat16)
    state = summed[:, :width].astype(jnp.float32)
    note = summed[:, width : width + live_count * CAP]
    inverse = lax.rsqrt(jnp.mean(state * state, axis=1, keepdims=True) + 1e-06)
    normed = (state * inverse * norm_gain[None, :]).astype(jnp.bfloat16)
    expert = lax.rem(exp_index, live_count)
    note = lax.dynamic_slice_in_dim(note, expert * CAP, CAP, 1).reshape(blocks, rows, CAP)
    buffer = jnp.einsum(
        "brc,brd->bcd", note, normed.reshape(blocks, rows, width), preferred_element_type=jnp.float32
    ).astype(jnp.bfloat16)
    buffer = buffer.reshape(blocks * CAP, width)
    other = swap(buffer, "tp", 1)
    flat_rows = jnp.concatenate([buffer, other], axis=0)
    gate = jnp.dot(flat_rows, w_gate[0], preferred_element_type=jnp.float32)
    up = jnp.dot(flat_rows, w_up[0], preferred_element_type=jnp.float32)
    hidden = silu_mul(gate, up).astype(jnp.bfloat16)
    result = jnp.dot(hidden, w_down[0], preferred_element_type=jnp.float32).astype(jnp.bfloat16)
    result = result.reshape(n_tp, blocks, CAP, width)
    result = jnp.where(tp_index == 0, result, result[::-1]).transpose(1, 0, 2, 3)
    returned = lax.all_to_all(
        result.reshape(n_exp * n_tp, CAP, width), ("exp", "tp"), split_axis=0, concat_axis=0, tiled=True
    )
    expert_output_rows = jnp.sum(
        returned.astype(jnp.float32).reshape(2, live_count, n_tp, CAP, width), axis=(0, 2)
    )
    moe = jnp.dot(
        mix,
        expert_output_rows.reshape(live_count * CAP, width),
        precision=lax.Precision.HIGHEST,
        preferred_element_type=jnp.float32,
    )
    own = lax.dynamic_slice_in_dim(state, exp_index * rows, rows, 0)
    return (own + moe).astype(jnp.bfloat16)


def solution(mesh):
    in_specs = (
        P("ctx", "tp", None, "exp", None),
        P("ctx", None, None),
        P("ctx", None, None),
        P("exp", None),
        P(),
        P(("ctx", "exp", "tp"), None),
        P(("ctx", "exp", "tp"), None),
        P("exp", None, "tp"),
        P("exp", None, "tp"),
        P("exp", "tp", None),
    )
    out_specs = P(("ctx", "exp", "tp"), None)
    return jax.shard_map(
        on_device, mesh=mesh, in_specs=in_specs, out_specs=out_specs, check_vma=False
    )
```

time: 115 us -> 42.7 us (0.37)
  blocking collectives: 43.9 us -> 0 us
  waiting for transfers between devices: 41.2 us -> 14.9 us
  between operations: 14.2 us -> 0.19 us
  starting transfers between devices: 0.04 us -> 12.7 us
  matrix products: 10 us -> 7.78 us
  other arithmetic: 1.92 us -> 4.09 us
    unnamed x2 -> x0, waiting for transfers between devices: 41.2 us -> none
    all_gather x2 -> x0, blocking collectives: 27.9 us -> none  [the longest x1 14.8 us: on_device(): value_portion = lax.all_gather(value_mine, 'ctx', axis=0, tiled=True)]
    all_to_all x2 -> x0, blocking collectives: 16 us -> none  [the longest x1 8.07 us: on_device(): lax.all_to_all(outgoing, ('exp', 'tp'), split_axis=0, concat_axis=0, tile...]
    ppermute x0 -> x6, waiting for transfers between devices: none -> 9.38 us  [the longest x3 7.01 us: swap_by_core(): return lax.ppermute(x, (axis, 'tp'), pairs)]
    ppermute x0 -> x6, starting transfers between devices: none -> 8.93 us  [the longest x3 4.72 us: swap_by_core(): return lax.ppermute(x, (axis, 'tp'), pairs)]
    all_to_all x0 -> x1, waiting for transfers between devices: none -> 5.51 us  [on_device(): lax.all_to_all(result.reshape(n_exp * n_tp, CAP, width), ('exp', 'tp'), s...]
    all_to_all x0 -> x1, starting transfers between devices: none -> 3.72 us  [on_device(): lax.all_to_all(result.reshape(n_exp * n_tp, CAP, width), ('exp', 'tp'), s...]
    dot_general x4 -> x3, matrix products: 4.1 us -> 2.33 us  [the longest x1 1.91 us: on_device(): up = jnp.dot(flat_rows, w_up[0], preferred_element_type=jnp.float32)]
  transfers between devices with their start and end apart: 1 -> 7, of which waited for: 1 -> 5; matrix products, arithmetic and copies ran while one was open for 1% -> 10% of each run, Pallas kernels for 0% -> 0%
where the time goes in v1:
time: 42.7 us; the launch traced here: 42.3 us
  waiting for transfers between devices  14.9 us (35%)
  starting transfers between devices  12.7 us (30%)
  matrix products  7.78 us (18%)
  other arithmetic  4.09 us (10%)
  local copies, waits for them, and re-layouts  2.66 us (6%)
    ppermute x3, waiting for transfers between devices, swap_by_core(): return lax.ppermute(x, (axis, 'tp'), pairs)  7.01 us
    all_to_all x1, waiting for transfers between devices, on_device(): lax.all_to_all(result.reshape(n_exp * n_tp, CAP, width), ('exp', 'tp'), s...  5.51 us
    ppermute x3, starting transfers between devices, swap_by_core(): return lax.ppermute(x, (axis, 'tp'), pairs)  4.72 us
    ppermute x3, starting transfers between devices, swap(): return lax.ppermute(x, axis, [(i, i ^ mask) for i in range(size)])  4.21 us
    all_to_all x1, starting transfers between devices, on_device(): lax.all_to_all(result.reshape(n_exp * n_tp, CAP, width), ('exp', 'tp'), s...  3.72 us
    dot_general x1, matrix products, on_device(): jnp.dot(hidden, w_down[0], preferred_element_type=jnp.float32)  3.12 us
    ppermute x3, waiting for transfers between devices, swap(): return lax.ppermute(x, axis, [(i, i ^ mask) for i in range(size)])  2.37 us
    dot_general x1, matrix products, on_device(): up = jnp.dot(flat_rows, w_up[0], preferred_element_type=jnp.float32)  1.91 us
  transfers between devices with their start and end apart: 7, of which 5 were waited for; matrix products, arithmetic and copies ran while one was open for 10% of the time, Pallas kernels for 0%

profile of v1, /device:TPU:0, one launch (start us, length us, event | category | flops | bytes accessed | tf_op | source)
XLA Modules:
  0.0 42.3 jit_solution(10585322741855046896)
XLA Ops:
  0.0 1.0 %constant_dynamic-slice_fusion.1 = (bf16[32,1,128]{2,1,0:T(2,128)(2,1)S(1)}, bf16[32,1,128]{2,1,0:T(2,128)(2,1)S(1)}) fusion(bf16[32,4,128]{2,1,0:T(4,128)(2,1)} %param.12, s32[]{:T(128)S(6)} %select_n.54, bf16[32,4,128]{2,1,0:T(4,128)(2,1)} %param.11), kind=kLoop, calls=%fused_computation.68 | loop fusion | bytes 32772 | tf_op jit(solution)/shard_map/jit(dynamic_index_in_dim)/dynamic_slice | solution.py:56
  1.0 4.1 %collective-permute-start.2 = (bf16[64,128]{1,0:T(8,128)(2,1)S(1)}, bf16[64,128]{1,0:T(8,128)(2,1)S(1)}, u32[]{:S(2)}, u32[]{:S(2)}) collective-permute-start(bf16[64,128]{1,0:T(8,128)(2,1)S(1)} %pad_maximum_fusion.1), channel_id=1, source_target_pairs={{0,16},{8,24},{16,0},{24,8},{1,17},{9,25},{17,1},{25,9},{2,18},{10... | collective-permute-start | bytes 49160 | tf_op jit(solution)/shard_map/ppermute | solution.py:15
  5.1 1.6 %collective-permute-start = (bf16[64,128]{1,0:T(8,128)(2,1)S(1)}, bf16[64,128]{1,0:T(8,128)(2,1)S(1)}, u32[]{:S(2)}, u32[]{:S(2)}) collective-permute-start(bf16[64,128]{1,0:T(8,128)(2,1)S(1)} %pad_maximum_fusion.1), channel_id=1, source_target_pairs={{0,8},{1,25},{8,0},{9,17},{16,24},{17,9},{24,16},{25,1},{2,10},{3,... | collective-permute-start | bytes 49160 | tf_op jit(solution)/shard_map/ppermute | solution.py:25
  6.7 0.8 %eq.46 = s32[32]{0:T(128)S(1)} reshape(s32[4,8]{1,0:T(4,128)} %param.15) | data formatting | bytes 256 | tf_op jit(solution)/shard_map/eq | solution.py:92
  7.5 0.2 convert_reduce_fusion.1
  7.7 0.7 %add_select_fusion = s32[4,8]{1,0:T(4,128)S(1)} fusion(s32[4,8]{1,0:T(4,128)S(1)} %reduce_sum.67, s32[4,8]{1,0:T(4,128)} %param.15), kind=kLoop, calls=%fused_computation.63 | loop fusion | flops 128 | bytes 384 | tf_op jit(solution)/shard_map/jit(_where)/select_n | solution.py:94
  8.4 0.8 %reduce_sum.69 = f32[4]{0:T(128)S(1)} reduce(f32[4,8]{1,0:T(4,128)} %param.16, f32[]{:T(128)} %constant.60.clone.1), dimensions={1}, to_apply=%region_4.5 | reduce | flops 28 | bytes 148 | tf_op jit(solution)/shard_map/reduce_sum | solution.py:102
  9.2 0.8 %broadcast_divide_fusion = f32[4,8]{1,0:T(4,128)S(1)} fusion(f32[4,8]{1,0:T(4,128)} %param.16, f32[4]{0:T(128)S(1)} %reduce_sum.69), kind=kLoop, calls=%fused_computation.65 | loop fusion | flops 32 | bytes 272 | tf_op jit(solution)/shard_map/div | solution.py:102
  10.0 0.1 convert_reduce_fusion.2
  10.1 0.1 copy.35
  10.2 0.1 broadcast_in_dim.68
  10.8 1.1 %collective-permute-done.1 = bf16[64,128]{1,0:T(8,128)(2,1)S(1)} collective-permute-done((bf16[64,128]{1,0:T(8,128)(2,1)S(1)}, bf16[64,128]{1,0:T(8,128)(2,1)S(1)}, u32[]{:S(2)}, u32[]{:S(2)}) %collective-permute-start.1) | collective-permute-done | bytes 16416 | tf_op jit(solution)/shard_map/ppermute | solution.py:15
  12.0 1.0 %fusion.53 = (f32[2,16]{1,0:T(2,128)S(1)}, bf16[2,16,128]{2,1,0:T(8,128)(2,1)S(1)}) fusion(bf16[32,128]{1,0:T(8,128)(2,1)S(1)} %get-tuple-element.11, bf16[32,128]{1,0:T(8,128)(2,1)S(1)} %get-tuple-element.9, bf16[32,128]{1,0:T(8,128)(2,1)S(1)} %get-tuple-element.7, bf16[32,128]{1,0:T(8,128)(2,1)S(1)} %bitcast.87, bf16[16,2,128]{2,1,0:T(2,128)(2,1)} %bitcast.91, ...), kind=kOutput, calls=%fused_computation.88 | convolution fusion | flops 1204351 | bytes 51328 | tf_op jit(solution)/shard_map/sub | solution.py:77
  13.0 0.1 fusion.14
  13.1 0.4 convolution_convert_fusion.1
  13.5 1.6 %collective-permute-start.3 = (bf16[16,4224]{1,0:T(8,128)(2,1)S(1)}, bf16[16,4224]{1,0:T(8,128)(2,1)S(1)}, u32[]{:S(2)}, u32[]{:S(2)}) collective-permute-start(bf16[16,4224]{1,0:T(8,128)(2,1)S(1)} %pad_maximum_fusion), channel_id=1, source_target_pairs={{0,2},{1,5},{2,0},{3,7},{4,6},{5,1},{6,4},{7,3},{8,10},{9,13},{10,... | collective-permute-start | bytes 405512 | tf_op jit(solution)/shard_map/ppermute | solution.py:25
  15.1 3.5 %collective-permute-done.3 = bf16[16,4224]{1,0:T(8,128)(2,1)S(1)} collective-permute-done((bf16[16,4224]{1,0:T(8,128)(2,1)S(1)}, bf16[16,4224]{1,0:T(8,128)(2,1)S(1)}, u32[]{:S(2)}, u32[]{:S(2)}) %collective-permute-start.3) | collective-permute-done | bytes 135200 | tf_op jit(solution)/shard_map/ppermute | solution.py:25
  18.7 1.6 %collective-permute-start.4 = (bf16[16,4224]{1,0:T(8,128)(2,1)S(1)}, bf16[16,4224]{1,0:T(8,128)(2,1)S(1)}, u32[]{:S(2)}, u32[]{:S(2)}) collective-permute-start(bf16[16,4224]{1,0:T(8,128)(2,1)S(1)} %add_convert_fusion.1), channel_id=1, source_target_pairs={{0,4},{1,3},{2,6},{3,1},{4,0},{5,7},{6,2},{7,5},{8,12},{9,11},{10,... | collective-permute-start | bytes 405512 | tf_op jit(solution)/shard_map/ppermute | solution.py:25
  20.2 3.5 %collective-permute-done.4 = bf16[16,4224]{1,0:T(8,128)(2,1)S(1)} collective-permute-done((bf16[16,4224]{1,0:T(8,128)(2,1)S(1)}, bf16[16,4224]{1,0:T(8,128)(2,1)S(1)}, u32[]{:S(2)}, u32[]{:S(2)}) %collective-permute-start.4) | collective-permute-done | bytes 135200 | tf_op jit(solution)/shard_map/ppermute | solution.py:25
  23.8 0.1 multiply_reduce_fusion
  24.0 0.1 multiply_convert_fusion
  24.2 0.3 convolution_convert_fusion.2
  24.6 1.2 %collective-permute-done.5 = bf16[8,4096]{1,0:T(8,128)(2,1)S(1)} collective-permute-done((bf16[8,4096]{1,0:T(8,128)(2,1)S(1)}, bf16[8,4096]{1,0:T(8,128)(2,1)S(1)}, u32[]{:S(2)}, u32[]{:S(2)}) %collective-permute-start.5) | collective-permute-done | bytes 65568 | tf_op jit(solution)/shard_map/ppermute | solution.py:15
  25.8 1.9 %fusion.3 = f32[16,192]{1,0:T(8,128)S(1)} fusion(bf16[16,4096]{1,0:T(8,128)(2,1)S(1)} %constant_dynamic-update-slice_fusion, bf16[1,4096,192]{1,2,0:T(8,128)(2,1)} %param.18), kind=kOutput, calls=%fused_computation.7 | convolution fusion | flops 25165824 | bytes 1716224 | tf_op jit(solution)/shard_map/dot_general | solution.py:128
  27.8 3.1 %convolution_convert_fusion = bf16[16,4096]{1,0:T(8,128)(2,1)S(1)} fusion(bf16[1,192,4096]{2,1,0:T(8,128)(2,1)} %param.19, f32[16,192]{1,0:T(8,128)S(1)} %fusion.3, bf16[16,4096]{1,0:T(8,128)(2,1)S(1)} %constant_dynamic-update-slice_fusion, bf16[1,4096,192]{1,2,0:T(8,128)(2,1)} %param.17), kind=kOutput, calls=%fused_computation.1 | convolution fusion | flops 50412544 | bytes 3420160 | tf_op jit(solution)/shard_map/dot_general | solution.py:130
  30.9 0.1 reshape.133
  31.0 0.1 copy.30
  31.1 0.8 %broadcast_select_fusion = bf16[2,4,2,4096]{3,2,0,1:T(2,128)(2,1)} fusion(bf16[2,4,2,4096]{3,2,0,1:T(2,128)(2,1)S(1)} %copy.30, pred[]{:T(512)S(6)} %eq.43), kind=kLoop, calls=%fused_computation.26 | loop fusion | flops 65536 | bytes 262145 | tf_op jit(solution)/shard_map/jit(_where)/select_n | solution.py:132
  31.9 3.7 %all-to-all-start = ((bf16[8,2,4096]{2,1,0:T(2,128)(2,1)}), bf16[8,2,4096]{2,1,0:T(2,128)(2,1)S(1)}, u32[]{:S(2)}, u32[]{:S(2)}) async-start(bf16[8,2,4096]{2,1,0:T(2,128)(2,1)} %bitcast.16), calls=%async_computation | async-start | bytes 262144 | tf_op jit(solution)/shard_map/all_to_all | solution.py:133
  35.6 5.5 %all-to-all-done = bf16[8,2,4096]{2,1,0:T(2,128)(2,1)S(1)} async-done(((bf16[8,2,4096]{2,1,0:T(2,128)(2,1)}), bf16[8,2,4096]{2,1,0:T(2,128)(2,1)S(1)}, u32[]{:S(2)}, u32[]{:S(2)}) %all-to-all-start) | async-done | bytes 131104 | tf_op jit(solution)/shard_map/all_to_all | solution.py:133
  41.1 0.1 convert_reduce_fusion
  41.3 0.9 %fusion.1 = bf16[4,4096]{1,0:T(4,128)(2,1)} fusion(f32[4,4]{1,0:T(4,128)S(1)} %get-tuple-element.6, f32[4,4096]{1,0:T(4,128)S(1)} %reshape.137, f32[16,4096]{1,0:T(8,128)S(1)} %slice_convert_fusion, s32[]{:T(128)S(6)} %select_n.59), kind=kOutput, calls=%fused_computation.5 | convolution fusion | flops 819200 | bytes 163908 | tf_op jit(solution)/shard_map/dot_general | solution.py:139
  (39 shorter events, 1.1 us)
Async XLA Ops:
  0.0 13.1 %copy-start = (bf16[256,4096]{1,0:T(8,128)(2,1)S(1)}, bf16[256,4096]{1,0:T(8,128)(2,1)}, u32[]{:S(2)}) copy-start(bf16[256,4096]{1,0:T(8,128)(2,1)} %param.13) | copy-start | bytes 6291460
  1.0 9.8 %collective-permute-start.2 = (bf16[64,128]{1,0:T(8,128)(2,1)S(1)}, bf16[64,128]{1,0:T(8,128)(2,1)S(1)}, u32[]{:S(2)}, u32[]{:S(2)}) collective-permute-start(bf16[64,128]{1,0:T(8,128)(2,1)S(1)} %pad_maximum_fusion.1), channel_id=1, source_target_pairs={{0,16},{8,24},{16,0},{24,8},{1,17},{9,25},{17,1},{25,9},{2,18},{10... | collective-permute-start | bytes 49160 | tf_op jit(solution)/shard_map/ppermute | solution.py:15
  5.1 5.7 %collective-permute-start = (bf16[64,128]{1,0:T(8,128)(2,1)S(1)}, bf16[64,128]{1,0:T(8,128)(2,1)S(1)}, u32[]{:S(2)}, u32[]{:S(2)}) collective-permute-start(bf16[64,128]{1,0:T(8,128)(2,1)S(1)} %pad_maximum_fusion.1), channel_id=1, source_target_pairs={{0,8},{1,25},{8,0},{9,17},{16,24},{17,9},{24,16},{25,1},{2,10},{3,... | collective-permute-start | bytes 49160 | tf_op jit(solution)/shard_map/ppermute | solution.py:25
  10.8 1.2 %collective-permute-start.1 = (bf16[64,128]{1,0:T(8,128)(2,1)S(1)}, bf16[64,128]{1,0:T(8,128)(2,1)S(1)}, u32[]{:S(2)}, u32[]{:S(2)}) collective-permute-start(bf16[64,128]{1,0:T(8,128)(2,1)S(1)} %collective-permute-done), channel_id=1, source_target_pairs={{0,1},{1,0},{2,3},{3,2},{4,5},{5,4},{6,7},{7,6},{8,9},{9,8},{10,11... | collective-permute-start | bytes 49160 | tf_op jit(solution)/shard_map/ppermute | solution.py:15
  13.1 10.8 %copy-start.1 = (f32[4096]{0:T(1024)S(1)}, f32[4096]{0:T(1024)}, u32[]{:S(2)}) copy-start(f32[4096]{0:T(1024)} %param.14) | copy-start | bytes 49156
  13.5 5.1 %collective-permute-start.3 = (bf16[16,4224]{1,0:T(8,128)(2,1)S(1)}, bf16[16,4224]{1,0:T(8,128)(2,1)S(1)}, u32[]{:S(2)}, u32[]{:S(2)}) collective-permute-start(bf16[16,4224]{1,0:T(8,128)(2,1)S(1)} %pad_maximum_fusion), channel_id=1, source_target_pairs={{0,2},{1,5},{2,0},{3,7},{4,6},{5,1},{6,4},{7,3},{8,10},{9,13},{10,... | collective-permute-start | bytes 405512 | tf_op jit(solution)/shard_map/ppermute | solution.py:25
  18.7 5.1 %collective-permute-start.4 = (bf16[16,4224]{1,0:T(8,128)(2,1)S(1)}, bf16[16,4224]{1,0:T(8,128)(2,1)S(1)}, u32[]{:S(2)}, u32[]{:S(2)}) collective-permute-start(bf16[16,4224]{1,0:T(8,128)(2,1)S(1)} %add_convert_fusion.1), channel_id=1, source_target_pairs={{0,4},{1,3},{2,6},{3,1},{4,0},{5,7},{6,2},{7,5},{8,12},{9,11},{10,... | collective-permute-start | bytes 405512 | tf_op jit(solution)/shard_map/ppermute | solution.py:25
  24.5 1.3 %collective-permute-start.5 = (bf16[8,4096]{1,0:T(8,128)(2,1)S(1)}, bf16[8,4096]{1,0:T(8,128)(2,1)S(1)}, u32[]{:S(2)}, u32[]{:S(2)}) collective-permute-start(bf16[8,4096]{1,0:T(8,128)(2,1)S(1)} %reshape.132), channel_id=1, source_target_pairs={{0,1},{1,0},{2,3},{3,2},{4,5},{5,4},{6,7},{7,6},{8,9},{9,8},{10,11... | collective-permute-start | bytes 196616 | tf_op jit(solution)/shard_map/ppermute | solution.py:15
  31.9 9.3 %all-to-all-start = ((bf16[8,2,4096]{2,1,0:T(2,128)(2,1)}), bf16[8,2,4096]{2,1,0:T(2,128)(2,1)S(1)}, u32[]{:S(2)}, u32[]{:S(2)}) async-start(bf16[8,2,4096]{2,1,0:T(2,128)(2,1)} %bitcast.16), calls=%async_computation | async-start | bytes 262144 | tf_op jit(solution)/shard_map/all_to_all | solution.py:133

commit v2 on v1

v2 whole, which is shorter than its diff:
```python
import functools

import jax
import jax.numpy as jnp
from jax import lax
from jax.experimental import pallas as pl
from jax.experimental.pallas import tpu as pltpu
from jax.sharding import PartitionSpec as P

CAP = 2
LANES = 128
VMEM_LIMIT = 24 * 1024 * 1024


def silu_mul(gate, up):
    return gate / (1.0 + jnp.exp(-gate)) * up


def swap(x, axis, mask):
    size = lax.axis_size(axis)
    return lax.ppermute(x, axis, [(i, i ^ mask) for i in range(size)])


def swap_by_core(x, axis, masks):
    size, cores = lax.axis_size(axis), lax.axis_size("tp")
    pairs = [
        (i * cores + t, (i ^ masks[t % len(masks)]) * cores + t)
        for i in range(size)
        for t in range(cores)
    ]
    return lax.ppermute(x, (axis, "tp"), pairs)


def gather_ctx(x):
    size = lax.axis_size("ctx")
    masks, got = [(0, 0)], [x]
    for low in range(1, size // 2):
        high = size - low
        mine = swap_by_core(x, "ctx", (low, high))
        masks += [(low, high), (high, low)]
        got += [mine, swap(mine, "tp", 1)]
    masks.append((size // 2, size // 2))
    got.append(swap(x, "ctx", size // 2))
    return masks, got


def call(kernel, outs, *args, flops=0, read=0, name=None):
    outs = [jax.ShapeDtypeStruct(shape, dtype) for shape, dtype in outs]
    return pl.pallas_call(
        kernel,
        out_shape=outs,
        in_specs=[pl.BlockSpec(memory_space=pltpu.VMEM)] * len(args),
        out_specs=[pl.BlockSpec(memory_space=pltpu.VMEM)] * len(outs),
        compiler_params=pltpu.CompilerParams(vmem_limit_bytes=VMEM_LIMIT),
        cost_estimate=pl.CostEstimate(flops=flops, bytes_accessed=read, transcendentals=0),
        name=name,
    )(*args)


def route_kernel(live, routes_ref, weight_ref, note_ref, mix_ref):
    rows, picks = routes_ref.shape
    width = mix_ref.shape[1]
    routes, weight = routes_ref[...], weight_ref[...]
    lane = lax.broadcasted_iota(jnp.int32, (rows, width), 1)
    expert = jnp.where(lane < live * CAP, lane // CAP, -1)
    has = jnp.zeros((rows, width), jnp.float32)
    part = jnp.zeros((rows, width), jnp.float32)
    for k in range(picks):
        hit = routes[:, k : k + 1] == expert
        has = has + jnp.where(hit, 1.0, 0.0)
        part = part + jnp.where(hit, weight[:, k : k + 1], 0.0)
    earlier = [jnp.zeros((1, width), jnp.float32)]
    for r in range(rows - 1):
        earlier.append(earlier[-1] + has[r : r + 1])
    slot = jnp.concatenate(earlier, axis=0)
    hit = jnp.where(slot == (lane % CAP).astype(jnp.float32), has, 0.0)
    mix_ref[...] = hit * part / jnp.sum(weight, axis=1, keepdims=True)
    blocks = note_ref.shape[0] // rows
    mine = lax.axis_index("exp")
    note_ref[...] = jnp.concatenate(
        [jnp.where(mine == b, hit, 0.0) for b in range(blocks)], axis=0
    ).astype(note_ref.dtype)


def attend_kernel(masks, blocks, q_ref, weight_ref, note_ref, *refs):
    kv_refs, out_ref = refs[:-1], refs[-1]
    count, heads, head_dim = q_ref.shape
    span = kv_refs[0].shape[0] // 2
    rows = count // blocks
    width = weight_ref.shape[1]
    n_tp = lax.axis_size("tp")
    ctx, core = lax.axis_index("ctx"), lax.axis_index("tp")
    query = jnp.concatenate([q_ref[:, h, :] for h in range(heads)], axis=0)
    key = jnp.concatenate([r[:span, :] for r in kv_refs], axis=0)
    value = jnp.concatenate([r[span:, :] for r in kv_refs], axis=0)
    score = lax.dot_general(
        query, key, (((1,), (1,)), ((), ())), preferred_element_type=jnp.float32
    ) * (head_dim ** (-0.5))
    lane = lax.broadcasted_iota(jnp.int32, (1, len(kv_refs) * span), 1)
    start = jnp.zeros_like(lane)
    for j, (even, odd) in enumerate(masks):
        block = ctx ^ jnp.where(core == 0, even, odd)
        start = jnp.where(lane // span == j, block * span, start)
    key_pos = start + lane % span
    row = lax.broadcasted_iota(jnp.int32, (heads * count, 1), 0) % count
    query_pos = ((ctx * blocks + row // rows) * n_tp + core) * rows + row % rows
    allowed = key_pos <= query_pos
    score = jnp.where(allowed, score, -1e30)
    prob = jnp.where(allowed, jnp.exp(score - jnp.max(score, axis=1, keepdims=True)), 0.0)
    total = jnp.sum(prob, axis=1, keepdims=True)
    mixed = jnp.dot(prob.astype(jnp.bfloat16), value, preferred_element_type=jnp.float32) / total
    mixed = mixed.astype(jnp.bfloat16)
    mixed = jnp.concatenate([mixed[h * count : (h + 1) * count] for h in range(heads)], axis=1)
    out_ref[:, :width] = jnp.dot(
        mixed, weight_ref[...], preferred_element_type=jnp.float32
    ).astype(out_ref.dtype)
    out_ref[:, width:] = note_ref[...]


def norm_kernel(blocks, live, mine_ref, other_ref, gain_ref, state_ref, buffer_ref):
    count, width = state_ref.shape
    rows = count // blocks
    summed = (mine_ref[:, :width].astype(jnp.float32) + other_ref[:, :width].astype(jnp.float32)).astype(
        jnp.bfloat16
    )
    state_ref[...] = summed
    state = summed.astype(jnp.float32)
    note = mine_ref[:, width:] + other_ref[:, width:]
    inverse = lax.rsqrt(jnp.mean(state * state, axis=1, keepdims=True) + 1e-06)
    normed = (state * inverse * gain_ref[...]).astype(jnp.bfloat16)
    expert = lax.rem(lax.axis_index("exp"), live)
    slots = blocks * CAP
    shape = (slots, note.shape[1])
    pick_lane = (
        lax.broadcasted_iota(jnp.int32, shape, 1)
        == expert * CAP + lax.broadcasted_iota(jnp.int32, shape, 0) % CAP
    )
    pick = lax.dot_general(
        pick_lane.astype(jnp.float32).astype(jnp.bfloat16),
        note,
        (((1,), (1,)), ((), ())),
        preferred_element_type=jnp.float32,
    )
    shape = (slots, count)
    same = (
        lax.broadcasted_iota(jnp.int32, shape, 0) // CAP
        == lax.broadcasted_iota(jnp.int32, shape, 1) // rows
    )
    pick = jnp.where(same, pick, 0.0).astype(jnp.bfloat16)
    buffer_ref[...] = jnp.dot(pick, normed, preferred_element_type=jnp.float32).astype(jnp.bfloat16)


def expert_kernel(mine_ref, other_ref, gate_ref, up_ref, down_ref, out_ref):
    slots = mine_ref.shape[0]
    x = jnp.concatenate([mine_ref[...], other_ref[...]], axis=0)
    last = (((1,), (1,)), ((), ()))
    gate = lax.dot_general(x, gate_ref[...], last, preferred_element_type=jnp.float32)
    up = lax.dot_general(x, up_ref[...], last, preferred_element_type=jnp.float32)
    hidden = silu_mul(gate, up).astype(jnp.bfloat16)
    result = jnp.dot(hidden, down_ref[...], preferred_element_type=jnp.float32).astype(jnp.bfloat16)
    core = lax.axis_index("tp")
    for half in range(2):
        for b in range(slots // CAP):
            at = half * slots + b * CAP
            out_ref[2 * b + (core ^ half)] = result[at : at + CAP]


def combine_kernel(live, back_ref, mix_ref, own_ref, out_ref):
    n_tp = lax.axis_size("tp")
    mix = mix_ref[...]
    total = own_ref[...].astype(jnp.float32)
    for x in range(live):
        parts = [back_ref[(h * live + x) * n_tp + t] for h in range(2) for t in range(n_tp)]
        rows = functools.reduce(lambda a, b: a + b, [p.astype(jnp.float32) for p in parts])
        for s in range(CAP):
            lane = x * CAP + s
            total = total + mix[:, lane : lane + 1] * rows[s : s + 1]
    out_ref[...] = total.astype(out_ref.dtype)


def on_device(
    queries, keys, values, out_weight, norm_gain, routes, route_weight, w_gate, w_up, w_down
):
    blocks, lanes, rows, local_heads, head_dim = queries.shape
    width = out_weight.shape[1]
    n_exp = lax.axis_size("exp")
    n_tp = lax.axis_size("tp")
    live = n_exp // 2
    count = blocks * rows
    exp_index = lax.axis_index("exp")
    group = local_heads * n_exp // keys.shape[1]
    kv_head = exp_index * local_heads // group
    key_mine = lax.dynamic_index_in_dim(keys, kv_head, 1, keepdims=False)
    value_mine = lax.dynamic_index_in_dim(values, kv_head, 1, keepdims=False)
    masks, got = gather_ctx(jnp.concatenate([key_mine, value_mine], axis=0))

    note_width = -(-(live * CAP) // LANES) * LANES
    note, mix = call(
        functools.partial(route_kernel, live),
        [((count, note_width), jnp.bfloat16), ((rows, note_width), jnp.float32)],
        routes,
        route_weight,
        name="route",
    )
    (summed,) = call(
        functools.partial(attend_kernel, masks, blocks),
        [((count, width + note_width), jnp.bfloat16)],
        queries.reshape(count, local_heads, head_dim),
        out_weight,
        note,
        *got,
        flops=2 * count * out_weight.size,
        read=2 * out_weight.size,
        name="attend",
    )
    steps = [1 << i for i in range(n_exp.bit_length() - 1)]
    for i, step in enumerate(steps):
        other = swap_by_core(summed, "exp", (step, steps[-1 - i]))
        if i < len(steps) - 1:
            summed = (summed.astype(jnp.float32) + other.astype(jnp.float32)).astype(jnp.bfloat16)
    state, buffer = call(
        functools.partial(norm_kernel, blocks, live),
        [((count, width), jnp.bfloat16), ((blocks * CAP, width), jnp.bfloat16)],
        summed,
        other,
        norm_gain.reshape(1, width),
        name="norm",
    )
    (result,) = call(
        expert_kernel,
        [((n_exp * n_tp, CAP, width), jnp.bfloat16)],
        buffer,
        swap(buffer, "tp", 1),
        w_gate[0].T,
        w_up[0].T,
        w_down[0],
        flops=2 * blocks * CAP * n_tp * 3 * w_down.size,
        read=6 * w_down.size,
        name="experts",
    )
    back = lax.all_to_all(result, ("exp", "tp"), split_axis=0, concat_axis=0, tiled=True)
    own = lax.dynamic_slice_in_dim(state, exp_index * rows, rows, 0)
    (out,) = call(
        functools.partial(combine_kernel, live),
        [((rows, width), jnp.bfloat16)],
        back,
        mix,
        own,
        name="combine",
    )
    return out


def solution(mesh):
    in_specs = (
        P("ctx", "tp", None, "exp", None),
        P("ctx", None, None),
        P("ctx", None, None),
        P("exp", None),
        P(),
        P(("ctx", "exp", "tp"), None),
        P(("ctx", "exp", "tp"), None),
        P("exp", None, "tp"),
        P("exp", None, "tp"),
        P("exp", "tp", None),
    )
    out_specs = P(("ctx", "exp", "tp"), None)
    return jax.shard_map(
        on_device, mesh=mesh, in_specs=in_specs, out_specs=out_specs, check_vma=False
    )
```

time: 42.7 us -> 38.6 us (0.904)
  matrix products: 7.78 us -> 0 us
  local copies, waits for them, and re-layouts: 2.66 us -> 7.33 us
  other arithmetic: 4.09 us -> 0.04 us
  Pallas kernels: 0 us -> 3.75 us
  waiting for transfers between devices: 14.9 us -> 14.3 us
    dot_general x6 -> x0, matrix products: 6.77 us -> none  [the longest x1 3.12 us: on_device(): jnp.dot(hidden, w_down[0], preferred_element_type=jnp.float32)]
    unnamed x8 -> x18, local copies, waits for them, and re-layouts: 0.13 us -> 6.48 us
    pallas_call x0 -> x5, Pallas kernels: none -> 3.75 us  [call(): pl.pallas_call(kernel, out_shape=outs, in_specs=[pl.BlockSpec(memory_spac...]
    select_n x3 -> x0, other arithmetic: 1.53 us -> none  [the longest x1 0.76 us: on_device(): jnp.where(tp_index == 0, result, result[::-1]).transpose(1, 0, 2, 3)]
    ppermute x3, starting transfers between devices: 4.72 us -> 6.2 us  [swap_by_core(): return lax.ppermute(x, (axis, 'tp'), pairs)]
    ppermute x3, starting transfers between devices: 4.21 us -> 2.78 us  [swap(): return lax.ppermute(x, axis, [(i, i ^ mask) for i in range(size)])]
    reduce_sum x5 -> x0, other arithmetic: 1.35 us -> none  [the longest x1 0.8 us: on_device(): share = route_weight / jnp.sum(route_weight, axis=1, keepdims=True)]
    sub x1 -> x0, matrix products: 1.01 us -> none  [on_device(): prob = jnp.where(allowed, jnp.exp(logit_score - high), 0.0)]
  transfers between devices with their start and end apart: 7 -> 7, of which waited for: 5 -> 5; matrix products, arithmetic and copies ran while one was open for 10% -> 0% of each run, Pallas kernels for 0% -> 0%
where the time goes in v2:
time: 38.6 us; the launch traced here: 38.2 us
  waiting for transfers between devices  14.3 us (37%)
  starting transfers between devices  12.7 us (33%)
  local copies, waits for them, and re-layouts  7.33 us (19%)
  Pallas kernels  3.75 us (10%)
    ppermute x3, waiting for transfers between devices, swap_by_core(): return lax.ppermute(x, (axis, 'tp'), pairs)  7.01 us
    unnamed x18, local copies, waits for them, and re-layouts  6.48 us
    ppermute x3, starting transfers between devices, swap_by_core(): return lax.ppermute(x, (axis, 'tp'), pairs)  6.2 us
    all_to_all x1, waiting for transfers between devices, on_device(): lax.all_to_all(result, ('exp', 'tp'), split_axis=0, concat_axis=0, tiled=...  5.5 us
    pallas_call x5, Pallas kernels, call(): pl.pallas_call(kernel, out_shape=outs, in_specs=[pl.BlockSpec(memory_spac...  3.75 us
    all_to_all x1, starting transfers between devices, on_device(): lax.all_to_all(result, ('exp', 'tp'), split_axis=0, concat_axis=0, tiled=...  3.72 us
    ppermute x3, starting transfers between devices, swap(): return lax.ppermute(x, axis, [(i, i ^ mask) for i in range(size)])  2.78 us
    ppermute x3, waiting for transfers between devices, swap(): return lax.ppermute(x, axis, [(i, i ^ mask) for i in range(size)])  1.78 us
  transfers between devices with their start and end apart: 7, of which 5 were waited for; matrix products, arithmetic and copies ran while one was open for 0% of the time, Pallas kernels for 0%

profile of v2, /device:TPU:0, one launch (start us, length us, event | category | flops | bytes accessed | tf_op | source)
XLA Modules:
  0.0 38.2 jit_solution(5579718605881714273)
XLA Ops:
  0.0 0.0 copy-start.4
  0.0 0.8 %constant_dynamic-slice_fusion.1 = (bf16[32,1,128]{2,1,0:T(2,128)(2,1)S(1)}, bf16[32,1,128]{2,1,0:T(2,128)(2,1)S(1)}) fusion(bf16[32,4,128]{2,1,0:T(4,128)(2,1)} %param.12, s32[]{:T(128)S(6)} %select_n.14, bf16[32,4,128]{2,1,0:T(4,128)(2,1)} %param.11), kind=kLoop, calls=%fused_computation.5 | loop fusion | bytes 32772 | tf_op jit(solution)/shard_map/jit(dynamic_index_in_dim)/dynamic_slice | solution.py:194
  0.9 3.1 %collective-permute-start = (bf16[64,128]{1,0:T(8,128)(2,1)S(1)}, bf16[64,128]{1,0:T(8,128)(2,1)S(1)}, u32[]{:S(2)}, u32[]{:S(2)}) collective-permute-start(bf16[64,128]{1,0:T(8,128)(2,1)S(1)} %pad_maximum_fusion.refs_0_), channel_id=1, source_target_pairs={{0,8},{1,25},{8,0},{9,17},{16,24},{17,9},{24,16},{25,1},{2,10},{3,... | collective-permute-start | bytes 49160 | tf_op jit(solution)/shard_map/ppermute | solution.py:31
  4.0 2.6 %collective-permute-start.2 = (bf16[64,128]{1,0:T(8,128)(2,1)S(1)}, bf16[64,128]{1,0:T(8,128)(2,1)S(1)}, u32[]{:S(2)}, u32[]{:S(2)}) collective-permute-start(bf16[64,128]{1,0:T(8,128)(2,1)S(1)} %pad_maximum_fusion.refs_0_), channel_id=1, source_target_pairs={{0,16},{8,24},{16,0},{24,8},{1,17},{9,25},{17,1},{25,9},{2,18},{10... | collective-permute-start | bytes 49160 | tf_op jit(solution)/shard_map/ppermute | solution.py:21
  6.5 0.0 collective-permute-done.refs_1_
  6.5 0.1 collective-permute-start.1
  6.7 0.0 copy-start.6
  6.7 0.7 %copy-done.6 = s32[4,8]{1,0:T(4,128)S(1)} copy-done((s32[4,8]{1,0:T(4,128)S(1)}, s32[4,8]{1,0:T(4,128)}, u32[]{:S(2)}) %copy-start.6) | copy-done | bytes 152
  7.3 0.0 copy-start.7
  7.3 0.7 %copy-done.7 = f32[4,8]{1,0:T(4,128)S(1)} copy-done((f32[4,8]{1,0:T(4,128)S(1)}, f32[4,8]{1,0:T(4,128)}, u32[]{:S(2)}) %copy-start.7) | copy-done | bytes 152
  8.0 0.1 route.1
  8.1 0.5 %collective-permute-done.2.refs_3_ = bf16[64,128]{1,0:T(8,128)(2,1)S(1)} collective-permute-done((bf16[64,128]{1,0:T(8,128)(2,1)S(1)}, bf16[64,128]{1,0:T(8,128)(2,1)S(1)}, u32[]{:S(2)}, u32[]{:S(2)}) %collective-permute-start.2) | collective-permute-done | bytes 16416 | tf_op jit(solution)/shard_map/ppermute | solution.py:21
  8.7 0.0 collective-permute-done.1.refs_2_
  8.7 0.0 copy-start
  8.7 1.6 %copy-done = bf16[256,4096]{1,0:T(8,128)(2,1)S(1)} copy-done((bf16[256,4096]{1,0:T(8,128)(2,1)S(1)}, bf16[256,4096]{1,0:T(8,128)(2,1)}, u32[]{:S(2)}) %copy-start) | copy-done | bytes 2097176
  10.3 0.7 %copy-done.5 = bf16[4,1,4,2,128]{4,3,2,1,0:T(2,128)(2,1)S(1)} copy-done((bf16[4,1,4,2,128]{4,3,2,1,0:T(2,128)(2,1)S(1)}, bf16[4,1,4,2,128]{4,3,2,1,0:T(2,128)(2,1)}, u32[]{:S(2)}) %copy-start.5) | copy-done | bytes 8216
  11.0 0.7 %attend.1 = bf16[16,4224]{1,0:T(8,128)(2,1)S(1)} custom-call(bf16[16,2,128]{2,1,0:T(2,128)(2,1)S(1)} %bitcast.19, bf16[256,4096]{1,0:T(8,128)(2,1)S(1)} %copy-done, bf16[16,128]{1,0:T(8,128)(2,1)S(1)} %get-tuple-element.9.note_ref, bf16[64,128]{1,0:T(8,128)(2,1)S(1)} %pad_maximum_fusion.refs_0_, bf16[64,128]{1,0:T(8,128)(2,1)S(1)} %collective-permute-done.refs_1_, ...), custom_call_target="tpu_custom_call" | custom-call | flops 33554432 | bytes 2097152 | tf_op jit(solution)/shard_map/attend/pallas_call | solution.py:49
  11.7 1.5 %collective-permute-start.3 = (bf16[16,4224]{1,0:T(8,128)(2,1)S(1)}, bf16[16,4224]{1,0:T(8,128)(2,1)S(1)}, u32[]{:S(2)}, u32[]{:S(2)}) collective-permute-start(bf16[16,4224]{1,0:T(8,128)(2,1)S(1)} %attend.1), channel_id=1, source_target_pairs={{0,2},{1,5},{2,0},{3,7},{4,6},{5,1},{6,4},{7,3},{8,10},{9,13},{10,... | collective-permute-start | bytes 405512 | tf_op jit(solution)/shard_map/ppermute | solution.py:31
  13.2 3.5 %collective-permute-done.3 = bf16[16,4224]{1,0:T(8,128)(2,1)S(1)} collective-permute-done((bf16[16,4224]{1,0:T(8,128)(2,1)S(1)}, bf16[16,4224]{1,0:T(8,128)(2,1)S(1)}, u32[]{:S(2)}, u32[]{:S(2)}) %collective-permute-start.3) | collective-permute-done | bytes 135200 | tf_op jit(solution)/shard_map/ppermute | solution.py:31
  16.7 1.6 %collective-permute-start.4 = (bf16[16,4224]{1,0:T(8,128)(2,1)S(1)}, bf16[16,4224]{1,0:T(8,128)(2,1)S(1)}, u32[]{:S(2)}, u32[]{:S(2)}) collective-permute-start(bf16[16,4224]{1,0:T(8,128)(2,1)S(1)} %add_convert_fusion.mine_ref), channel_id=1, source_target_pairs={{0,4},{1,3},{2,6},{3,1},{4,0},{5,7},{6,2},{7,5},{8,12},{9,11},{10,... | collective-permute-start | bytes 405512 | tf_op jit(solution)/shard_map/ppermute | solution.py:31
  18.3 3.5 %collective-permute-done.4.other_ref = bf16[16,4224]{1,0:T(8,128)(2,1)S(1)} collective-permute-done((bf16[16,4224]{1,0:T(8,128)(2,1)S(1)}, bf16[16,4224]{1,0:T(8,128)(2,1)S(1)}, u32[]{:S(2)}, u32[]{:S(2)}) %collective-permute-start.4) | collective-permute-done | bytes 135200 | tf_op jit(solution)/shard_map/ppermute | solution.py:31
  21.8 0.0 copy-done.4
  21.8 0.3 norm.1
  22.1 0.1 collective-permute-start.5
  22.2 1.2 %collective-permute-done.5.other_ref = bf16[8,4096]{1,0:T(8,128)(2,1)S(1)} collective-permute-done((bf16[8,4096]{1,0:T(8,128)(2,1)S(1)}, bf16[8,4096]{1,0:T(8,128)(2,1)S(1)}, u32[]{:S(2)}, u32[]{:S(2)}) %collective-permute-start.5) | collective-permute-done | bytes 65568 | tf_op jit(solution)/shard_map/ppermute | solution.py:21
  23.5 0.0 copy-done.1
  23.5 1.4 %copy-done.2 = bf16[1,4096,192]{1,2,0:T(8,128)(2,1)S(1)} copy-done((bf16[1,4096,192]{1,2,0:T(8,128)(2,1)S(1)}, bf16[1,4096,192]{1,2,0:T(8,128)(2,1)}, u32[]{:S(2)}) %copy-start.2) | copy-done | bytes 1572888
  24.9 1.4 %copy-done.3 = bf16[1,192,4096]{2,1,0:T(8,128)(2,1)S(1)} copy-done((bf16[1,192,4096]{2,1,0:T(8,128)(2,1)S(1)}, bf16[1,192,4096]{2,1,0:T(8,128)(2,1)}, u32[]{:S(2)}) %copy-start.3) | copy-done | bytes 1572888
  26.3 1.9 %experts.1 = bf16[8,2,4096]{2,1,0:T(2,128)(2,1)} custom-call(bf16[8,4096]{1,0:T(8,128)(2,1)S(1)} %get-tuple-element.10.mine_ref, bf16[8,4096]{1,0:T(8,128)(2,1)S(1)} %collective-permute-done.5.other_ref, bf16[192,4096]{1,0:T(8,128)(2,1)S(1)} %bitcast.15, bf16[192,4096]{1,0:T(8,128)(2,1)S(1)} %bitcast.16, bf16[192,4096]{1,0:T(8,128)(2,1)S(1)} %bitcast.17), custom_call_target="tpu_custom_call" | custom-call | flops 75497472 | bytes 4718592 | tf_op jit(solution)/shard_map/experts/pallas_call | solution.py:49
  28.2 3.7 %all-to-all-start = ((bf16[8,2,4096]{2,1,0:T(2,128)(2,1)}), bf16[8,2,4096]{2,1,0:T(2,128)(2,1)S(1)}, u32[]{:S(2)}, u32[]{:S(2)}) async-start(bf16[8,2,4096]{2,1,0:T(2,128)(2,1)} %experts.1), calls=%async_computation | async-start | bytes 262144 | tf_op jit(solution)/shard_map/all_to_all | solution.py:241
  31.9 5.5 %all-to-all-done.back_ref = bf16[8,2,4096]{2,1,0:T(2,128)(2,1)S(1)} async-done(((bf16[8,2,4096]{2,1,0:T(2,128)(2,1)}), bf16[8,2,4096]{2,1,0:T(2,128)(2,1)S(1)}, u32[]{:S(2)}, u32[]{:S(2)}) %all-to-all-start) | async-done | bytes 131104 | tf_op jit(solution)/shard_map/all_to_all | solution.py:241
  37.4 0.7 %combine.1 = bf16[4,4096]{1,0:T(4,128)(2,1)} custom-call(bf16[8,2,4096]{2,1,0:T(2,128)(2,1)S(1)} %all-to-all-done.back_ref, f32[4,128]{1,0:T(4,128)S(1)} %get-tuple-element.11.mix_ref, bf16[4,4096]{1,0:T(4,128)(2,1)S(1)} %constant_dynamic-slice_fusion.own_ref), custom_call_target="tpu_custom_call" | custom-call | tf_op jit(solution)/shard_map/combine/pallas_call | solution.py:49
  (9 shorter events, 0.1 us)
Async XLA Ops:
  0.0 21.8 %copy-start.4 = (f32[4096]{0:T(1024)S(1)}, f32[4096]{0:T(1024)}, u32[]{:S(2)}) copy-start(f32[4096]{0:T(1024)} %param.14) | copy-start | bytes 49156
  0.9 5.7 %collective-permute-start = (bf16[64,128]{1,0:T(8,128)(2,1)S(1)}, bf16[64,128]{1,0:T(8,128)(2,1)S(1)}, u32[]{:S(2)}, u32[]{:S(2)}) collective-permute-start(bf16[64,128]{1,0:T(8,128)(2,1)S(1)} %pad_maximum_fusion.refs_0_), channel_id=1, source_target_pairs={{0,8},{1,25},{8,0},{9,17},{16,24},{17,9},{24,16},{25,1},{2,10},{3,... | collective-permute-start | bytes 49160 | tf_op jit(solution)/shard_map/ppermute | solution.py:31
  4.0 4.7 %collective-permute-start.2 = (bf16[64,128]{1,0:T(8,128)(2,1)S(1)}, bf16[64,128]{1,0:T(8,128)(2,1)S(1)}, u32[]{:S(2)}, u32[]{:S(2)}) collective-permute-start(bf16[64,128]{1,0:T(8,128)(2,1)S(1)} %pad_maximum_fusion.refs_0_), channel_id=1, source_target_pairs={{0,16},{8,24},{16,0},{24,8},{1,17},{9,25},{17,1},{25,9},{2,18},{10... | collective-permute-start | bytes 49160 | tf_op jit(solution)/shard_map/ppermute | solution.py:21
  6.5 2.1 %collective-permute-start.1 = (bf16[64,128]{1,0:T(8,128)(2,1)S(1)}, bf16[64,128]{1,0:T(8,128)(2,1)S(1)}, u32[]{:S(2)}, u32[]{:S(2)}) collective-permute-start(bf16[64,128]{1,0:T(8,128)(2,1)S(1)} %collective-permute-done.refs_1_), channel_id=1, source_target_pairs={{0,1},{1,0},{2,3},{3,2},{4,5},{5,4},{6,7},{7,6},{8,9},{9,8},{10,11... | collective-permute-start | bytes 49160 | tf_op jit(solution)/shard_map/ppermute | solution.py:21
  6.7 0.7 %copy-start.6 = (s32[4,8]{1,0:T(4,128)S(1)}, s32[4,8]{1,0:T(4,128)}, u32[]{:S(2)}) copy-start(s32[4,8]{1,0:T(4,128)} %routes_ref.1) | copy-start | bytes 388
  7.3 0.7 %copy-start.7 = (f32[4,8]{1,0:T(4,128)S(1)}, f32[4,8]{1,0:T(4,128)}, u32[]{:S(2)}) copy-start(f32[4,8]{1,0:T(4,128)} %weight_ref.2) | copy-start | bytes 388
  8.7 1.6 %copy-start = (bf16[256,4096]{1,0:T(8,128)(2,1)S(1)}, bf16[256,4096]{1,0:T(8,128)(2,1)}, u32[]{:S(2)}) copy-start(bf16[256,4096]{1,0:T(8,128)(2,1)} %weight_ref.3) | copy-start | bytes 6291460
  10.3 0.7 %copy-start.5 = (bf16[4,1,4,2,128]{4,3,2,1,0:T(2,128)(2,1)S(1)}, bf16[4,1,4,2,128]{4,3,2,1,0:T(2,128)(2,1)}, u32[]{:S(2)}) copy-start(bf16[4,1,4,2,128]{4,3,2,1,0:T(2,128)(2,1)} %param.10) | copy-start | bytes 24580
  11.0 12.5 %copy-start.1 = (bf16[1,4096,192]{1,2,0:T(8,128)(2,1)S(1)}, bf16[1,4096,192]{1,2,0:T(8,128)(2,1)}, u32[]{:S(2)}) copy-start(bf16[1,4096,192]{1,2,0:T(8,128)(2,1)} %param.17) | copy-start | bytes 4718596
  11.7 5.0 %collective-permute-start.3 = (bf16[16,4224]{1,0:T(8,128)(2,1)S(1)}, bf16[16,4224]{1,0:T(8,128)(2,1)S(1)}, u32[]{:S(2)}, u32[]{:S(2)}) collective-permute-start(bf16[16,4224]{1,0:T(8,128)(2,1)S(1)} %attend.1), channel_id=1, source_target_pairs={{0,2},{1,5},{2,0},{3,7},{4,6},{5,1},{6,4},{7,3},{8,10},{9,13},{10,... | collective-permute-start | bytes 405512 | tf_op jit(solution)/shard_map/ppermute | solution.py:31
  16.7 5.1 %collective-permute-start.4 = (bf16[16,4224]{1,0:T(8,128)(2,1)S(1)}, bf16[16,4224]{1,0:T(8,128)(2,1)S(1)}, u32[]{:S(2)}, u32[]{:S(2)}) collective-permute-start(bf16[16,4224]{1,0:T(8,128)(2,1)S(1)} %add_convert_fusion.mine_ref), channel_id=1, source_target_pairs={{0,4},{1,3},{2,6},{3,1},{4,0},{5,7},{6,2},{7,5},{8,12},{9,11},{10,... | collective-permute-start | bytes 405512 | tf_op jit(solution)/shard_map/ppermute | solution.py:31
  22.1 1.3 %collective-permute-start.5 = (bf16[8,4096]{1,0:T(8,128)(2,1)S(1)}, bf16[8,4096]{1,0:T(8,128)(2,1)S(1)}, u32[]{:S(2)}, u32[]{:S(2)}) collective-permute-start(bf16[8,4096]{1,0:T(8,128)(2,1)S(1)} %get-tuple-element.10.mine_ref), channel_id=1, source_target_pairs={{0,1},{1,0},{2,3},{3,2},{4,5},{5,4},{6,7},{7,6},{8,9},{9,8},{10,11... | collective-permute-start | bytes 196616 | tf_op jit(solution)/shard_map/ppermute | solution.py:21
  23.5 1.4 %copy-start.2 = (bf16[1,4096,192]{1,2,0:T(8,128)(2,1)S(1)}, bf16[1,4096,192]{1,2,0:T(8,128)(2,1)}, u32[]{:S(2)}) copy-start(bf16[1,4096,192]{1,2,0:T(8,128)(2,1)} %param.18) | copy-start | bytes 4718596
  24.9 1.4 %copy-start.3 = (bf16[1,192,4096]{2,1,0:T(8,128)(2,1)S(1)}, bf16[1,192,4096]{2,1,0:T(8,128)(2,1)}, u32[]{:S(2)}) copy-start(bf16[1,192,4096]{2,1,0:T(8,128)(2,1)} %param.19) | copy-start | bytes 4718596
  28.2 9.3 %all-to-all-start = ((bf16[8,2,4096]{2,1,0:T(2,128)(2,1)}), bf16[8,2,4096]{2,1,0:T(2,128)(2,1)S(1)}, u32[]{:S(2)}, u32[]{:S(2)}) async-start(bf16[8,2,4096]{2,1,0:T(2,128)(2,1)} %experts.1), calls=%async_computation | async-start | bytes 262144 | tf_op jit(solution)/shard_map/all_to_all | solution.py:241

commit v3 on v2

v3 whole, which is shorter than its diff:
```python
import functools

import jax
import jax.numpy as jnp
from jax import lax
from jax.experimental import pallas as pl
from jax.experimental.pallas import tpu as pltpu
from jax.sharding import PartitionSpec as P

CAP = 2
LANES = 128
VMEM_LIMIT = 24 * 1024 * 1024


def silu_mul(gate, up):
    return gate / (1.0 + jnp.exp(-gate)) * up


def swap(x, axis, mask):
    size = lax.axis_size(axis)
    return lax.ppermute(x, axis, [(i, i ^ mask) for i in range(size)])


def swap_by_core(x, axis, masks):
    size, cores = lax.axis_size(axis), lax.axis_size("tp")
    pairs = [
        (i * cores + t, (i ^ masks[t % len(masks)]) * cores + t)
        for i in range(size)
        for t in range(cores)
    ]
    return lax.ppermute(x, (axis, "tp"), pairs)


def gather_ctx(x):
    size = lax.axis_size("ctx")
    masks, got = [(0, 0)], [x]
    for low in range(1, size // 2):
        high = size - low
        mine = swap_by_core(x, "ctx", (low, high))
        masks += [(low, high), (high, low)]
        got += [mine, swap(mine, "tp", 1)]
    masks.append((size // 2, size // 2))
    got.append(swap(x, "ctx", size // 2))
    return masks, got


def far(args):
    return [pltpu.with_memory_space_constraint(a, pltpu.HBM) for a in args]


def call(kernel, outs, *args, where=pltpu.VMEM, scratch=(), kept=pltpu.VMEM, flops=0, read=0, name=None):
    return pl.pallas_call(
        kernel,
        out_shape=[kept(shape, dtype) for shape, dtype in outs],
        in_specs=[pl.BlockSpec(memory_space=where)] * len(args),
        out_specs=[pl.BlockSpec(memory_space=pltpu.VMEM)] * len(outs),
        scratch_shapes=scratch,
        compiler_params=pltpu.CompilerParams(vmem_limit_bytes=VMEM_LIMIT),
        cost_estimate=pl.CostEstimate(flops=flops, bytes_accessed=read, transcendentals=0),
        name=name,
    )(*args)


def open_kernel(live, blocks, group, *refs):
    ins, (kv_ref, q_ref, note_ref, mix_ref), held = refs[:5], refs[5:9], refs[9:14]
    sems = refs[14]
    copies = [pltpu.make_async_copy(i, h, sems.at[n]) for n, (i, h) in enumerate(zip(ins, held))]
    for copy in copies:
        copy.start()
    key_ref, value_ref, query_ref, routes_ref, weight_ref = held
    span = key_ref.shape[0]
    heads = query_ref.shape[1]
    mine = lax.axis_index("exp")
    kv_head = mine * heads // group
    for n, ref in enumerate((key_ref, value_ref)):
        copies[n].wait()
        wanted = lax.broadcasted_iota(jnp.int32, ref.shape, 1) == kv_head
        kept = jnp.sum(jnp.where(wanted, ref[...].astype(jnp.float32), 0.0), axis=1)
        kv_ref[n * span : (n + 1) * span, :] = kept.astype(kv_ref.dtype)
    copies[2].wait()
    q_ref[...] = jnp.concatenate([query_ref[:, h, :] for h in range(heads)], axis=0)
    copies[3].wait()
    copies[4].wait()
    rows, picks = routes_ref.shape
    width = mix_ref.shape[1]
    routes, weight = routes_ref[...], weight_ref[...]
    lane = lax.broadcasted_iota(jnp.int32, (rows, width), 1)
    expert = jnp.where(lane < live * CAP, lane // CAP, -1)
    has = jnp.zeros((rows, width), jnp.float32)
    part = jnp.zeros((rows, width), jnp.float32)
    for k in range(picks):
        hit = routes[:, k : k + 1] == expert
        has = has + jnp.where(hit, 1.0, 0.0)
        part = part + jnp.where(hit, weight[:, k : k + 1], 0.0)
    earlier = [jnp.zeros((1, width), jnp.float32)]
    for r in range(rows - 1):
        earlier.append(earlier[-1] + has[r : r + 1])
    slot = jnp.concatenate(earlier, axis=0)
    hit = jnp.where(slot == (lane % CAP).astype(jnp.float32), has, 0.0)
    mix_ref[...] = hit * part / jnp.sum(weight, axis=1, keepdims=True)
    note_ref[...] = jnp.concatenate(
        [jnp.where(mine == b, hit, 0.0) for b in range(blocks)], axis=0
    ).astype(note_ref.dtype)


def attend_kernel(masks, blocks, q_ref, *refs):
    kv_refs, out_ref = refs[:-1], refs[-1]
    count = out_ref.shape[0]
    heads = q_ref.shape[0] // count
    head_dim = q_ref.shape[1]
    span = kv_refs[0].shape[0] // 2
    rows = count // blocks
    n_tp = lax.axis_size("tp")
    ctx, core = lax.axis_index("ctx"), lax.axis_index("tp")
    key = jnp.concatenate([r[:span, :] for r in kv_refs], axis=0)
    value = jnp.concatenate([r[span:, :] for r in kv_refs], axis=0)
    score = lax.dot_general(
        q_ref[...], key, (((1,), (1,)), ((), ())), preferred_element_type=jnp.float32
    ) * (head_dim ** (-0.5))
    lane = lax.broadcasted_iota(jnp.int32, (1, len(kv_refs) * span), 1)
    start = jnp.zeros_like(lane)
    for j, (even, odd) in enumerate(masks):
        block = ctx ^ jnp.where(core == 0, even, odd)
        start = jnp.where(lane // span == j, block * span, start)
    key_pos = start + lane % span
    row = lax.broadcasted_iota(jnp.int32, (heads * count, 1), 0) % count
    query_pos = ((ctx * blocks + row // rows) * n_tp + core) * rows + row % rows
    allowed = key_pos <= query_pos
    score = jnp.where(allowed, score, -1e30)
    prob = jnp.where(allowed, jnp.exp(score - jnp.max(score, axis=1, keepdims=True)), 0.0)
    total = jnp.sum(prob, axis=1, keepdims=True)
    mixed = jnp.dot(prob.astype(jnp.bfloat16), value, preferred_element_type=jnp.float32) / total
    mixed = mixed.astype(jnp.bfloat16)
    for h in range(heads):
        out_ref[:, h * head_dim : (h + 1) * head_dim] = mixed[h * count : (h + 1) * count]


def load_kernel(*refs):
    n = len(refs) // 2
    copies = [pltpu.make_async_copy(refs[i], refs[n + i], refs[-1].at[i]) for i in range(n)]
    for copy in copies:
        copy.start()
    for copy in copies:
        copy.wait()


def load(weights, name):
    return call(
        load_kernel,
        [(w.shape, w.dtype) for w in weights],
        *far(weights),
        where=pltpu.HBM,
        scratch=[pltpu.SemaphoreType.DMA((len(weights),))],
        read=2 * sum(w.size for w in weights),
        name=name,
    )


def hidden_units(x, gate_ref, up_ref, down_ref):
    last = (((1,), (1,)), ((), ()))
    gate = lax.dot_general(x, gate_ref[...], last, preferred_element_type=jnp.float32)
    up = lax.dot_general(x, up_ref[...], last, preferred_element_type=jnp.float32)
    hidden = silu_mul(gate, up).astype(jnp.bfloat16)
    return jnp.dot(hidden, down_ref[...], preferred_element_type=jnp.float32)


def first_kernel(blocks, live, mine_ref, other_ref, gain_ref, gate_ref, up_ref, down_ref, *outs):
    own_ref, x_ref, part_ref = outs
    count, width = mine_ref.shape[0], x_ref.shape[1]
    rows = count // blocks
    mine = lax.axis_index("exp")
    summed = (mine_ref[:, :width].astype(jnp.float32) + other_ref[:, :width].astype(jnp.float32)).astype(
        jnp.bfloat16
    )
    shape = (rows, count)
    own = (
        lax.broadcasted_iota(jnp.int32, shape, 0) + mine * rows
        == lax.broadcasted_iota(jnp.int32, shape, 1)
    )
    own = own.astype(jnp.float32).astype(jnp.bfloat16)
    own_ref[...] = jnp.dot(own, summed, preferred_element_type=jnp.float32)
    state = summed.astype(jnp.float32)
    note = mine_ref[:, width:] + other_ref[:, width:]
    inverse = lax.rsqrt(jnp.mean(state * state, axis=1, keepdims=True) + 1e-06)
    normed = (state * inverse * gain_ref[...]).astype(jnp.bfloat16)
    expert = lax.rem(mine, live)
    slots = blocks * CAP
    shape = (slots, note.shape[1])
    pick_lane = (
        lax.broadcasted_iota(jnp.int32, shape, 1)
        == expert * CAP + lax.broadcasted_iota(jnp.int32, shape, 0) % CAP
    )
    pick = lax.dot_general(
        pick_lane.astype(jnp.float32).astype(jnp.bfloat16),
        note,
        (((1,), (1,)), ((), ())),
        preferred_element_type=jnp.float32,
    )
    shape = (slots, count)
    same = (
        lax.broadcasted_iota(jnp.int32, shape, 0) // CAP
        == (lax.broadcasted_iota(jnp.int32, shape, 1) // rows) ^ mine
    )
    pick = jnp.where(same, pick, 0.0).astype(jnp.bfloat16)
    x = jnp.dot(pick, normed, preferred_element_type=jnp.float32).astype(jnp.bfloat16)
    x_ref[...] = x
    part_ref[...] = hidden_units(x, gate_ref, up_ref, down_ref)


def second_kernel(x_ref, part_ref, gate_ref, up_ref, down_ref, *outs):
    result = part_ref[...] + hidden_units(x_ref[...], gate_ref, up_ref, down_ref)
    for m, out_ref in enumerate(outs):
        out_ref[...] = result[m * CAP : (m + 1) * CAP].astype(out_ref.dtype)


def combine_kernel(live, mix_ref, own_ref, *refs):
    back_refs, out_ref = refs[:-1], refs[-1]
    mine = lax.axis_index("exp")
    mix = mix_ref[...]
    lane = lax.broadcasted_iota(jnp.int32, mix.shape, 1)
    total = own_ref[...]
    for m, back_ref in enumerate(back_refs):
        expert = lax.rem(mine ^ m, live)
        back = back_ref[...].astype(jnp.float32)
        for s in range(CAP):
            share = jnp.sum(jnp.where(lane == expert * CAP + s, mix, 0.0), axis=1, keepdims=True)
            total = total + share * back[s : s + 1]
    out_ref[...] = total.astype(out_ref.dtype)


def on_device(
    queries, keys, values, out_weight, norm_gain, routes, route_weight, w_gate, w_up, w_down
):
    blocks, lanes, rows, heads, head_dim = queries.shape
    width = out_weight.shape[1]
    n_exp = lax.axis_size("exp")
    live = n_exp // 2
    count = blocks * rows
    group = heads * n_exp // keys.shape[1]
    note_width = -(-(live * CAP) // LANES) * LANES
    small = (keys, values, queries.reshape(count, heads, head_dim), routes, route_weight)
    kv, query, note, mix = call(
        functools.partial(open_kernel, live, blocks, group),
        [
            ((2 * keys.shape[0], head_dim), jnp.bfloat16),
            ((heads * count, head_dim), jnp.bfloat16),
            ((count, note_width), jnp.bfloat16),
            ((rows, note_width), jnp.float32),
        ],
        *far(small),
        where=pltpu.HBM,
        scratch=[pltpu.VMEM(a.shape, a.dtype) for a in small] + [pltpu.SemaphoreType.DMA((5,))],
        name="open",
    )
    masks, got = gather_ctx(kv)
    (mixed,) = call(
        functools.partial(attend_kernel, masks, blocks),
        [((count, heads * head_dim), jnp.bfloat16)],
        query,
        *got,
        name="attend",
    )
    term = jnp.dot(mixed, out_weight, preferred_element_type=jnp.float32).astype(jnp.bfloat16)
    summed = jnp.concatenate([term, note], axis=1)
    weights = (w_gate[0].T, w_up[0].T, w_down[0])
    got[1], *moving = lax.optimization_barrier((got[1], *weights))
    moved = [swap(w, "tp", 1) for w in moving]
    summed, *weights = lax.optimization_barrier((summed, *weights))
    weights = load(weights, "load_mine")
    steps = [1 << i for i in range(n_exp.bit_length() - 1)]
    for i, step in enumerate(steps):
        other = swap_by_core(summed, "exp", (step, steps[-1 - i]))
        if i < len(steps) - 1:
            summed = (summed.astype(jnp.float32) + other.astype(jnp.float32)).astype(jnp.bfloat16)
    slots = blocks * CAP
    own, x, part = call(
        functools.partial(first_kernel, blocks, live),
        [
            ((rows, width), jnp.float32),
            ((slots, width), jnp.bfloat16),
            ((slots, width), jnp.float32),
        ],
        summed,
        other,
        norm_gain.reshape(1, width),
        *weights,
        flops=6 * slots * w_down.size,
        read=6 * w_down.size,
        name="first",
    )
    results = call(
        second_kernel,
        [((CAP, width), jnp.bfloat16)] * n_exp,
        x,
        part,
        *moved,
        flops=6 * slots * w_down.size,
        read=6 * w_down.size,
        name="second",
    )
    back = [results[0]] + [swap(r, "exp", m) for m, r in enumerate(results) if m]
    (out,) = call(
        functools.partial(combine_kernel, live),
        [((rows, width), jnp.bfloat16)],
        mix,
        own,
        *back,
        kept=jax.ShapeDtypeStruct,
        name="combine",
    )
    return out


def solution(mesh):
    in_specs = (
        P("ctx", "tp", None, "exp", None),
        P("ctx", None, None),
        P("ctx", None, None),
        P("exp", None),
        P(),
        P(("ctx", "exp", "tp"), None),
        P(("ctx", "exp", "tp"), None),
        P("exp", None, "tp"),
        P("exp", None, "tp"),
        P("exp", "tp", None),
    )
    out_specs = P(("ctx", "exp", "tp"), None)
    return jax.shard_map(
        on_device, mesh=mesh, in_specs=in_specs, out_specs=out_specs, check_vma=False
    )
```

time: 38.6 us -> 31.4 us (0.81)
  local copies, waits for them, and re-layouts: 7.33 us -> 0.01 us
  waiting for transfers between devices: 14.3 us -> 9.9 us
  Pallas kernels: 3.75 us -> 7.45 us
  starting transfers between devices: 12.7 us -> 13.4 us
  matrix products: 0 us -> 0.4 us
    unnamed x18 -> x4, local copies, waits for them, and re-layouts: 6.48 us -> 0.01 us
    all_to_all x1 -> x0, waiting for transfers between devices: 5.5 us -> none  [on_device(): lax.all_to_all(result, ('exp', 'tp'), split_axis=0, concat_axis=0, tiled=...]
    ppermute x3 -> x8, starting transfers between devices: 2.78 us -> 7.15 us  [swap(): return lax.ppermute(x, axis, [(i, i ^ mask) for i in range(size)])]
    all_to_all x1 -> x0, starting transfers between devices: 3.72 us -> none  [on_device(): lax.all_to_all(result, ('exp', 'tp'), split_axis=0, concat_axis=0, tiled=...]
    pallas_call x5 -> x6, Pallas kernels: 3.75 us -> 7.45 us  [call(): pl.pallas_call(kernel, out_shape=[kept(shape, dtype) for shape, dtype in...]
    ppermute x3 -> x8, waiting for transfers between devices: 1.78 us -> 5.27 us  [swap(): return lax.ppermute(x, axis, [(i, i ^ mask) for i in range(size)])]
    ppermute x3, waiting for transfers between devices: 7.01 us -> 4.63 us  [swap_by_core(): return lax.ppermute(x, (axis, 'tp'), pairs)]
    dynamic_slice x2 -> x0, local copies, waits for them, and re-layouts: 0.85 us -> none  [the longest x1 0.82 us: on_device(): value_mine = lax.dynamic_index_in_dim(values, kv_head, 1, keepdims=False)]
  transfers between devices with their start and end apart: 7 -> 11, of which waited for: 5 -> 6; matrix products, arithmetic and copies ran while one was open for 0% -> 1% of each run, Pallas kernels for 0% -> 13%
where the time goes in v3:
time: 31.4 us; the launch traced here: 31.2 us
  starting transfers between devices  13.4 us (43%)
  waiting for transfers between devices  9.9 us (32%)
  Pallas kernels  7.45 us (24%)
  matrix products  0.4 us (1%)
    pallas_call x6, Pallas kernels, call(): pl.pallas_call(kernel, out_shape=[kept(shape, dtype) for shape, dtype in...  7.45 us
    ppermute x8, starting transfers between devices, swap(): return lax.ppermute(x, axis, [(i, i ^ mask) for i in range(size)])  7.15 us
    ppermute x3, starting transfers between devices, swap_by_core(): return lax.ppermute(x, (axis, 'tp'), pairs)  6.23 us
    ppermute x8, waiting for transfers between devices, swap(): return lax.ppermute(x, axis, [(i, i ^ mask) for i in range(size)])  5.27 us
    ppermute x3, waiting for transfers between devices, swap_by_core(): return lax.ppermute(x, (axis, 'tp'), pairs)  4.63 us
  transfers between devices with their start and end apart: 11, of which 6 were waited for; matrix products, arithmetic and copies ran while one was open for 1% of the time, Pallas kernels for 13%

profile of v3, /device:TPU:0, one launch (start us, length us, event | category | flops | bytes accessed | tf_op | source)
XLA Modules:
  0.0 31.2 jit_solution(10047752348351220557)
XLA Ops:
  0.0 0.0 copy-start
  0.0 1.2 %open.1 = (bf16[64,128]{1,0:T(8,128)(2,1)S(1)}, bf16[32,128]{1,0:T(8,128)(2,1)S(1)}, bf16[16,128]{1,0:T(8,128)(2,1)S(1)}, f32[4,128]{1,0:T(4,128)S(1)}) custom-call(bf16[32,4,128]{2,1,0:T(4,128)(2,1)} %refs_0_.1, bf16[32,4,128]{2,1,0:T(4,128)(2,1)} %refs_1_.1, bf16[16,2,128]{2,1,0:T(2,128)(2,1)} %bitcast.18, s32[4,8]{1,0:T(4,128)} %refs_3_.1, f32[4,8]{1,0:T(4,128)} %refs_4_.1), custom_call_target="tpu_custom_call" | custom-call | tf_op jit(solution)/shard_map/open/pallas_call | solution.py:52
  1.2 3.1 %collective-permute-start = (bf16[64,128]{1,0:T(8,128)(2,1)S(1)}, bf16[64,128]{1,0:T(8,128)(2,1)S(1)}, u32[]{:S(2)}, u32[]{:S(2)}) collective-permute-start(bf16[64,128]{1,0:T(8,128)(2,1)S(1)} %get-tuple-element.28.refs_0_), channel_id=1, source_target_pairs={{0,8},{1,25},{8,0},{9,17},{16,24},{17,9},{24,16},{25,1},{2,10},{3,... | collective-permute-start | bytes 49160 | tf_op jit(solution)/shard_map/ppermute | solution.py:31
  4.3 2.6 %collective-permute-start.2 = (bf16[64,128]{1,0:T(8,128)(2,1)S(1)}, bf16[64,128]{1,0:T(8,128)(2,1)S(1)}, u32[]{:S(2)}, u32[]{:S(2)}) collective-permute-start(bf16[64,128]{1,0:T(8,128)(2,1)S(1)} %get-tuple-element.28.refs_0_), channel_id=1, source_target_pairs={{0,16},{8,24},{16,0},{24,8},{1,17},{9,25},{17,1},{25,9},{2,18},{10... | collective-permute-start | bytes 49160 | tf_op jit(solution)/shard_map/ppermute | solution.py:21
  6.9 0.0 collective-permute-done.refs_1_
  6.9 0.1 collective-permute-start.1
  7.0 0.4 %collective-permute-start.5 = (bf16[192,4096]{1,0:T(8,128)(2,1)}, bf16[192,4096]{1,0:T(8,128)(2,1)S(1)}, u32[]{:S(2)}, u32[]{:S(2)}) collective-permute-start(bf16[192,4096]{1,0:T(8,128)(2,1)} %bitcast.12), channel_id=1, source_target_pairs={{0,1},{1,0},{2,3},{3,2},{4,5},{5,4},{6,7},{7,6},{8,9},{9,8},{10,11... | collective-permute-start | bytes 4718600 | tf_op jit(solution)/shard_map/ppermute | solution.py:21
  7.4 0.1 collective-permute-start.6
  7.5 0.4 %collective-permute-start.7 = (bf16[192,4096]{1,0:T(8,128)(2,1)}, bf16[192,4096]{1,0:T(8,128)(2,1)S(1)}, u32[]{:S(2)}, u32[]{:S(2)}) collective-permute-start(bf16[192,4096]{1,0:T(8,128)(2,1)} %bitcast.16), channel_id=1, source_target_pairs={{0,1},{1,0},{2,3},{3,2},{4,5},{5,4},{6,7},{7,6},{8,9},{9,8},{10,11... | collective-permute-start | bytes 4718600 | tf_op jit(solution)/shard_map/ppermute | solution.py:21
  7.9 1.1 %collective-permute-done.2.refs_3_ = bf16[64,128]{1,0:T(8,128)(2,1)S(1)} collective-permute-done((bf16[64,128]{1,0:T(8,128)(2,1)S(1)}, bf16[64,128]{1,0:T(8,128)(2,1)S(1)}, u32[]{:S(2)}, u32[]{:S(2)}) %collective-permute-start.2) | collective-permute-done | bytes 16416 | tf_op jit(solution)/shard_map/ppermute | solution.py:21
  9.0 0.0 collective-permute-done.1.refs_2_
  9.0 0.3 %attend.1 = bf16[16,256]{1,0:T(8,128)(2,1)S(1)} custom-call(bf16[32,128]{1,0:T(8,128)(2,1)S(1)} %get-tuple-element.27.q_ref, bf16[64,128]{1,0:T(8,128)(2,1)S(1)} %get-tuple-element.28.refs_0_, bf16[64,128]{1,0:T(8,128)(2,1)S(1)} %collective-permute-done.refs_1_, bf16[64,128]{1,0:T(8,128)(2,1)S(1)} %collective-permute-done.1.refs_2_, ...), custom_call_target="tpu_custom_call" | custom-call | tf_op jit(solution)/shard_map/attend/pallas_call | solution.py:52
  9.4 0.0 copy-done
  9.4 0.4 %convolution_convert_fusion = bf16[16,4096]{1,0:T(8,128)(2,1)S(1)} fusion(bf16[16,256]{1,0:T(8,128)(2,1)S(1)} %attend.1, bf16[256,4096]{1,0:T(8,128)(2,1)S(1)} %copy-done), kind=kOutput, calls=%fused_computation | convolution fusion | flops 33619968 | bytes 2236416 | tf_op jit(solution)/shard_map/dot_general | solution.py:263
  9.8 1.6 %collective-permute-start.3 = (bf16[16,4224]{1,0:T(8,128)(2,1)S(1)}, bf16[16,4224]{1,0:T(8,128)(2,1)S(1)}, u32[]{:S(2)}, u32[]{:S(2)}) collective-permute-start(bf16[16,4224]{1,0:T(8,128)(2,1)S(1)} %pad_maximum_fusion), channel_id=1, source_target_pairs={{0,2},{1,5},{2,0},{3,7},{4,6},{5,1},{6,4},{7,3},{8,10},{9,13},{10,... | collective-permute-start | bytes 405512 | tf_op jit(solution)/shard_map/ppermute | solution.py:31
  11.3 3.5 %collective-permute-done.3 = bf16[16,4224]{1,0:T(8,128)(2,1)S(1)} collective-permute-done((bf16[16,4224]{1,0:T(8,128)(2,1)S(1)}, bf16[16,4224]{1,0:T(8,128)(2,1)S(1)}, u32[]{:S(2)}, u32[]{:S(2)}) %collective-permute-start.3) | collective-permute-done | bytes 135200 | tf_op jit(solution)/shard_map/ppermute | solution.py:31
  14.9 0.0 copy-start.1
  14.9 1.6 %collective-permute-start.4 = (bf16[16,4224]{1,0:T(8,128)(2,1)S(1)}, bf16[16,4224]{1,0:T(8,128)(2,1)S(1)}, u32[]{:S(2)}, u32[]{:S(2)}) collective-permute-start(bf16[16,4224]{1,0:T(8,128)(2,1)S(1)} %add_convert_fusion.mine_ref), channel_id=1, source_target_pairs={{0,4},{1,3},{2,6},{3,1},{4,0},{5,7},{6,2},{7,5},{8,12},{9,11},{10,... | collective-permute-start | bytes 405512 | tf_op jit(solution)/shard_map/ppermute | solution.py:31
  16.5 2.4 %load_mine.1 = (bf16[192,4096]{1,0:T(8,128)(2,1)S(1)}, bf16[192,4096]{1,0:T(8,128)(2,1)S(1)}, bf16[192,4096]{1,0:T(8,128)(2,1)S(1)}) custom-call(bf16[192,4096]{1,0:T(8,128)(2,1)} %bitcast.13, bf16[192,4096]{1,0:T(8,128)(2,1)} %bitcast.15, bf16[192,4096]{1,0:T(8,128)(2,1)} %bitcast.17), custom_call_target="tpu_custom_call" | custom-call | bytes 4718592 | tf_op jit(solution)/shard_map/load_mine/pallas_call | solution.py:52
  18.9 1.1 %collective-permute-done.4.other_ref = bf16[16,4224]{1,0:T(8,128)(2,1)S(1)} collective-permute-done((bf16[16,4224]{1,0:T(8,128)(2,1)S(1)}, bf16[16,4224]{1,0:T(8,128)(2,1)S(1)}, u32[]{:S(2)}, u32[]{:S(2)}) %collective-permute-start.4) | collective-permute-done | bytes 135200 | tf_op jit(solution)/shard_map/ppermute | solution.py:31
  20.0 1.5 %first.1 = (f32[4,4096]{1,0:T(4,128)S(1)}, bf16[8,4096]{1,0:T(8,128)(2,1)S(1)}, f32[8,4096]{1,0:T(8,128)S(1)}) custom-call(bf16[16,4224]{1,0:T(8,128)(2,1)S(1)} %add_convert_fusion.mine_ref, bf16[16,4224]{1,0:T(8,128)(2,1)S(1)} %collective-permute-done.4.other_ref, f32[1,4096]{1,0:T(1,128)S(1)} %bitcast.11, ...), custom_call_target="tpu_custom_call" | custom-call | flops 37748736 | bytes 4718592 | tf_op jit(solution)/shard_map/first/pallas_call | solution.py:52
  21.5 0.0 collective-permute-done.5.gate_ref
  21.5 0.0 collective-permute-done.6.up_ref
  21.5 0.0 collective-permute-done.7.down_ref
  21.5 1.2 %second.1 = (bf16[2,4096]{1,0:T(2,128)(2,1)S(1)}, bf16[2,4096]{1,0:T(2,128)(2,1)S(1)}, bf16[2,4096]{1,0:T(2,128)(2,1)S(1)}, bf16[2,4096]{1,0:T(2,128)(2,1)S(1)}) custom-call(bf16[8,4096]{1,0:T(8,128)(2,1)S(1)} %get-tuple-element.38.x_ref, f32[8,4096]{1,0:T(8,128)S(1)} %get-tuple-element.39.part_ref, bf16[192,4096]{1,0:T(8,128)(2,1)S(1)} %collective-permute-done.5.gate_ref, ...), custom_call_target="tpu_custom_call" | custom-call | flops 37748736 | bytes 4718592 | tf_op jit(solution)/shard_map/second/pallas_call | solution.py:52
  22.7 1.5 %collective-permute-start.8 = (bf16[2,4096]{1,0:T(2,128)(2,1)S(1)}, bf16[2,4096]{1,0:T(2,128)(2,1)S(1)}, u32[]{:S(2)}, u32[]{:S(2)}) collective-permute-start(bf16[2,4096]{1,0:T(2,128)(2,1)S(1)} %get-tuple-element.44), channel_id=1, source_target_pairs={{0,2},{2,0},{4,6},{6,4},{1,3},{3,1},{5,7},{7,5},{8,10},{10,8},{12,... | collective-permute-start | bytes 49160 | tf_op jit(solution)/shard_map/ppermute | solution.py:21
  24.3 1.5 %collective-permute-start.9 = (bf16[2,4096]{1,0:T(2,128)(2,1)S(1)}, bf16[2,4096]{1,0:T(2,128)(2,1)S(1)}, u32[]{:S(2)}, u32[]{:S(2)}) collective-permute-start(bf16[2,4096]{1,0:T(2,128)(2,1)S(1)} %get-tuple-element.45), channel_id=1, source_target_pairs={{0,4},{2,6},{4,0},{6,2},{1,5},{3,7},{5,1},{7,3},{8,12},{10,14},{12... | collective-permute-start | bytes 49160 | tf_op jit(solution)/shard_map/ppermute | solution.py:21
  25.8 0.5 %collective-permute-start.10 = (bf16[2,4096]{1,0:T(2,128)(2,1)S(1)}, bf16[2,4096]{1,0:T(2,128)(2,1)S(1)}, u32[]{:S(2)}, u32[]{:S(2)}) collective-permute-start(bf16[2,4096]{1,0:T(2,128)(2,1)S(1)} %get-tuple-element.46), channel_id=1, source_target_pairs={{0,6},{2,4},{4,2},{6,0},{1,7},{3,5},{5,3},{7,1},{8,14},{10,12},{12... | collective-permute-start | bytes 49160 | tf_op jit(solution)/shard_map/ppermute | solution.py:21
  26.3 0.2 collective-permute-done.8.refs_1_
  26.5 1.5 %collective-permute-done.9.refs_2_ = bf16[2,4096]{1,0:T(2,128)(2,1)S(1)} collective-permute-done((bf16[2,4096]{1,0:T(2,128)(2,1)S(1)}, bf16[2,4096]{1,0:T(2,128)(2,1)S(1)}, u32[]{:S(2)}, u32[]{:S(2)}) %collective-permute-start.9) | collective-permute-done | bytes 16416 | tf_op jit(solution)/shard_map/ppermute | solution.py:21
  28.0 2.4 %collective-permute-done.10.refs_3_ = bf16[2,4096]{1,0:T(2,128)(2,1)S(1)} collective-permute-done((bf16[2,4096]{1,0:T(2,128)(2,1)S(1)}, bf16[2,4096]{1,0:T(2,128)(2,1)S(1)}, u32[]{:S(2)}, u32[]{:S(2)}) %collective-permute-start.10) | collective-permute-done | bytes 16416 | tf_op jit(solution)/shard_map/ppermute | solution.py:21
  30.4 0.8 %combine.1 = bf16[4,4096]{1,0:T(4,128)(2,1)} custom-call(f32[4,128]{1,0:T(4,128)S(1)} %get-tuple-element.26.mix_ref, f32[4,4096]{1,0:T(4,128)S(1)} %get-tuple-element.37.own_ref, bf16[2,4096]{1,0:T(2,128)(2,1)S(1)} %get-tuple-element.43.refs_0_, bf16[2,4096]{1,0:T(2,128)(2,1)S(1)} %collective-permute-done.8.refs_1_, ...), custom_call_target="tpu_custom_call" | custom-call | tf_op jit(solution)/shard_map/combine/pallas_call | solution.py:52
  (3 shorter events, 0.1 us)
Async XLA Ops:
  0.0 9.4 %copy-start = (bf16[256,4096]{1,0:T(8,128)(2,1)S(1)}, bf16[256,4096]{1,0:T(8,128)(2,1)}, u32[]{:S(2)}) copy-start(bf16[256,4096]{1,0:T(8,128)(2,1)} %param.13) | copy-start | bytes 6291460
  1.2 5.7 %collective-permute-start = (bf16[64,128]{1,0:T(8,128)(2,1)S(1)}, bf16[64,128]{1,0:T(8,128)(2,1)S(1)}, u32[]{:S(2)}, u32[]{:S(2)}) collective-permute-start(bf16[64,128]{1,0:T(8,128)(2,1)S(1)} %get-tuple-element.28.refs_0_), channel_id=1, source_target_pairs={{0,8},{1,25},{8,0},{9,17},{16,24},{17,9},{24,16},{25,1},{2,10},{3,... | collective-permute-start | bytes 49160 | tf_op jit(solution)/shard_map/ppermute | solution.py:31
  4.3 4.7 %collective-permute-start.2 = (bf16[64,128]{1,0:T(8,128)(2,1)S(1)}, bf16[64,128]{1,0:T(8,128)(2,1)S(1)}, u32[]{:S(2)}, u32[]{:S(2)}) collective-permute-start(bf16[64,128]{1,0:T(8,128)(2,1)S(1)} %get-tuple-element.28.refs_0_), channel_id=1, source_target_pairs={{0,16},{8,24},{16,0},{24,8},{1,17},{9,25},{17,1},{25,9},{2,18},{10... | collective-permute-start | bytes 49160 | tf_op jit(solution)/shard_map/ppermute | solution.py:21
  6.9 2.1 %collective-permute-start.1 = (bf16[64,128]{1,0:T(8,128)(2,1)S(1)}, bf16[64,128]{1,0:T(8,128)(2,1)S(1)}, u32[]{:S(2)}, u32[]{:S(2)}) collective-permute-start(bf16[64,128]{1,0:T(8,128)(2,1)S(1)} %collective-permute-done.refs_1_), channel_id=1, source_target_pairs={{0,1},{1,0},{2,3},{3,2},{4,5},{5,4},{6,7},{7,6},{8,9},{9,8},{10,11... | collective-permute-start | bytes 49160 | tf_op jit(solution)/shard_map/ppermute | solution.py:21
  7.0 14.5 %collective-permute-start.5 = (bf16[192,4096]{1,0:T(8,128)(2,1)}, bf16[192,4096]{1,0:T(8,128)(2,1)S(1)}, u32[]{:S(2)}, u32[]{:S(2)}) collective-permute-start(bf16[192,4096]{1,0:T(8,128)(2,1)} %bitcast.12), channel_id=1, source_target_pairs={{0,1},{1,0},{2,3},{3,2},{4,5},{5,4},{6,7},{7,6},{8,9},{9,8},{10,11... | collective-permute-start | bytes 4718600 | tf_op jit(solution)/shard_map/ppermute | solution.py:21
  7.4 14.1 %collective-permute-start.6 = (bf16[192,4096]{1,0:T(8,128)(2,1)}, bf16[192,4096]{1,0:T(8,128)(2,1)S(1)}, u32[]{:S(2)}, u32[]{:S(2)}) collective-permute-start(bf16[192,4096]{1,0:T(8,128)(2,1)} %bitcast.14), channel_id=1, source_target_pairs={{0,1},{1,0},{2,3},{3,2},{4,5},{5,4},{6,7},{7,6},{8,9},{9,8},{10,11... | collective-permute-start | bytes 4718600 | tf_op jit(solution)/shard_map/ppermute | solution.py:21
  7.5 14.0 %collective-permute-start.7 = (bf16[192,4096]{1,0:T(8,128)(2,1)}, bf16[192,4096]{1,0:T(8,128)(2,1)S(1)}, u32[]{:S(2)}, u32[]{:S(2)}) collective-permute-start(bf16[192,4096]{1,0:T(8,128)(2,1)} %bitcast.16), channel_id=1, source_target_pairs={{0,1},{1,0},{2,3},{3,2},{4,5},{5,4},{6,7},{7,6},{8,9},{9,8},{10,11... | collective-permute-start | bytes 4718600 | tf_op jit(solution)/shard_map/ppermute | solution.py:21
  9.8 5.1 %collective-permute-start.3 = (bf16[16,4224]{1,0:T(8,128)(2,1)S(1)}, bf16[16,4224]{1,0:T(8,128)(2,1)S(1)}, u32[]{:S(2)}, u32[]{:S(2)}) collective-permute-start(bf16[16,4224]{1,0:T(8,128)(2,1)S(1)} %pad_maximum_fusion), channel_id=1, source_target_pairs={{0,2},{1,5},{2,0},{3,7},{4,6},{5,1},{6,4},{7,3},{8,10},{9,13},{10,... | collective-permute-start | bytes 405512 | tf_op jit(solution)/shard_map/ppermute | solution.py:31
  14.9 5.1 %copy-start.1 = (f32[4096]{0:T(1024)S(1)}, f32[4096]{0:T(1024)}, u32[]{:S(2)}) copy-start(f32[4096]{0:T(1024)} %param.14) | copy-start | bytes 49156
  14.9 5.1 %collective-permute-start.4 = (bf16[16,4224]{1,0:T(8,128)(2,1)S(1)}, bf16[16,4224]{1,0:T(8,128)(2,1)S(1)}, u32[]{:S(2)}, u32[]{:S(2)}) collective-permute-start(bf16[16,4224]{1,0:T(8,128)(2,1)S(1)} %add_convert_fusion.mine_ref), channel_id=1, source_target_pairs={{0,4},{1,3},{2,6},{3,1},{4,0},{5,7},{6,2},{7,5},{8,12},{9,11},{10,... | collective-permute-start | bytes 405512 | tf_op jit(solution)/shard_map/ppermute | solution.py:31
  22.7 3.8 %collective-permute-start.8 = (bf16[2,4096]{1,0:T(2,128)(2,1)S(1)}, bf16[2,4096]{1,0:T(2,128)(2,1)S(1)}, u32[]{:S(2)}, u32[]{:S(2)}) collective-permute-start(bf16[2,4096]{1,0:T(2,128)(2,1)S(1)} %get-tuple-element.44), channel_id=1, source_target_pairs={{0,2},{2,0},{4,6},{6,4},{1,3},{3,1},{5,7},{7,5},{8,10},{10,8},{12,... | collective-permute-start | bytes 49160 | tf_op jit(solution)/shard_map/ppermute | solution.py:21
  24.3 3.7 %collective-permute-start.9 = (bf16[2,4096]{1,0:T(2,128)(2,1)S(1)}, bf16[2,4096]{1,0:T(2,128)(2,1)S(1)}, u32[]{:S(2)}, u32[]{:S(2)}) collective-permute-start(bf16[2,4096]{1,0:T(2,128)(2,1)S(1)} %get-tuple-element.45), channel_id=1, source_target_pairs={{0,4},{2,6},{4,0},{6,2},{1,5},{3,7},{5,1},{7,3},{8,12},{10,14},{12... | collective-permute-start | bytes 49160 | tf_op jit(solution)/shard_map/ppermute | solution.py:21
  25.8 4.6 %collective-permute-start.10 = (bf16[2,4096]{1,0:T(2,128)(2,1)S(1)}, bf16[2,4096]{1,0:T(2,128)(2,1)S(1)}, u32[]{:S(2)}, u32[]{:S(2)}) collective-permute-start(bf16[2,4096]{1,0:T(2,128)(2,1)S(1)} %get-tuple-element.46), channel_id=1, source_target_pairs={{0,6},{2,4},{4,2},{6,0},{1,7},{3,5},{5,3},{7,1},{8,14},{10,12},{12... | collective-permute-start | bytes 49160 | tf_op jit(solution)/shard_map/ppermute | solution.py:21

commit v4 on v3

--- a/solution.py
+++ b/solution.py
@@ -61,26 +61,33 @@
     )(*args)
 
 
-def open_kernel(live, blocks, group, *refs):
-    ins, (kv_ref, q_ref, note_ref, mix_ref), held = refs[:5], refs[5:9], refs[9:14]
-    sems = refs[14]
-    copies = [pltpu.make_async_copy(i, h, sems.at[n]) for n, (i, h) in enumerate(zip(ins, held))]
+def open_kernel(heads, group, key_hbm, value_hbm, kv_ref, key_ref, value_ref, sems):
+    copies = [
+        pltpu.make_async_copy(key_hbm, key_ref, sems.at[0]),
+        pltpu.make_async_copy(value_hbm, value_ref, sems.at[1]),
+    ]
     for copy in copies:
         copy.start()
-    key_ref, value_ref, query_ref, routes_ref, weight_ref = held
     span = key_ref.shape[0]
-    heads = query_ref.shape[1]
-    mine = lax.axis_index("exp")
-    kv_head = mine * heads // group
+    kv_head = lax.axis_index("exp") * heads // group
     for n, ref in enumerate((key_ref, value_ref)):
         copies[n].wait()
         wanted = lax.broadcasted_iota(jnp.int32, ref.shape, 1) == kv_head
         kept = jnp.sum(jnp.where(wanted, ref[...].astype(jnp.float32), 0.0), axis=1)
         kv_ref[n * span : (n + 1) * span, :] = kept.astype(kv_ref.dtype)
-    copies[2].wait()
+
+
+def route_kernel(live, blocks, *refs):
+    ins, (q_ref, note_ref, mix_ref), held, sems = refs[:3], refs[3:6], refs[6:9], refs[9]
+    copies = [pltpu.make_async_copy(i, h, sems.at[n]) for n, (i, h) in enumerate(zip(ins, held))]
+    for copy in copies:
+        copy.start()
+    query_ref, routes_ref, weight_ref = held
+    heads = query_ref.shape[1]
+    mine = lax.axis_index("exp")
+    for copy in copies:
+        copy.wait()
     q_ref[...] = jnp.concatenate([query_ref[:, h, :] for h in range(heads)], axis=0)
-    copies[3].wait()
-    copies[4].wait()
     rows, picks = routes_ref.shape
     width = mix_ref.shape[1]
     routes, weight = routes_ref[...], weight_ref[...]
@@ -164,7 +171,7 @@
     return jnp.dot(hidden, down_ref[...], preferred_element_type=jnp.float32)
 
 
-def first_kernel(blocks, live, mine_ref, other_ref, gain_ref, gate_ref, up_ref, down_ref, *outs):
+def first_kernel(blocks, live, masks, mine_ref, other_ref, gain_ref, gate_ref, up_ref, down_ref, *outs):
     own_ref, x_ref, part_ref = outs
     count, width = mine_ref.shape[0], x_ref.shape[1]
     rows = count // blocks
@@ -197,10 +204,12 @@
         preferred_element_type=jnp.float32,
     )
     shape = (slots, count)
-    same = (
-        lax.broadcasted_iota(jnp.int32, shape, 0) // CAP
-        == (lax.broadcasted_iota(jnp.int32, shape, 1) // rows) ^ mine
-    )
+    place = lax.broadcasted_iota(jnp.int32, shape, 0) // CAP
+    core = lax.axis_index("tp")
+    mask = jnp.zeros(shape, jnp.int32)
+    for i, (even, odd) in enumerate(masks):
+        mask = jnp.where(place == i, jnp.where(core == 0, even, odd), mask)
+    same = mask == (lax.broadcasted_iota(jnp.int32, shape, 1) // rows) ^ mine
     pick = jnp.where(same, pick, 0.0).astype(jnp.bfloat16)
     x = jnp.dot(pick, normed, preferred_element_type=jnp.float32).astype(jnp.bfloat16)
     x_ref[...] = x
@@ -213,14 +222,15 @@
         out_ref[...] = result[m * CAP : (m + 1) * CAP].astype(out_ref.dtype)
 
 
-def combine_kernel(live, mix_ref, own_ref, *refs):
+def combine_kernel(live, masks, mix_ref, own_ref, *refs):
     back_refs, out_ref = refs[:-1], refs[-1]
     mine = lax.axis_index("exp")
     mix = mix_ref[...]
     lane = lax.broadcasted_iota(jnp.int32, mix.shape, 1)
     total = own_ref[...]
-    for m, back_ref in enumerate(back_refs):
-        expert = lax.rem(mine ^ m, live)
+    core = lax.axis_index("tp")
+    for (even, odd), back_ref in zip(masks, back_refs):
+        expert = lax.rem(mine ^ jnp.where(core == 0, even, odd), live)
         back = back_ref[...].astype(jnp.float32)
         for s in range(CAP):
             share = jnp.sum(jnp.where(lane == expert * CAP + s, mix, 0.0), axis=1, keepdims=True)
@@ -238,21 +248,32 @@
     count = blocks * rows
     group = heads * n_exp // keys.shape[1]
     note_width = -(-(live * CAP) // LANES) * LANES
-    small = (keys, values, queries.reshape(count, heads, head_dim), routes, route_weight)
-    kv, query, note, mix = call(
-        functools.partial(open_kernel, live, blocks, group),
+    (kv,) = call(
+        functools.partial(open_kernel, heads, group),
+        [((2 * keys.shape[0], head_dim), jnp.bfloat16)],
+        *far((keys, values)),
+        where=pltpu.HBM,
+        scratch=[pltpu.VMEM(a.shape, a.dtype) for a in (keys, values)]
+        + [pltpu.SemaphoreType.DMA((2,))],
+        name="open",
+    )
+    masks, got = gather_ctx(kv)
+    weights = (w_gate[0].T, w_up[0].T, w_down[0])
+    small = (queries.reshape(count, heads, head_dim), routes, route_weight)
+    got[1], *tied = lax.optimization_barrier((got[1], *weights, *small))
+    moved = [swap(w, "tp", 1) for w in tied[:3]]
+    query, note, mix = call(
+        functools.partial(route_kernel, live, blocks),
         [
-            ((2 * keys.shape[0], head_dim), jnp.bfloat16),
             ((heads * count, head_dim), jnp.bfloat16),
             ((count, note_width), jnp.bfloat16),
             ((rows, note_width), jnp.float32),
         ],
-        *far(small),
+        *far(tied[3:]),
         where=pltpu.HBM,
-        scratch=[pltpu.VMEM(a.shape, a.dtype) for a in small] + [pltpu.SemaphoreType.DMA((5,))],
-        name="open",
-    )
-    masks, got = gather_ctx(kv)
+        scratch=[pltpu.VMEM(a.shape, a.dtype) for a in small] + [pltpu.SemaphoreType.DMA((3,))],
+        name="route",
+    )
     (mixed,) = call(
         functools.partial(attend_kernel, masks, blocks),
         [((count, heads * head_dim), jnp.bfloat16)],
@@ -262,9 +283,6 @@
     )
     term = jnp.dot(mixed, out_weight, preferred_element_type=jnp.float32).astype(jnp.bfloat16)
     summed = jnp.concatenate([term, note], axis=1)
-    weights = (w_gate[0].T, w_up[0].T, w_down[0])
-    got[1], *moving = lax.optimization_barrier((got[1], *weights))
-    moved = [swap(w, "tp", 1) for w in moving]
     summed, *weights = lax.optimization_barrier((summed, *weights))
     weights = load(weights, "load_mine")
     steps = [1 << i for i in range(n_exp.bit_length() - 1)]
@@ -272,9 +290,10 @@
         other = swap_by_core(summed, "exp", (step, steps[-1 - i]))
         if i < len(steps) - 1:
             summed = (summed.astype(jnp.float32) + other.astype(jnp.float32)).astype(jnp.bfloat16)
+    masks = [(0, 0), (3, 3), (1, 2), (2, 1)]
     slots = blocks * CAP
     own, x, part = call(
-        functools.partial(first_kernel, blocks, live),
+        functools.partial(first_kernel, blocks, live, masks),
         [
             ((rows, width), jnp.float32),
             ((slots, width), jnp.bfloat16),
@@ -298,9 +317,12 @@
         read=6 * w_down.size,
         name="second",
     )
-    back = [results[0]] + [swap(r, "exp", m) for m, r in enumerate(results) if m]
+    back = [
+        results[0] if even == 0 else swap_by_core(results[i], "exp", (even, odd))
+        for i, (even, odd) in enumerate(masks)
+    ]
     (out,) = call(
-        functools.partial(combine_kernel, live),
+        functools.partial(combine_kernel, live, masks),
         [((rows, width), jnp.bfloat16)],
         mix,
         own,

time: 31.4 us -> 30.4 us (0.968)
  waiting for transfers between devices: 9.9 us -> 8.12 us
  Pallas kernels: 7.45 us -> 8.13 us
    ppermute x8 -> x5, waiting for transfers between devices: 5.27 us -> 0.26 us  [swap(): return lax.ppermute(x, axis, [(i, i ^ mask) for i in range(size)])]
    ppermute x3 -> x6, starting transfers between devices: 6.23 us -> 9.77 us  [swap_by_core(): return lax.ppermute(x, (axis, 'tp'), pairs)]
    ppermute x8 -> x5, starting transfers between devices: 7.15 us -> 3.61 us  [swap(): return lax.ppermute(x, axis, [(i, i ^ mask) for i in range(size)])]
    ppermute x3 -> x6, waiting for transfers between devices: 4.63 us -> 7.86 us  [swap_by_core(): return lax.ppermute(x, (axis, 'tp'), pairs)]
    pallas_call x6 -> x7, Pallas kernels: 7.45 us -> 8.13 us  [call(): pl.pallas_call(kernel, out_shape=[kept(shape, dtype) for shape, dtype in...]
  transfers between devices with their start and end apart: 11 -> 11, of which waited for: 6 -> 6; matrix products, arithmetic and copies ran while one was open for 1% -> 1% of each run, Pallas kernels for 13% -> 17%
where the time goes in v4:
time: 30.4 us; the launch traced here: 30.2 us
  starting transfers between devices  13.4 us (44%)
  Pallas kernels  8.13 us (27%)
  waiting for transfers between devices  8.12 us (27%)
  matrix products  0.4 us (1%)
    ppermute x6, starting transfers between devices, swap_by_core(): return lax.ppermute(x, (axis, 'tp'), pairs)  9.77 us
    pallas_call x7, Pallas kernels, call(): pl.pallas_call(kernel, out_shape=[kept(shape, dtype) for shape, dtype in...  8.13 us
    ppermute x6, waiting for transfers between devices, swap_by_core(): return lax.ppermute(x, (axis, 'tp'), pairs)  7.86 us
    ppermute x5, starting transfers between devices, swap(): return lax.ppermute(x, axis, [(i, i ^ mask) for i in range(size)])  3.61 us
  transfers between devices with their start and end apart: 11, of which 6 were waited for; matrix products, arithmetic and copies ran while one was open for 1% of the time, Pallas kernels for 17%

profile of v4, /device:TPU:0, one launch (start us, length us, event | category | flops | bytes accessed | tf_op | source)
XLA Modules:
  0.0 30.2 jit_solution(5322722491971505394)
XLA Ops:
  0.0 0.0 copy-start
  0.0 1.0 %open.1.refs_0_ = bf16[64,128]{1,0:T(8,128)(2,1)S(1)} custom-call(bf16[32,4,128]{2,1,0:T(4,128)(2,1)} %key_hbm.1, bf16[32,4,128]{2,1,0:T(4,128)(2,1)} %value_hbm.1), custom_call_target="tpu_custom_call" | custom-call | tf_op jit(solution)/shard_map/open/pallas_call | solution.py:52
  1.0 3.1 %collective-permute-start = (bf16[64,128]{1,0:T(8,128)(2,1)S(1)}, bf16[64,128]{1,0:T(8,128)(2,1)S(1)}, u32[]{:S(2)}, u32[]{:S(2)}) collective-permute-start(bf16[64,128]{1,0:T(8,128)(2,1)S(1)} %open.1.refs_0_), channel_id=1, source_target_pairs={{0,8},{1,25},{8,0},{9,17},{16,24},{17,9},{24,16},{25,1},{2,10},{3,... | collective-permute-start | bytes 49160 | tf_op jit(solution)/shard_map/ppermute | solution.py:31
  4.1 2.6 %collective-permute-start.2 = (bf16[64,128]{1,0:T(8,128)(2,1)S(1)}, bf16[64,128]{1,0:T(8,128)(2,1)S(1)}, u32[]{:S(2)}, u32[]{:S(2)}) collective-permute-start(bf16[64,128]{1,0:T(8,128)(2,1)S(1)} %open.1.refs_0_), channel_id=1, source_target_pairs={{0,16},{8,24},{16,0},{24,8},{1,17},{9,25},{17,1},{25,9},{2,18},{10... | collective-permute-start | bytes 49160 | tf_op jit(solution)/shard_map/ppermute | solution.py:21
  6.7 0.0 collective-permute-done.refs_1_
  6.7 0.1 collective-permute-start.1
  6.8 0.4 %collective-permute-start.5 = (bf16[192,4096]{1,0:T(8,128)(2,1)}, bf16[192,4096]{1,0:T(8,128)(2,1)S(1)}, u32[]{:S(2)}, u32[]{:S(2)}) collective-permute-start(bf16[192,4096]{1,0:T(8,128)(2,1)} %bitcast.12), channel_id=1, source_target_pairs={{0,1},{1,0},{2,3},{3,2},{4,5},{5,4},{6,7},{7,6},{8,9},{9,8},{10,11... | collective-permute-start | bytes 4718600 | tf_op jit(solution)/shard_map/ppermute | solution.py:21
  7.2 0.1 collective-permute-start.6
  7.4 0.4 %collective-permute-start.7 = (bf16[192,4096]{1,0:T(8,128)(2,1)}, bf16[192,4096]{1,0:T(8,128)(2,1)S(1)}, u32[]{:S(2)}, u32[]{:S(2)}) collective-permute-start(bf16[192,4096]{1,0:T(8,128)(2,1)} %bitcast.16), channel_id=1, source_target_pairs={{0,1},{1,0},{2,3},{3,2},{4,5},{5,4},{6,7},{7,6},{8,9},{9,8},{10,11... | collective-permute-start | bytes 4718600 | tf_op jit(solution)/shard_map/ppermute | solution.py:21
  7.8 0.8 %route.1 = (bf16[32,128]{1,0:T(8,128)(2,1)S(1)}, bf16[16,128]{1,0:T(8,128)(2,1)S(1)}, f32[4,128]{1,0:T(4,128)S(1)}) custom-call(bf16[16,2,128]{2,1,0:T(2,128)(2,1)} %bitcast.18, s32[4,8]{1,0:T(4,128)} %refs_1_, f32[4,8]{1,0:T(4,128)} %refs_2_), custom_call_target="tpu_custom_call" | custom-call | tf_op jit(solution)/shard_map/route/pallas_call | solution.py:52
  8.6 0.2 collective-permute-done.2.refs_3_
  8.9 0.0 collective-permute-done.1.refs_2_
  8.9 0.3 %attend.1 = bf16[16,256]{1,0:T(8,128)(2,1)S(1)} custom-call(bf16[32,128]{1,0:T(8,128)(2,1)S(1)} %get-tuple-element.33.q_ref, bf16[64,128]{1,0:T(8,128)(2,1)S(1)} %open.1.refs_0_, bf16[64,128]{1,0:T(8,128)(2,1)S(1)} %collective-permute-done.refs_1_, bf16[64,128]{1,0:T(8,128)(2,1)S(1)} %collective-permute-done.1.refs_2_, ...), custom_call_target="tpu_custom_call" | custom-call | tf_op jit(solution)/shard_map/attend/pallas_call | solution.py:52
  9.2 0.4 %convolution_convert_fusion = bf16[16,4096]{1,0:T(8,128)(2,1)S(1)} fusion(bf16[16,256]{1,0:T(8,128)(2,1)S(1)} %attend.1, bf16[256,4096]{1,0:T(8,128)(2,1)S(1)} %copy-done), kind=kOutput, calls=%fused_computation | convolution fusion | flops 33619968 | bytes 2236416 | tf_op jit(solution)/shard_map/dot_general | solution.py:284
  9.6 1.6 %collective-permute-start.3 = (bf16[16,4224]{1,0:T(8,128)(2,1)S(1)}, bf16[16,4224]{1,0:T(8,128)(2,1)S(1)}, u32[]{:S(2)}, u32[]{:S(2)}) collective-permute-start(bf16[16,4224]{1,0:T(8,128)(2,1)S(1)} %pad_maximum_fusion), channel_id=1, source_target_pairs={{0,2},{1,5},{2,0},{3,7},{4,6},{5,1},{6,4},{7,3},{8,10},{9,13},{10,... | collective-permute-start | bytes 405512 | tf_op jit(solution)/shard_map/ppermute | solution.py:31
  11.2 3.5 %collective-permute-done.3 = bf16[16,4224]{1,0:T(8,128)(2,1)S(1)} collective-permute-done((bf16[16,4224]{1,0:T(8,128)(2,1)S(1)}, bf16[16,4224]{1,0:T(8,128)(2,1)S(1)}, u32[]{:S(2)}, u32[]{:S(2)}) %collective-permute-start.3) | collective-permute-done | bytes 135200 | tf_op jit(solution)/shard_map/ppermute | solution.py:31
  14.7 0.0 copy-start.1
  14.7 1.6 %collective-permute-start.4 = (bf16[16,4224]{1,0:T(8,128)(2,1)S(1)}, bf16[16,4224]{1,0:T(8,128)(2,1)S(1)}, u32[]{:S(2)}, u32[]{:S(2)}) collective-permute-start(bf16[16,4224]{1,0:T(8,128)(2,1)S(1)} %add_convert_fusion.mine_ref), channel_id=1, source_target_pairs={{0,4},{1,3},{2,6},{3,1},{4,0},{5,7},{6,2},{7,5},{8,12},{9,11},{10,... | collective-permute-start | bytes 405512 | tf_op jit(solution)/shard_map/ppermute | solution.py:31
  16.3 2.4 %load_mine.1 = (bf16[192,4096]{1,0:T(8,128)(2,1)S(1)}, bf16[192,4096]{1,0:T(8,128)(2,1)S(1)}, bf16[192,4096]{1,0:T(8,128)(2,1)S(1)}) custom-call(bf16[192,4096]{1,0:T(8,128)(2,1)} %bitcast.13, bf16[192,4096]{1,0:T(8,128)(2,1)} %bitcast.15, bf16[192,4096]{1,0:T(8,128)(2,1)} %bitcast.17), custom_call_target="tpu_custom_call" | custom-call | bytes 4718592 | tf_op jit(solution)/shard_map/load_mine/pallas_call | solution.py:52
  18.7 1.1 %collective-permute-done.4.other_ref = bf16[16,4224]{1,0:T(8,128)(2,1)S(1)} collective-permute-done((bf16[16,4224]{1,0:T(8,128)(2,1)S(1)}, bf16[16,4224]{1,0:T(8,128)(2,1)S(1)}, u32[]{:S(2)}, u32[]{:S(2)}) %collective-permute-start.4) | collective-permute-done | bytes 135200 | tf_op jit(solution)/shard_map/ppermute | solution.py:31
  19.8 1.5 %first.1 = (f32[4,4096]{1,0:T(4,128)S(1)}, bf16[8,4096]{1,0:T(8,128)(2,1)S(1)}, f32[8,4096]{1,0:T(8,128)S(1)}) custom-call(bf16[16,4224]{1,0:T(8,128)(2,1)S(1)} %add_convert_fusion.mine_ref, bf16[16,4224]{1,0:T(8,128)(2,1)S(1)} %collective-permute-done.4.other_ref, f32[1,4096]{1,0:T(1,128)S(1)} %bitcast.11, ...), custom_call_target="tpu_custom_call" | custom-call | flops 37748736 | bytes 4718592 | tf_op jit(solution)/shard_map/first/pallas_call | solution.py:52
  21.3 0.0 collective-permute-done.5.gate_ref
  21.3 0.0 collective-permute-done.6.up_ref
  21.3 0.0 collective-permute-done.7.down_ref
  21.3 1.2 %second.1 = (bf16[2,4096]{1,0:T(2,128)(2,1)S(1)}, bf16[2,4096]{1,0:T(2,128)(2,1)S(1)}, bf16[2,4096]{1,0:T(2,128)(2,1)S(1)}, bf16[2,4096]{1,0:T(2,128)(2,1)S(1)}) custom-call(bf16[8,4096]{1,0:T(8,128)(2,1)S(1)} %get-tuple-element.44.x_ref, f32[8,4096]{1,0:T(8,128)S(1)} %get-tuple-element.45.part_ref, bf16[192,4096]{1,0:T(8,128)(2,1)S(1)} %collective-permute-done.5.gate_ref, ...), custom_call_target="tpu_custom_call" | custom-call | flops 37748736 | bytes 4718592 | tf_op jit(solution)/shard_map/second/pallas_call | solution.py:52
  22.6 2.5 %collective-permute-start.8 = (bf16[2,4096]{1,0:T(2,128)(2,1)S(1)}, bf16[2,4096]{1,0:T(2,128)(2,1)S(1)}, u32[]{:S(2)}, u32[]{:S(2)}) collective-permute-start(bf16[2,4096]{1,0:T(2,128)(2,1)S(1)} %get-tuple-element.50), channel_id=1, source_target_pairs={{0,6},{1,7},{2,4},{3,5},{4,2},{5,3},{6,0},{7,1},{8,14},{9,15},{10,... | collective-permute-start | bytes 49160 | tf_op jit(solution)/shard_map/ppermute | solution.py:31
  25.1 0.5 %collective-permute-start.9 = (bf16[2,4096]{1,0:T(2,128)(2,1)S(1)}, bf16[2,4096]{1,0:T(2,128)(2,1)S(1)}, u32[]{:S(2)}, u32[]{:S(2)}) collective-permute-start(bf16[2,4096]{1,0:T(2,128)(2,1)S(1)} %get-tuple-element.51), channel_id=1, source_target_pairs={{0,2},{1,5},{2,0},{3,7},{4,6},{5,1},{6,4},{7,3},{8,10},{9,13},{10,... | collective-permute-start | bytes 49160 | tf_op jit(solution)/shard_map/ppermute | solution.py:31
  25.6 0.5 %collective-permute-start.10 = (bf16[2,4096]{1,0:T(2,128)(2,1)S(1)}, bf16[2,4096]{1,0:T(2,128)(2,1)S(1)}, u32[]{:S(2)}, u32[]{:S(2)}) collective-permute-start(bf16[2,4096]{1,0:T(2,128)(2,1)S(1)} %get-tuple-element.52), channel_id=1, source_target_pairs={{0,4},{1,3},{2,6},{3,1},{4,0},{5,7},{6,2},{7,5},{8,12},{9,11},{10,... | collective-permute-start | bytes 49160 | tf_op jit(solution)/shard_map/ppermute | solution.py:31
  26.1 1.2 %collective-permute-done.8.refs_1_ = bf16[2,4096]{1,0:T(2,128)(2,1)S(1)} collective-permute-done((bf16[2,4096]{1,0:T(2,128)(2,1)S(1)}, bf16[2,4096]{1,0:T(2,128)(2,1)S(1)}, u32[]{:S(2)}, u32[]{:S(2)}) %collective-permute-start.8) | collective-permute-done | bytes 16416 | tf_op jit(solution)/shard_map/ppermute | solution.py:31
  27.3 1.5 %collective-permute-done.9.refs_2_ = bf16[2,4096]{1,0:T(2,128)(2,1)S(1)} collective-permute-done((bf16[2,4096]{1,0:T(2,128)(2,1)S(1)}, bf16[2,4096]{1,0:T(2,128)(2,1)S(1)}, u32[]{:S(2)}, u32[]{:S(2)}) %collective-permute-start.9) | collective-permute-done | bytes 16416 | tf_op jit(solution)/shard_map/ppermute | solution.py:31
  28.8 0.5 %collective-permute-done.10.refs_3_ = bf16[2,4096]{1,0:T(2,128)(2,1)S(1)} collective-permute-done((bf16[2,4096]{1,0:T(2,128)(2,1)S(1)}, bf16[2,4096]{1,0:T(2,128)(2,1)S(1)}, u32[]{:S(2)}, u32[]{:S(2)}) %collective-permute-start.10) | collective-permute-done | bytes 16416 | tf_op jit(solution)/shard_map/ppermute | solution.py:31
  29.3 0.8 %combine.1 = bf16[4,4096]{1,0:T(4,128)(2,1)} custom-call(f32[4,128]{1,0:T(4,128)S(1)} %get-tuple-element.32.mix_ref, f32[4,4096]{1,0:T(4,128)S(1)} %get-tuple-element.43.own_ref, bf16[2,4096]{1,0:T(2,128)(2,1)S(1)} %get-tuple-element.49.refs_0_, bf16[2,4096]{1,0:T(2,128)(2,1)S(1)} %collective-permute-done.8.refs_1_, ...), custom_call_target="tpu_custom_call" | custom-call | tf_op jit(solution)/shard_map/combine/pallas_call | solution.py:52
  (4 shorter events, 0.1 us)
Async XLA Ops:
  0.0 9.2 %copy-start = (bf16[256,4096]{1,0:T(8,128)(2,1)S(1)}, bf16[256,4096]{1,0:T(8,128)(2,1)}, u32[]{:S(2)}) copy-start(bf16[256,4096]{1,0:T(8,128)(2,1)} %param.13) | copy-start | bytes 6291460
  1.0 5.7 %collective-permute-start = (bf16[64,128]{1,0:T(8,128)(2,1)S(1)}, bf16[64,128]{1,0:T(8,128)(2,1)S(1)}, u32[]{:S(2)}, u32[]{:S(2)}) collective-permute-start(bf16[64,128]{1,0:T(8,128)(2,1)S(1)} %open.1.refs_0_), channel_id=1, source_target_pairs={{0,8},{1,25},{8,0},{9,17},{16,24},{17,9},{24,16},{25,1},{2,10},{3,... | collective-permute-start | bytes 49160 | tf_op jit(solution)/shard_map/ppermute | solution.py:31
  4.1 4.7 %collective-permute-start.2 = (bf16[64,128]{1,0:T(8,128)(2,1)S(1)}, bf16[64,128]{1,0:T(8,128)(2,1)S(1)}, u32[]{:S(2)}, u32[]{:S(2)}) collective-permute-start(bf16[64,128]{1,0:T(8,128)(2,1)S(1)} %open.1.refs_0_), channel_id=1, source_target_pairs={{0,16},{8,24},{16,0},{24,8},{1,17},{9,25},{17,1},{25,9},{2,18},{10... | collective-permute-start | bytes 49160 | tf_op jit(solution)/shard_map/ppermute | solution.py:21
  6.7 2.1 %collective-permute-start.1 = (bf16[64,128]{1,0:T(8,128)(2,1)S(1)}, bf16[64,128]{1,0:T(8,128)(2,1)S(1)}, u32[]{:S(2)}, u32[]{:S(2)}) collective-permute-start(bf16[64,128]{1,0:T(8,128)(2,1)S(1)} %collective-permute-done.refs_1_), channel_id=1, source_target_pairs={{0,1},{1,0},{2,3},{3,2},{4,5},{5,4},{6,7},{7,6},{8,9},{9,8},{10,11... | collective-permute-start | bytes 49160 | tf_op jit(solution)/shard_map/ppermute | solution.py:21
  6.8 14.5 %collective-permute-start.5 = (bf16[192,4096]{1,0:T(8,128)(2,1)}, bf16[192,4096]{1,0:T(8,128)(2,1)S(1)}, u32[]{:S(2)}, u32[]{:S(2)}) collective-permute-start(bf16[192,4096]{1,0:T(8,128)(2,1)} %bitcast.12), channel_id=1, source_target_pairs={{0,1},{1,0},{2,3},{3,2},{4,5},{5,4},{6,7},{7,6},{8,9},{9,8},{10,11... | collective-permute-start | bytes 4718600 | tf_op jit(solution)/shard_map/ppermute | solution.py:21
  7.2 14.1 %collective-permute-start.6 = (bf16[192,4096]{1,0:T(8,128)(2,1)}, bf16[192,4096]{1,0:T(8,128)(2,1)S(1)}, u32[]{:S(2)}, u32[]{:S(2)}) collective-permute-start(bf16[192,4096]{1,0:T(8,128)(2,1)} %bitcast.14), channel_id=1, source_target_pairs={{0,1},{1,0},{2,3},{3,2},{4,5},{5,4},{6,7},{7,6},{8,9},{9,8},{10,11... | collective-permute-start | bytes 4718600 | tf_op jit(solution)/shard_map/ppermute | solution.py:21
  7.4 14.0 %collective-permute-start.7 = (bf16[192,4096]{1,0:T(8,128)(2,1)}, bf16[192,4096]{1,0:T(8,128)(2,1)S(1)}, u32[]{:S(2)}, u32[]{:S(2)}) collective-permute-start(bf16[192,4096]{1,0:T(8,128)(2,1)} %bitcast.16), channel_id=1, source_target_pairs={{0,1},{1,0},{2,3},{3,2},{4,5},{5,4},{6,7},{7,6},{8,9},{9,8},{10,11... | collective-permute-start | bytes 4718600 | tf_op jit(solution)/shard_map/ppermute | solution.py:21
  9.6 5.1 %collective-permute-start.3 = (bf16[16,4224]{1,0:T(8,128)(2,1)S(1)}, bf16[16,4224]{1,0:T(8,128)(2,1)S(1)}, u32[]{:S(2)}, u32[]{:S(2)}) collective-permute-start(bf16[16,4224]{1,0:T(8,128)(2,1)S(1)} %pad_maximum_fusion), channel_id=1, source_target_pairs={{0,2},{1,5},{2,0},{3,7},{4,6},{5,1},{6,4},{7,3},{8,10},{9,13},{10,... | collective-permute-start | bytes 405512 | tf_op jit(solution)/shard_map/ppermute | solution.py:31
  14.7 5.1 %copy-start.1 = (f32[4096]{0:T(1024)S(1)}, f32[4096]{0:T(1024)}, u32[]{:S(2)}) copy-start(f32[4096]{0:T(1024)} %param.14) | copy-start | bytes 49156
  14.7 5.1 %collective-permute-start.4 = (bf16[16,4224]{1,0:T(8,128)(2,1)S(1)}, bf16[16,4224]{1,0:T(8,128)(2,1)S(1)}, u32[]{:S(2)}, u32[]{:S(2)}) collective-permute-start(bf16[16,4224]{1,0:T(8,128)(2,1)S(1)} %add_convert_fusion.mine_ref), channel_id=1, source_target_pairs={{0,4},{1,3},{2,6},{3,1},{4,0},{5,7},{6,2},{7,5},{8,12},{9,11},{10,... | collective-permute-start | bytes 405512 | tf_op jit(solution)/shard_map/ppermute | solution.py:31
  22.6 4.7 %collective-permute-start.8 = (bf16[2,4096]{1,0:T(2,128)(2,1)S(1)}, bf16[2,4096]{1,0:T(2,128)(2,1)S(1)}, u32[]{:S(2)}, u32[]{:S(2)}) collective-permute-start(bf16[2,4096]{1,0:T(2,128)(2,1)S(1)} %get-tuple-element.50), channel_id=1, source_target_pairs={{0,6},{1,7},{2,4},{3,5},{4,2},{5,3},{6,0},{7,1},{8,14},{9,15},{10,... | collective-permute-start | bytes 49160 | tf_op jit(solution)/shard_map/ppermute | solution.py:31
  25.1 3.7 %collective-permute-start.9 = (bf16[2,4096]{1,0:T(2,128)(2,1)S(1)}, bf16[2,4096]{1,0:T(2,128)(2,1)S(1)}, u32[]{:S(2)}, u32[]{:S(2)}) collective-permute-start(bf16[2,4096]{1,0:T(2,128)(2,1)S(1)} %get-tuple-element.51), channel_id=1, source_target_pairs={{0,2},{1,5},{2,0},{3,7},{4,6},{5,1},{6,4},{7,3},{8,10},{9,13},{10,... | collective-permute-start | bytes 49160 | tf_op jit(solution)/shard_map/ppermute | solution.py:31
  25.6 3.7 %collective-permute-start.10 = (bf16[2,4096]{1,0:T(2,128)(2,1)S(1)}, bf16[2,4096]{1,0:T(2,128)(2,1)S(1)}, u32[]{:S(2)}, u32[]{:S(2)}) collective-permute-start(bf16[2,4096]{1,0:T(2,128)(2,1)S(1)} %get-tuple-element.52), channel_id=1, source_target_pairs={{0,4},{1,3},{2,6},{3,1},{4,0},{5,7},{6,2},{7,5},{8,12},{9,11},{10,... | collective-permute-start | bytes 49160 | tf_op jit(solution)/shard_map/ppermute | solution.py:31

commit v5 on v4

--- a/solution.py
+++ b/solution.py
@@ -29,6 +29,13 @@
         for t in range(cores)
     ]
     return lax.ppermute(x, (axis, "tp"), pairs)
+
+
+def by_distance(size):
+    bits = size.bit_length() - 1
+    mirror = [sum((m >> i & 1) << (bits - 1 - i) for i in range(bits)) for m in range(size)]
+    far_first = sorted(range(1, size), key=lambda m: -m.bit_count())
+    return [(0, 0)] + [(m, mirror[m]) for m in far_first]
 
 
 def gather_ctx(x):
@@ -142,38 +149,34 @@
         out_ref[:, h * head_dim : (h + 1) * head_dim] = mixed[h * count : (h + 1) * count]
 
 
-def load_kernel(*refs):
-    n = len(refs) // 2
-    copies = [pltpu.make_async_copy(refs[i], refs[n + i], refs[-1].at[i]) for i in range(n)]
+def turn(gate_ref, up_ref, out_ref):
+    units, width = gate_ref.shape
+    for at in range(0, width, LANES):
+        both = jnp.concatenate([gate_ref[:, at : at + LANES], up_ref[:, at : at + LANES]], axis=0)
+        out_ref[at : at + LANES, :] = both.T
+
+
+def load_kernel(gate_hbm, up_hbm, down_hbm, wide_ref, down_ref, gate_ref, up_ref, sems):
+    ends = ((gate_hbm, gate_ref), (up_hbm, up_ref), (down_hbm, down_ref))
+    copies = [pltpu.make_async_copy(i, o, sems.at[n]) for n, (i, o) in enumerate(ends)]
     for copy in copies:
         copy.start()
-    for copy in copies:
-        copy.wait()
-
-
-def load(weights, name):
-    return call(
-        load_kernel,
-        [(w.shape, w.dtype) for w in weights],
-        *far(weights),
-        where=pltpu.HBM,
-        scratch=[pltpu.SemaphoreType.DMA((len(weights),))],
-        read=2 * sum(w.size for w in weights),
-        name=name,
-    )
-
-
-def hidden_units(x, gate_ref, up_ref, down_ref):
-    last = (((1,), (1,)), ((), ()))
-    gate = lax.dot_general(x, gate_ref[...], last, preferred_element_type=jnp.float32)
-    up = lax.dot_general(x, up_ref[...], last, preferred_element_type=jnp.float32)
-    hidden = silu_mul(gate, up).astype(jnp.bfloat16)
+    copies[0].wait()
+    copies[1].wait()
+    turn(gate_ref, up_ref, wide_ref)
+    copies[2].wait()
+
+
+def hidden_units(x, wide_ref, down_ref):
+    units = down_ref.shape[0]
+    both = jnp.dot(x, wide_ref[...], preferred_element_type=jnp.float32)
+    hidden = silu_mul(both[:, :units], both[:, units:]).astype(jnp.bfloat16)
     return jnp.dot(hidden, down_ref[...], preferred_element_type=jnp.float32)
 
 
-def first_kernel(blocks, live, masks, mine_ref, other_ref, gain_ref, gate_ref, up_ref, down_ref, *outs):
-    own_ref, x_ref, part_ref = outs
-    count, width = mine_ref.shape[0], x_ref.shape[1]
+def experts_kernel(blocks, live, masks, mine_ref, other_ref, gain_ref, *refs):
+    weights, own_ref, outs = refs[:4], refs[4], refs[5:]
+    count, width = mine_ref.shape[0], own_ref.shape[1]
     rows = count // blocks
     mine = lax.axis_index("exp")
     summed = (mine_ref[:, :width].astype(jnp.float32) + other_ref[:, :width].astype(jnp.float32)).astype(
@@ -212,12 +215,7 @@
     same = mask == (lax.broadcasted_iota(jnp.int32, shape, 1) // rows) ^ mine
     pick = jnp.where(same, pick, 0.0).astype(jnp.bfloat16)
     x = jnp.dot(pick, normed, preferred_element_type=jnp.float32).astype(jnp.bfloat16)
-    x_ref[...] = x
-    part_ref[...] = hidden_units(x, gate_ref, up_ref, down_ref)
-
-
-def second_kernel(x_ref, part_ref, gate_ref, up_ref, down_ref, *outs):
-    result = part_ref[...] + hidden_units(x_ref[...], gate_ref, up_ref, down_ref)
+    result = hidden_units(x, *weights[:2]) + hidden_units(x, *weights[2:])
     for m, out_ref in enumerate(outs):
         out_ref[...] = result[m * CAP : (m + 1) * CAP].astype(out_ref.dtype)
 
@@ -283,39 +281,42 @@
     )
     term = jnp.dot(mixed, out_weight, preferred_element_type=jnp.float32).astype(jnp.bfloat16)
     summed = jnp.concatenate([term, note], axis=1)
+    units = w_down.shape[1]
     summed, *weights = lax.optimization_barrier((summed, *weights))
-    weights = load(weights, "load_mine")
+    weights = call(
+        load_kernel,
+        [((width, 2 * units), w_down.dtype), ((units, width), w_down.dtype)],
+        *far(weights),
+        where=pltpu.HBM,
+        scratch=[pltpu.VMEM((units, width), w_down.dtype)] * 2 + [pltpu.SemaphoreType.DMA((3,))],
+        read=6 * w_down.size,
+        name="load",
+    )
     steps = [1 << i for i in range(n_exp.bit_length() - 1)]
     for i, step in enumerate(steps):
         other = swap_by_core(summed, "exp", (step, steps[-1 - i]))
         if i < len(steps) - 1:
             summed = (summed.astype(jnp.float32) + other.astype(jnp.float32)).astype(jnp.bfloat16)
-    masks = [(0, 0), (3, 3), (1, 2), (2, 1)]
+            if i == 0:
+                summed, *tied = lax.optimization_barrier((summed, *weights, *moved[:2]))
+                weights, moved[:2] = tied[:2], tied[2:]
+    (wide,) = call(
+        turn, [((width, 2 * units), w_down.dtype)], *moved[:2], read=4 * w_down.size, name="turn"
+    )
+    masks = by_distance(n_exp)
     slots = blocks * CAP
-    own, x, part = call(
-        functools.partial(first_kernel, blocks, live, masks),
-        [
-            ((rows, width), jnp.float32),
-            ((slots, width), jnp.bfloat16),
-            ((slots, width), jnp.float32),
-        ],
+    own, *results = call(
+        functools.partial(experts_kernel, blocks, live, masks),
+        [((rows, width), jnp.float32)] + [((CAP, width), jnp.bfloat16)] * n_exp,
         summed,
         other,
         norm_gain.reshape(1, width),
         *weights,
-        flops=6 * slots * w_down.size,
-        read=6 * w_down.size,
-        name="first",
-    )
-    results = call(
-        second_kernel,
-        [((CAP, width), jnp.bfloat16)] * n_exp,
-        x,
-        part,
-        *moved,
-        flops=6 * slots * w_down.size,
-        read=6 * w_down.size,
-        name="second",
+        wide,
+        moved[2],
+        flops=12 * slots * w_down.size,
+        read=12 * w_down.size,
+        name="experts",
     )
     back = [
         results[0] if even == 0 else swap_by_core(results[i], "exp", (even, odd))

time: 30.4 us -> 29.4 us (0.967)
  waiting for transfers between devices: 8.12 us -> 6.81 us
  Pallas kernels: 8.13 us -> 8.45 us
    ppermute x6, waiting for transfers between devices: 7.86 us -> 6.56 us  [swap_by_core(): return lax.ppermute(x, (axis, 'tp'), pairs)]
    pallas_call x7, Pallas kernels: 8.13 us -> 8.45 us  [call(): pl.pallas_call(kernel, out_shape=[kept(shape, dtype) for shape, dtype in...]
  transfers between devices with their start and end apart: 11 -> 11, of which waited for: 6 -> 6; matrix products, arithmetic and copies ran while one was open for 1% -> 2% of each run, Pallas kernels for 17% -> 17%
where the time goes in v5:
time: 29.4 us; the launch traced here: 29.2 us
  starting transfers between devices  13.4 us (46%)
  Pallas kernels  8.45 us (29%)
  waiting for transfers between devices  6.81 us (23%)
  matrix products  0.4 us (1%)
    ppermute x6, starting transfers between devices, swap_by_core(): return lax.ppermute(x, (axis, 'tp'), pairs)  9.77 us
    pallas_call x7, Pallas kernels, call(): pl.pallas_call(kernel, out_shape=[kept(shape, dtype) for shape, dtype in...  8.45 us
    ppermute x6, waiting for transfers between devices, swap_by_core(): return lax.ppermute(x, (axis, 'tp'), pairs)  6.56 us
    ppermute x5, starting transfers between devices, swap(): return lax.ppermute(x, axis, [(i, i ^ mask) for i in range(size)])  3.61 us
  transfers between devices with their start and end apart: 11, of which 6 were waited for; matrix products, arithmetic and copies ran while one was open for 2% of the time, Pallas kernels for 17%

profile of v5, /device:TPU:0, one launch (start us, length us, event | category | flops | bytes accessed | tf_op | source)
XLA Modules:
  0.0 29.2 jit_solution(17222674048975044424)
XLA Ops:
  0.0 0.0 copy-start
  0.0 1.0 %open.1.refs_0_ = bf16[64,128]{1,0:T(8,128)(2,1)S(1)} custom-call(bf16[32,4,128]{2,1,0:T(4,128)(2,1)} %key_hbm.1, bf16[32,4,128]{2,1,0:T(4,128)(2,1)} %value_hbm.1), custom_call_target="tpu_custom_call" | custom-call | tf_op jit(solution)/shard_map/open/pallas_call | solution.py:59
  1.0 3.1 %collective-permute-start = (bf16[64,128]{1,0:T(8,128)(2,1)S(1)}, bf16[64,128]{1,0:T(8,128)(2,1)S(1)}, u32[]{:S(2)}, u32[]{:S(2)}) collective-permute-start(bf16[64,128]{1,0:T(8,128)(2,1)S(1)} %open.1.refs_0_), channel_id=1, source_target_pairs={{0,8},{1,25},{8,0},{9,17},{16,24},{17,9},{24,16},{25,1},{2,10},{3,... | collective-permute-start | bytes 49160 | tf_op jit(solution)/shard_map/ppermute | solution.py:31
  4.1 2.6 %collective-permute-start.2 = (bf16[64,128]{1,0:T(8,128)(2,1)S(1)}, bf16[64,128]{1,0:T(8,128)(2,1)S(1)}, u32[]{:S(2)}, u32[]{:S(2)}) collective-permute-start(bf16[64,128]{1,0:T(8,128)(2,1)S(1)} %open.1.refs_0_), channel_id=1, source_target_pairs={{0,16},{8,24},{16,0},{24,8},{1,17},{9,25},{17,1},{25,9},{2,18},{10... | collective-permute-start | bytes 49160 | tf_op jit(solution)/shard_map/ppermute | solution.py:21
  6.7 0.0 collective-permute-done.refs_1_
  6.7 0.1 collective-permute-start.1
  6.8 0.4 %collective-permute-start.4 = (bf16[192,4096]{1,0:T(8,128)(2,1)}, bf16[192,4096]{1,0:T(8,128)(2,1)S(1)}, u32[]{:S(2)}, u32[]{:S(2)}) collective-permute-start(bf16[192,4096]{1,0:T(8,128)(2,1)} %bitcast.12), channel_id=1, source_target_pairs={{0,1},{1,0},{2,3},{3,2},{4,5},{5,4},{6,7},{7,6},{8,9},{9,8},{10,11... | collective-permute-start | bytes 4718600 | tf_op jit(solution)/shard_map/ppermute | solution.py:21
  7.2 0.1 collective-permute-start.5
  7.4 0.4 %collective-permute-start.7 = (bf16[192,4096]{1,0:T(8,128)(2,1)}, bf16[192,4096]{1,0:T(8,128)(2,1)S(1)}, u32[]{:S(2)}, u32[]{:S(2)}) collective-permute-start(bf16[192,4096]{1,0:T(8,128)(2,1)} %bitcast.16), channel_id=1, source_target_pairs={{0,1},{1,0},{2,3},{3,2},{4,5},{5,4},{6,7},{7,6},{8,9},{9,8},{10,11... | collective-permute-start | bytes 4718600 | tf_op jit(solution)/shard_map/ppermute | solution.py:21
  7.8 0.8 %route.1 = (bf16[32,128]{1,0:T(8,128)(2,1)S(1)}, bf16[16,128]{1,0:T(8,128)(2,1)S(1)}, f32[4,128]{1,0:T(4,128)S(1)}) custom-call(bf16[16,2,128]{2,1,0:T(2,128)(2,1)} %bitcast.18, s32[4,8]{1,0:T(4,128)} %refs_1_, f32[4,8]{1,0:T(4,128)} %refs_2_), custom_call_target="tpu_custom_call" | custom-call | tf_op jit(solution)/shard_map/route/pallas_call | solution.py:59
  8.6 0.2 collective-permute-done.2.refs_3_
  8.9 0.0 collective-permute-done.1.refs_2_
  8.9 0.3 %attend.1 = bf16[16,256]{1,0:T(8,128)(2,1)S(1)} custom-call(bf16[32,128]{1,0:T(8,128)(2,1)S(1)} %get-tuple-element.35.q_ref, bf16[64,128]{1,0:T(8,128)(2,1)S(1)} %open.1.refs_0_, bf16[64,128]{1,0:T(8,128)(2,1)S(1)} %collective-permute-done.refs_1_, bf16[64,128]{1,0:T(8,128)(2,1)S(1)} %collective-permute-done.1.refs_2_, ...), custom_call_target="tpu_custom_call" | custom-call | tf_op jit(solution)/shard_map/attend/pallas_call | solution.py:59
  9.2 0.4 %convolution_convert_fusion = bf16[16,4096]{1,0:T(8,128)(2,1)S(1)} fusion(bf16[16,256]{1,0:T(8,128)(2,1)S(1)} %attend.1, bf16[256,4096]{1,0:T(8,128)(2,1)S(1)} %copy-done), kind=kOutput, calls=%fused_computation | convolution fusion | flops 33619968 | bytes 2236416 | tf_op jit(solution)/shard_map/dot_general | solution.py:282
  9.6 1.6 %collective-permute-start.3 = (bf16[16,4224]{1,0:T(8,128)(2,1)S(1)}, bf16[16,4224]{1,0:T(8,128)(2,1)S(1)}, u32[]{:S(2)}, u32[]{:S(2)}) collective-permute-start(bf16[16,4224]{1,0:T(8,128)(2,1)S(1)} %pad_maximum_fusion), channel_id=1, source_target_pairs={{0,2},{1,5},{2,0},{3,7},{4,6},{5,1},{6,4},{7,3},{8,10},{9,13},{10,... | collective-permute-start | bytes 405512 | tf_op jit(solution)/shard_map/ppermute | solution.py:31
  11.2 2.8 %load.1 = (bf16[4096,384]{1,0:T(8,128)(2,1)S(1)}, bf16[192,4096]{1,0:T(8,128)(2,1)S(1)}) custom-call(bf16[192,4096]{1,0:T(8,128)(2,1)} %bitcast.13, bf16[192,4096]{1,0:T(8,128)(2,1)} %bitcast.15, bf16[192,4096]{1,0:T(8,128)(2,1)} %bitcast.17), custom_call_target="tpu_custom_call" | custom-call | bytes 4718592 | tf_op jit(solution)/shard_map/load/pallas_call | solution.py:59
  14.0 0.7 %collective-permute-done.3 = bf16[16,4224]{1,0:T(8,128)(2,1)S(1)} collective-permute-done((bf16[16,4224]{1,0:T(8,128)(2,1)S(1)}, bf16[16,4224]{1,0:T(8,128)(2,1)S(1)}, u32[]{:S(2)}, u32[]{:S(2)}) %collective-permute-start.3) | collective-permute-done | bytes 135200 | tf_op jit(solution)/shard_map/ppermute | solution.py:31
  14.7 0.0 collective-permute-done.4.gate_ref
  14.7 0.0 collective-permute-done.5.up_ref
  14.8 0.0 copy-start.1
  14.8 1.6 %collective-permute-start.6 = (bf16[16,4224]{1,0:T(8,128)(2,1)S(1)}, bf16[16,4224]{1,0:T(8,128)(2,1)S(1)}, u32[]{:S(2)}, u32[]{:S(2)}) collective-permute-start(bf16[16,4224]{1,0:T(8,128)(2,1)S(1)} %add_convert_fusion.mine_ref), channel_id=1, source_target_pairs={{0,4},{1,3},{2,6},{3,1},{4,0},{5,7},{6,2},{7,5},{8,12},{9,11},{10,... | collective-permute-start | bytes 405512 | tf_op jit(solution)/shard_map/ppermute | solution.py:31
  16.4 0.9 %turn.1.refs_2_ = bf16[4096,384]{1,0:T(8,128)(2,1)S(1)} custom-call(bf16[192,4096]{1,0:T(8,128)(2,1)S(1)} %collective-permute-done.4.gate_ref, bf16[192,4096]{1,0:T(8,128)(2,1)S(1)} %collective-permute-done.5.up_ref), custom_call_target="tpu_custom_call" | custom-call | bytes 3145728 | tf_op jit(solution)/shard_map/turn/pallas_call | solution.py:59
  17.2 0.0 collective-permute-done.7.refs_3_
  17.2 2.6 %collective-permute-done.6.other_ref = bf16[16,4224]{1,0:T(8,128)(2,1)S(1)} collective-permute-done((bf16[16,4224]{1,0:T(8,128)(2,1)S(1)}, bf16[16,4224]{1,0:T(8,128)(2,1)S(1)}, u32[]{:S(2)}, u32[]{:S(2)}) %collective-permute-start.6) | collective-permute-done | bytes 135200 | tf_op jit(solution)/shard_map/ppermute | solution.py:31
  19.8 1.8 %experts.1 = (f32[4,4096]{1,0:T(4,128)S(1)}, bf16[2,4096]{1,0:T(2,128)(2,1)S(1)}, bf16[2,4096]{1,0:T(2,128)(2,1)S(1)}, bf16[2,4096]{1,0:T(2,128)(2,1)S(1)}, bf16[2,4096]{1,0:T(2,128)(2,1)S(1)}) custom-call(bf16[16,4224]{1,0:T(8,128)(2,1)S(1)} %add_convert_fusion.mine_ref, bf16[16,4224]{1,0:T(8,128)(2,1)S(1)} %collective-permute-done.6.other_ref, ...), custom_call_target="tpu_custom_call" | custom-call | flops 75497472 | bytes 9437184 | tf_op jit(solution)/shard_map/experts/pallas_call | solution.py:59
  21.6 1.6 %collective-permute-start.10 = (bf16[2,4096]{1,0:T(2,128)(2,1)S(1)}, bf16[2,4096]{1,0:T(2,128)(2,1)S(1)}, u32[]{:S(2)}, u32[]{:S(2)}) collective-permute-start(bf16[2,4096]{1,0:T(2,128)(2,1)S(1)} %get-tuple-element.56), channel_id=1, source_target_pairs={{0,4},{1,3},{2,6},{3,1},{4,0},{5,7},{6,2},{7,5},{8,12},{9,11},{10,... | collective-permute-start | bytes 49160 | tf_op jit(solution)/shard_map/ppermute | solution.py:31
  23.2 1.4 %collective-permute-start.8 = (bf16[2,4096]{1,0:T(2,128)(2,1)S(1)}, bf16[2,4096]{1,0:T(2,128)(2,1)S(1)}, u32[]{:S(2)}, u32[]{:S(2)}) collective-permute-start(bf16[2,4096]{1,0:T(2,128)(2,1)S(1)} %get-tuple-element.54), channel_id=1, source_target_pairs={{0,6},{1,7},{2,4},{3,5},{4,2},{5,3},{6,0},{7,1},{8,14},{9,15},{10,... | collective-permute-start | bytes 49160 | tf_op jit(solution)/shard_map/ppermute | solution.py:31
  24.6 0.5 %collective-permute-start.9 = (bf16[2,4096]{1,0:T(2,128)(2,1)S(1)}, bf16[2,4096]{1,0:T(2,128)(2,1)S(1)}, u32[]{:S(2)}, u32[]{:S(2)}) collective-permute-start(bf16[2,4096]{1,0:T(2,128)(2,1)S(1)} %get-tuple-element.55), channel_id=1, source_target_pairs={{0,2},{1,5},{2,0},{3,7},{4,6},{5,1},{6,4},{7,3},{8,10},{9,13},{10,... | collective-permute-start | bytes 49160 | tf_op jit(solution)/shard_map/ppermute | solution.py:31
  25.2 0.2 collective-permute-done.10.refs_3_
  25.4 2.4 %collective-permute-done.8.refs_1_ = bf16[2,4096]{1,0:T(2,128)(2,1)S(1)} collective-permute-done((bf16[2,4096]{1,0:T(2,128)(2,1)S(1)}, bf16[2,4096]{1,0:T(2,128)(2,1)S(1)}, u32[]{:S(2)}, u32[]{:S(2)}) %collective-permute-start.8) | collective-permute-done | bytes 16416 | tf_op jit(solution)/shard_map/ppermute | solution.py:31
  27.9 0.5 %collective-permute-done.9.refs_2_ = bf16[2,4096]{1,0:T(2,128)(2,1)S(1)} collective-permute-done((bf16[2,4096]{1,0:T(2,128)(2,1)S(1)}, bf16[2,4096]{1,0:T(2,128)(2,1)S(1)}, u32[]{:S(2)}, u32[]{:S(2)}) %collective-permute-start.9) | collective-permute-done | bytes 16416 | tf_op jit(solution)/shard_map/ppermute | solution.py:31
  28.4 0.8 %combine.1 = bf16[4,4096]{1,0:T(4,128)(2,1)} custom-call(f32[4,128]{1,0:T(4,128)S(1)} %get-tuple-element.34.mix_ref, f32[4,4096]{1,0:T(4,128)S(1)} %get-tuple-element.52.own_ref, bf16[2,4096]{1,0:T(2,128)(2,1)S(1)} %get-tuple-element.53.refs_0_, bf16[2,4096]{1,0:T(2,128)(2,1)S(1)} %collective-permute-done.8.refs_1_, ...), custom_call_target="tpu_custom_call" | custom-call | tf_op jit(solution)/shard_map/combine/pallas_call | solution.py:59
  (4 shorter events, 0.1 us)
Async XLA Ops:
  0.0 9.2 %copy-start = (bf16[256,4096]{1,0:T(8,128)(2,1)S(1)}, bf16[256,4096]{1,0:T(8,128)(2,1)}, u32[]{:S(2)}) copy-start(bf16[256,4096]{1,0:T(8,128)(2,1)} %param.13) | copy-start | bytes 6291460
  1.0 5.7 %collective-permute-start = (bf16[64,128]{1,0:T(8,128)(2,1)S(1)}, bf16[64,128]{1,0:T(8,128)(2,1)S(1)}, u32[]{:S(2)}, u32[]{:S(2)}) collective-permute-start(bf16[64,128]{1,0:T(8,128)(2,1)S(1)} %open.1.refs_0_), channel_id=1, source_target_pairs={{0,8},{1,25},{8,0},{9,17},{16,24},{17,9},{24,16},{25,1},{2,10},{3,... | collective-permute-start | bytes 49160 | tf_op jit(solution)/shard_map/ppermute | solution.py:31
  4.1 4.7 %collective-permute-start.2 = (bf16[64,128]{1,0:T(8,128)(2,1)S(1)}, bf16[64,128]{1,0:T(8,128)(2,1)S(1)}, u32[]{:S(2)}, u32[]{:S(2)}) collective-permute-start(bf16[64,128]{1,0:T(8,128)(2,1)S(1)} %open.1.refs_0_), channel_id=1, source_target_pairs={{0,16},{8,24},{16,0},{24,8},{1,17},{9,25},{17,1},{25,9},{2,18},{10... | collective-permute-start | bytes 49160 | tf_op jit(solution)/shard_map/ppermute | solution.py:21
  6.7 2.1 %collective-permute-start.1 = (bf16[64,128]{1,0:T(8,128)(2,1)S(1)}, bf16[64,128]{1,0:T(8,128)(2,1)S(1)}, u32[]{:S(2)}, u32[]{:S(2)}) collective-permute-start(bf16[64,128]{1,0:T(8,128)(2,1)S(1)} %collective-permute-done.refs_1_), channel_id=1, source_target_pairs={{0,1},{1,0},{2,3},{3,2},{4,5},{5,4},{6,7},{7,6},{8,9},{9,8},{10,11... | collective-permute-start | bytes 49160 | tf_op jit(solution)/shard_map/ppermute | solution.py:21
  6.8 7.9 %collective-permute-start.4 = (bf16[192,4096]{1,0:T(8,128)(2,1)}, bf16[192,4096]{1,0:T(8,128)(2,1)S(1)}, u32[]{:S(2)}, u32[]{:S(2)}) collective-permute-start(bf16[192,4096]{1,0:T(8,128)(2,1)} %bitcast.12), channel_id=1, source_target_pairs={{0,1},{1,0},{2,3},{3,2},{4,5},{5,4},{6,7},{7,6},{8,9},{9,8},{10,11... | collective-permute-start | bytes 4718600 | tf_op jit(solution)/shard_map/ppermute | solution.py:21
  7.2 7.5 %collective-permute-start.5 = (bf16[192,4096]{1,0:T(8,128)(2,1)}, bf16[192,4096]{1,0:T(8,128)(2,1)S(1)}, u32[]{:S(2)}, u32[]{:S(2)}) collective-permute-start(bf16[192,4096]{1,0:T(8,128)(2,1)} %bitcast.14), channel_id=1, source_target_pairs={{0,1},{1,0},{2,3},{3,2},{4,5},{5,4},{6,7},{7,6},{8,9},{9,8},{10,11... | collective-permute-start | bytes 4718600 | tf_op jit(solution)/shard_map/ppermute | solution.py:21
  7.4 9.9 %collective-permute-start.7 = (bf16[192,4096]{1,0:T(8,128)(2,1)}, bf16[192,4096]{1,0:T(8,128)(2,1)S(1)}, u32[]{:S(2)}, u32[]{:S(2)}) collective-permute-start(bf16[192,4096]{1,0:T(8,128)(2,1)} %bitcast.16), channel_id=1, source_target_pairs={{0,1},{1,0},{2,3},{3,2},{4,5},{5,4},{6,7},{7,6},{8,9},{9,8},{10,11... | collective-permute-start | bytes 4718600 | tf_op jit(solution)/shard_map/ppermute | solution.py:21
  9.6 5.1 %collective-permute-start.3 = (bf16[16,4224]{1,0:T(8,128)(2,1)S(1)}, bf16[16,4224]{1,0:T(8,128)(2,1)S(1)}, u32[]{:S(2)}, u32[]{:S(2)}) collective-permute-start(bf16[16,4224]{1,0:T(8,128)(2,1)S(1)} %pad_maximum_fusion), channel_id=1, source_target_pairs={{0,2},{1,5},{2,0},{3,7},{4,6},{5,1},{6,4},{7,3},{8,10},{9,13},{10,... | collective-permute-start | bytes 405512 | tf_op jit(solution)/shard_map/ppermute | solution.py:31
  14.8 5.1 %copy-start.1 = (f32[4096]{0:T(1024)S(1)}, f32[4096]{0:T(1024)}, u32[]{:S(2)}) copy-start(f32[4096]{0:T(1024)} %param.14) | copy-start | bytes 49156
  14.8 5.1 %collective-permute-start.6 = (bf16[16,4224]{1,0:T(8,128)(2,1)S(1)}, bf16[16,4224]{1,0:T(8,128)(2,1)S(1)}, u32[]{:S(2)}, u32[]{:S(2)}) collective-permute-start(bf16[16,4224]{1,0:T(8,128)(2,1)S(1)} %add_convert_fusion.mine_ref), channel_id=1, source_target_pairs={{0,4},{1,3},{2,6},{3,1},{4,0},{5,7},{6,2},{7,5},{8,12},{9,11},{10,... | collective-permute-start | bytes 405512 | tf_op jit(solution)/shard_map/ppermute | solution.py:31
  21.6 3.8 %collective-permute-start.10 = (bf16[2,4096]{1,0:T(2,128)(2,1)S(1)}, bf16[2,4096]{1,0:T(2,128)(2,1)S(1)}, u32[]{:S(2)}, u32[]{:S(2)}) collective-permute-start(bf16[2,4096]{1,0:T(2,128)(2,1)S(1)} %get-tuple-element.56), channel_id=1, source_target_pairs={{0,4},{1,3},{2,6},{3,1},{4,0},{5,7},{6,2},{7,5},{8,12},{9,11},{10,... | collective-permute-start | bytes 49160 | tf_op jit(solution)/shard_map/ppermute | solution.py:31
  23.2 4.6 %collective-permute-start.8 = (bf16[2,4096]{1,0:T(2,128)(2,1)S(1)}, bf16[2,4096]{1,0:T(2,128)(2,1)S(1)}, u32[]{:S(2)}, u32[]{:S(2)}) collective-permute-start(bf16[2,4096]{1,0:T(2,128)(2,1)S(1)} %get-tuple-element.54), channel_id=1, source_target_pairs={{0,6},{1,7},{2,4},{3,5},{4,2},{5,3},{6,0},{7,1},{8,14},{9,15},{10,... | collective-permute-start | bytes 49160 | tf_op jit(solution)/shard_map/ppermute | solution.py:31
  24.6 3.7 %collective-permute-start.9 = (bf16[2,4096]{1,0:T(2,128)(2,1)S(1)}, bf16[2,4096]{1,0:T(2,128)(2,1)S(1)}, u32[]{:S(2)}, u32[]{:S(2)}) collective-permute-start(bf16[2,4096]{1,0:T(2,128)(2,1)S(1)} %get-tuple-element.55), channel_id=1, source_target_pairs={{0,2},{1,5},{2,0},{3,7},{4,6},{5,1},{6,4},{7,3},{8,10},{9,13},{10,... | collective-permute-start | bytes 49160 | tf_op jit(solution)/shard_map/ppermute | solution.py:31

commit v6 on v5

--- a/solution.py
+++ b/solution.py
@@ -21,10 +21,10 @@
     return lax.ppermute(x, axis, [(i, i ^ mask) for i in range(size)])
 
 
-def swap_by_core(x, axis, masks):
+def swap_by_core(x, axis, masks, across=0):
     size, cores = lax.axis_size(axis), lax.axis_size("tp")
     pairs = [
-        (i * cores + t, (i ^ masks[t % len(masks)]) * cores + t)
+        (i * cores + t, (i ^ masks[t % len(masks)]) * cores + (t ^ across))
         for i in range(size)
         for t in range(cores)
     ]
@@ -47,7 +47,7 @@
         masks += [(low, high), (high, low)]
         got += [mine, swap(mine, "tp", 1)]
     masks.append((size // 2, size // 2))
-    got.append(swap(x, "ctx", size // 2))
+    got.append(swap_by_core(x, "ctx", masks[-1], across=1))
     return masks, got
 
 
@@ -318,10 +318,11 @@
         read=12 * w_down.size,
         name="experts",
     )
-    back = [
-        results[0] if even == 0 else swap_by_core(results[i], "exp", (even, odd))
-        for i, (even, odd) in enumerate(masks)
-    ]
+    back = [results[0]]
+    for (even, odd), result in zip(masks[1:], results[1:]):
+        across = int(even.bit_count() > 1)
+        result = swap_by_core(result, "exp", (even, odd), across)
+        back.append(swap(result, "tp", 1) if across else result)
     (out,) = call(
         functools.partial(combine_kernel, live, masks),
         [((rows, width), jnp.bfloat16)],

time: 29.4 us -> 28 us (0.952)
  starting transfers between devices: 13.4 us -> 11.7 us
    ppermute x5, starting transfers between devices: 3.61 us -> 1.62 us  [swap(): return lax.ppermute(x, axis, [(i, i ^ mask) for i in range(size)])]
    ppermute x6 -> x7, waiting for transfers between devices: 6.56 us -> 7.03 us  [swap_by_core(): return lax.ppermute(x, (axis, 'tp'), pairs)]
    ppermute x6 -> x7, starting transfers between devices: 9.77 us -> 10.1 us  [swap_by_core(): return lax.ppermute(x, (axis, 'tp'), pairs)]
  transfers between devices with their start and end apart: 11 -> 12, of which waited for: 6 -> 6; matrix products, arithmetic and copies ran while one was open for 2% -> 2% of each run, Pallas kernels for 17% -> 17%
where the time goes in v6:
time: 28 us; the launch traced here: 27.8 us
  starting transfers between devices  11.7 us (42%)
  Pallas kernels  8.45 us (30%)
  waiting for transfers between devices  7.04 us (25%)
  matrix products  0.4 us (1%)
    ppermute x7, starting transfers between devices, swap_by_core(): return lax.ppermute(x, (axis, 'tp'), pairs)  10.1 us
    pallas_call x7, Pallas kernels, call(): pl.pallas_call(kernel, out_shape=[kept(shape, dtype) for shape, dtype in...  8.45 us
    ppermute x7, waiting for transfers between devices, swap_by_core(): return lax.ppermute(x, (axis, 'tp'), pairs)  7.03 us
    ppermute x5, starting transfers between devices, swap(): return lax.ppermute(x, axis, [(i, i ^ mask) for i in range(size)])  1.62 us
  transfers between devices with their start and end apart: 12, of which 6 were waited for; matrix products, arithmetic and copies ran while one was open for 2% of the time, Pallas kernels for 17%

profile of v6, /device:TPU:0, one launch (start us, length us, event | category | flops | bytes accessed | tf_op | source)
XLA Modules:
  0.0 27.8 jit_solution(9747023472961646995)
XLA Ops:
  0.0 1.0 %open.1.refs_0_ = bf16[64,128]{1,0:T(8,128)(2,1)S(1)} custom-call(bf16[32,4,128]{2,1,0:T(4,128)(2,1)} %key_hbm.1, bf16[32,4,128]{2,1,0:T(4,128)(2,1)} %value_hbm.1), custom_call_target="tpu_custom_call" | custom-call | tf_op jit(solution)/shard_map/open/pallas_call | solution.py:59
  1.0 3.1 %collective-permute-start = (bf16[64,128]{1,0:T(8,128)(2,1)S(1)}, bf16[64,128]{1,0:T(8,128)(2,1)S(1)}, u32[]{:S(2)}, u32[]{:S(2)}) collective-permute-start(bf16[64,128]{1,0:T(8,128)(2,1)S(1)} %open.1.refs_0_), channel_id=1, source_target_pairs={{0,8},{1,25},{8,0},{9,17},{16,24},{17,9},{24,16},{25,1},{2,10},{3,... | collective-permute-start | bytes 49160 | tf_op jit(solution)/shard_map/ppermute | solution.py:31
  4.1 0.6 %collective-permute-start.2 = (bf16[64,128]{1,0:T(8,128)(2,1)S(1)}, bf16[64,128]{1,0:T(8,128)(2,1)S(1)}, u32[]{:S(2)}, u32[]{:S(2)}) collective-permute-start(bf16[64,128]{1,0:T(8,128)(2,1)S(1)} %open.1.refs_0_), channel_id=1, source_target_pairs={{0,17},{1,16},{8,25},{9,24},{16,1},{17,0},{24,9},{25,8},{2,19},{3,... | collective-permute-start | bytes 49160 | tf_op jit(solution)/shard_map/ppermute | solution.py:31
  4.8 1.1 %collective-permute-done.refs_1_ = bf16[64,128]{1,0:T(8,128)(2,1)S(1)} collective-permute-done((bf16[64,128]{1,0:T(8,128)(2,1)S(1)}, bf16[64,128]{1,0:T(8,128)(2,1)S(1)}, u32[]{:S(2)}, u32[]{:S(2)}) %collective-permute-start) | collective-permute-done | bytes 16416 | tf_op jit(solution)/shard_map/ppermute | solution.py:31
  5.9 1.0 %collective-permute-start.1 = (bf16[64,128]{1,0:T(8,128)(2,1)S(1)}, bf16[64,128]{1,0:T(8,128)(2,1)S(1)}, u32[]{:S(2)}, u32[]{:S(2)}) collective-permute-start(bf16[64,128]{1,0:T(8,128)(2,1)S(1)} %collective-permute-done.refs_1_), channel_id=1, source_target_pairs={{0,1},{1,0},{2,3},{3,2},{4,5},{5,4},{6,7},{7,6},{8,9},{9,8},{10,11... | collective-permute-start | bytes 49160 | tf_op jit(solution)/shard_map/ppermute | solution.py:21
  6.8 0.0 collective-permute-start.4
  6.8 0.5 %collective-permute-start.5 = (bf16[192,4096]{1,0:T(8,128)(2,1)}, bf16[192,4096]{1,0:T(8,128)(2,1)S(1)}, u32[]{:S(2)}, u32[]{:S(2)}) collective-permute-start(bf16[192,4096]{1,0:T(8,128)(2,1)} %bitcast.14), channel_id=1, source_target_pairs={{0,1},{1,0},{2,3},{3,2},{4,5},{5,4},{6,7},{7,6},{8,9},{9,8},{10,11... | collective-permute-start | bytes 4718600 | tf_op jit(solution)/shard_map/ppermute | solution.py:21
  7.4 0.0 collective-permute-start.7
  7.4 0.8 %route.1 = (bf16[32,128]{1,0:T(8,128)(2,1)S(1)}, bf16[16,128]{1,0:T(8,128)(2,1)S(1)}, f32[4,128]{1,0:T(4,128)S(1)}) custom-call(bf16[16,2,128]{2,1,0:T(2,128)(2,1)} %bitcast.18, s32[4,8]{1,0:T(4,128)} %refs_1_, f32[4,8]{1,0:T(4,128)} %refs_2_), custom_call_target="tpu_custom_call" | custom-call | tf_op jit(solution)/shard_map/route/pallas_call | solution.py:59
  8.2 0.0 collective-permute-done.2.refs_3_
  8.2 0.0 collective-permute-done.1.refs_2_
  8.2 0.3 %attend.1 = bf16[16,256]{1,0:T(8,128)(2,1)S(1)} custom-call(bf16[32,128]{1,0:T(8,128)(2,1)S(1)} %get-tuple-element.35.q_ref, bf16[64,128]{1,0:T(8,128)(2,1)S(1)} %open.1.refs_0_, bf16[64,128]{1,0:T(8,128)(2,1)S(1)} %collective-permute-done.refs_1_, bf16[64,128]{1,0:T(8,128)(2,1)S(1)} %collective-permute-done.1.refs_2_, ...), custom_call_target="tpu_custom_call" | custom-call | tf_op jit(solution)/shard_map/attend/pallas_call | solution.py:59
  8.6 0.4 %convolution_convert_fusion = bf16[16,4096]{1,0:T(8,128)(2,1)S(1)} fusion(bf16[16,256]{1,0:T(8,128)(2,1)S(1)} %attend.1, bf16[256,4096]{1,0:T(8,128)(2,1)S(1)} %copy-done), kind=kOutput, calls=%fused_computation | convolution fusion | flops 33619968 | bytes 2236416 | tf_op jit(solution)/shard_map/dot_general | solution.py:282
  9.0 1.6 %collective-permute-start.3 = (bf16[16,4224]{1,0:T(8,128)(2,1)S(1)}, bf16[16,4224]{1,0:T(8,128)(2,1)S(1)}, u32[]{:S(2)}, u32[]{:S(2)}) collective-permute-start(bf16[16,4224]{1,0:T(8,128)(2,1)S(1)} %pad_maximum_fusion), channel_id=1, source_target_pairs={{0,2},{1,5},{2,0},{3,7},{4,6},{5,1},{6,4},{7,3},{8,10},{9,13},{10,... | collective-permute-start | bytes 405512 | tf_op jit(solution)/shard_map/ppermute | solution.py:31
  10.6 2.8 %load.1 = (bf16[4096,384]{1,0:T(8,128)(2,1)S(1)}, bf16[192,4096]{1,0:T(8,128)(2,1)S(1)}) custom-call(bf16[192,4096]{1,0:T(8,128)(2,1)} %bitcast.13, bf16[192,4096]{1,0:T(8,128)(2,1)} %bitcast.15, bf16[192,4096]{1,0:T(8,128)(2,1)} %bitcast.17), custom_call_target="tpu_custom_call" | custom-call | bytes 4718592 | tf_op jit(solution)/shard_map/load/pallas_call | solution.py:59
  13.4 0.7 %collective-permute-done.3 = bf16[16,4224]{1,0:T(8,128)(2,1)S(1)} collective-permute-done((bf16[16,4224]{1,0:T(8,128)(2,1)S(1)}, bf16[16,4224]{1,0:T(8,128)(2,1)S(1)}, u32[]{:S(2)}, u32[]{:S(2)}) %collective-permute-start.3) | collective-permute-done | bytes 135200 | tf_op jit(solution)/shard_map/ppermute | solution.py:31
  14.1 0.0 collective-permute-done.4.gate_ref
  14.1 0.0 collective-permute-done.5.up_ref
  14.1 0.0 copy-start.1
  14.2 1.6 %collective-permute-start.6 = (bf16[16,4224]{1,0:T(8,128)(2,1)S(1)}, bf16[16,4224]{1,0:T(8,128)(2,1)S(1)}, u32[]{:S(2)}, u32[]{:S(2)}) collective-permute-start(bf16[16,4224]{1,0:T(8,128)(2,1)S(1)} %add_convert_fusion.mine_ref), channel_id=1, source_target_pairs={{0,4},{1,3},{2,6},{3,1},{4,0},{5,7},{6,2},{7,5},{8,12},{9,11},{10,... | collective-permute-start | bytes 405512 | tf_op jit(solution)/shard_map/ppermute | solution.py:31
  15.8 0.9 %turn.1.refs_2_ = bf16[4096,384]{1,0:T(8,128)(2,1)S(1)} custom-call(bf16[192,4096]{1,0:T(8,128)(2,1)S(1)} %collective-permute-done.4.gate_ref, bf16[192,4096]{1,0:T(8,128)(2,1)S(1)} %collective-permute-done.5.up_ref), custom_call_target="tpu_custom_call" | custom-call | bytes 3145728 | tf_op jit(solution)/shard_map/turn/pallas_call | solution.py:59
  16.6 0.0 collective-permute-done.7.refs_3_
  16.6 2.6 %collective-permute-done.6.other_ref = bf16[16,4224]{1,0:T(8,128)(2,1)S(1)} collective-permute-done((bf16[16,4224]{1,0:T(8,128)(2,1)S(1)}, bf16[16,4224]{1,0:T(8,128)(2,1)S(1)}, u32[]{:S(2)}, u32[]{:S(2)}) %collective-permute-start.6) | collective-permute-done | bytes 135200 | tf_op jit(solution)/shard_map/ppermute | solution.py:31
  19.2 1.8 %experts.1 = (f32[4,4096]{1,0:T(4,128)S(1)}, bf16[2,4096]{1,0:T(2,128)(2,1)S(1)}, bf16[2,4096]{1,0:T(2,128)(2,1)S(1)}, bf16[2,4096]{1,0:T(2,128)(2,1)S(1)}, bf16[2,4096]{1,0:T(2,128)(2,1)S(1)}) custom-call(bf16[16,4224]{1,0:T(8,128)(2,1)S(1)} %add_convert_fusion.mine_ref, bf16[16,4224]{1,0:T(8,128)(2,1)S(1)} %collective-permute-done.6.other_ref, ...), custom_call_target="tpu_custom_call" | custom-call | flops 75497472 | bytes 9437184 | tf_op jit(solution)/shard_map/experts/pallas_call | solution.py:59
  21.0 1.6 %collective-permute-start.8 = (bf16[2,4096]{1,0:T(2,128)(2,1)S(1)}, bf16[2,4096]{1,0:T(2,128)(2,1)S(1)}, u32[]{:S(2)}, u32[]{:S(2)}) collective-permute-start(bf16[2,4096]{1,0:T(2,128)(2,1)S(1)} %get-tuple-element.54), channel_id=1, source_target_pairs={{0,7},{1,6},{2,5},{3,4},{4,3},{5,2},{6,1},{7,0},{8,15},{9,14},{10,... | collective-permute-start | bytes 49160 | tf_op jit(solution)/shard_map/ppermute | solution.py:31
  22.7 0.5 %collective-permute-start.10 = (bf16[2,4096]{1,0:T(2,128)(2,1)S(1)}, bf16[2,4096]{1,0:T(2,128)(2,1)S(1)}, u32[]{:S(2)}, u32[]{:S(2)}) collective-permute-start(bf16[2,4096]{1,0:T(2,128)(2,1)S(1)} %get-tuple-element.55), channel_id=1, source_target_pairs={{0,2},{1,5},{2,0},{3,7},{4,6},{5,1},{6,4},{7,3},{8,10},{9,13},{10,... | collective-permute-start | bytes 49160 | tf_op jit(solution)/shard_map/ppermute | solution.py:31
  23.2 1.0 %collective-permute-start.11 = (bf16[2,4096]{1,0:T(2,128)(2,1)S(1)}, bf16[2,4096]{1,0:T(2,128)(2,1)S(1)}, u32[]{:S(2)}, u32[]{:S(2)}) collective-permute-start(bf16[2,4096]{1,0:T(2,128)(2,1)S(1)} %get-tuple-element.56), channel_id=1, source_target_pairs={{0,4},{1,3},{2,6},{3,1},{4,0},{5,7},{6,2},{7,5},{8,12},{9,11},{10,... | collective-permute-start | bytes 49160 | tf_op jit(solution)/shard_map/ppermute | solution.py:31
  24.2 1.0 %collective-permute-done.8 = bf16[2,4096]{1,0:T(2,128)(2,1)S(1)} collective-permute-done((bf16[2,4096]{1,0:T(2,128)(2,1)S(1)}, bf16[2,4096]{1,0:T(2,128)(2,1)S(1)}, u32[]{:S(2)}, u32[]{:S(2)}) %collective-permute-start.8) | collective-permute-done | bytes 16416 | tf_op jit(solution)/shard_map/ppermute | solution.py:31
  25.2 0.1 collective-permute-start.9
  25.3 1.1 %collective-permute-done.10.refs_2_ = bf16[2,4096]{1,0:T(2,128)(2,1)S(1)} collective-permute-done((bf16[2,4096]{1,0:T(2,128)(2,1)S(1)}, bf16[2,4096]{1,0:T(2,128)(2,1)S(1)}, u32[]{:S(2)}, u32[]{:S(2)}) %collective-permute-start.10) | collective-permute-done | bytes 16416 | tf_op jit(solution)/shard_map/ppermute | solution.py:31
  26.4 0.5 %collective-permute-done.11.refs_3_ = bf16[2,4096]{1,0:T(2,128)(2,1)S(1)} collective-permute-done((bf16[2,4096]{1,0:T(2,128)(2,1)S(1)}, bf16[2,4096]{1,0:T(2,128)(2,1)S(1)}, u32[]{:S(2)}, u32[]{:S(2)}) %collective-permute-start.11) | collective-permute-done | bytes 16416 | tf_op jit(solution)/shard_map/ppermute | solution.py:31
  26.9 0.8 %combine.1 = bf16[4,4096]{1,0:T(4,128)(2,1)} custom-call(f32[4,128]{1,0:T(4,128)S(1)} %get-tuple-element.34.mix_ref, f32[4,4096]{1,0:T(4,128)S(1)} %get-tuple-element.52.own_ref, bf16[2,4096]{1,0:T(2,128)(2,1)S(1)} %get-tuple-element.53.refs_0_, bf16[2,4096]{1,0:T(2,128)(2,1)S(1)} %collective-permute-done.9.refs_1_, ...), custom_call_target="tpu_custom_call" | custom-call | tf_op jit(solution)/shard_map/combine/pallas_call | solution.py:59
  (6 shorter events, 0.1 us)
Async XLA Ops:
  0.0 8.6 %copy-start = (bf16[256,4096]{1,0:T(8,128)(2,1)S(1)}, bf16[256,4096]{1,0:T(8,128)(2,1)}, u32[]{:S(2)}) copy-start(bf16[256,4096]{1,0:T(8,128)(2,1)} %param.13) | copy-start | bytes 6291460
  1.0 4.8 %collective-permute-start = (bf16[64,128]{1,0:T(8,128)(2,1)S(1)}, bf16[64,128]{1,0:T(8,128)(2,1)S(1)}, u32[]{:S(2)}, u32[]{:S(2)}) collective-permute-start(bf16[64,128]{1,0:T(8,128)(2,1)S(1)} %open.1.refs_0_), channel_id=1, source_target_pairs={{0,8},{1,25},{8,0},{9,17},{16,24},{17,9},{24,16},{25,1},{2,10},{3,... | collective-permute-start | bytes 49160 | tf_op jit(solution)/shard_map/ppermute | solution.py:31
  4.1 4.1 %collective-permute-start.2 = (bf16[64,128]{1,0:T(8,128)(2,1)S(1)}, bf16[64,128]{1,0:T(8,128)(2,1)S(1)}, u32[]{:S(2)}, u32[]{:S(2)}) collective-permute-start(bf16[64,128]{1,0:T(8,128)(2,1)S(1)} %open.1.refs_0_), channel_id=1, source_target_pairs={{0,17},{1,16},{8,25},{9,24},{16,1},{17,0},{24,9},{25,8},{2,19},{3,... | collective-permute-start | bytes 49160 | tf_op jit(solution)/shard_map/ppermute | solution.py:31
  5.9 2.4 %collective-permute-start.1 = (bf16[64,128]{1,0:T(8,128)(2,1)S(1)}, bf16[64,128]{1,0:T(8,128)(2,1)S(1)}, u32[]{:S(2)}, u32[]{:S(2)}) collective-permute-start(bf16[64,128]{1,0:T(8,128)(2,1)S(1)} %collective-permute-done.refs_1_), channel_id=1, source_target_pairs={{0,1},{1,0},{2,3},{3,2},{4,5},{5,4},{6,7},{7,6},{8,9},{9,8},{10,11... | collective-permute-start | bytes 49160 | tf_op jit(solution)/shard_map/ppermute | solution.py:21
  6.8 7.3 %collective-permute-start.4 = (bf16[192,4096]{1,0:T(8,128)(2,1)}, bf16[192,4096]{1,0:T(8,128)(2,1)S(1)}, u32[]{:S(2)}, u32[]{:S(2)}) collective-permute-start(bf16[192,4096]{1,0:T(8,128)(2,1)} %bitcast.12), channel_id=1, source_target_pairs={{0,1},{1,0},{2,3},{3,2},{4,5},{5,4},{6,7},{7,6},{8,9},{9,8},{10,11... | collective-permute-start | bytes 4718600 | tf_op jit(solution)/shard_map/ppermute | solution.py:21
  6.8 7.3 %collective-permute-start.5 = (bf16[192,4096]{1,0:T(8,128)(2,1)}, bf16[192,4096]{1,0:T(8,128)(2,1)S(1)}, u32[]{:S(2)}, u32[]{:S(2)}) collective-permute-start(bf16[192,4096]{1,0:T(8,128)(2,1)} %bitcast.14), channel_id=1, source_target_pairs={{0,1},{1,0},{2,3},{3,2},{4,5},{5,4},{6,7},{7,6},{8,9},{9,8},{10,11... | collective-permute-start | bytes 4718600 | tf_op jit(solution)/shard_map/ppermute | solution.py:21
  7.4 9.3 %collective-permute-start.7 = (bf16[192,4096]{1,0:T(8,128)(2,1)}, bf16[192,4096]{1,0:T(8,128)(2,1)S(1)}, u32[]{:S(2)}, u32[]{:S(2)}) collective-permute-start(bf16[192,4096]{1,0:T(8,128)(2,1)} %bitcast.16), channel_id=1, source_target_pairs={{0,1},{1,0},{2,3},{3,2},{4,5},{5,4},{6,7},{7,6},{8,9},{9,8},{10,11... | collective-permute-start | bytes 4718600 | tf_op jit(solution)/shard_map/ppermute | solution.py:21
  9.0 5.1 %collective-permute-start.3 = (bf16[16,4224]{1,0:T(8,128)(2,1)S(1)}, bf16[16,4224]{1,0:T(8,128)(2,1)S(1)}, u32[]{:S(2)}, u32[]{:S(2)}) collective-permute-start(bf16[16,4224]{1,0:T(8,128)(2,1)S(1)} %pad_maximum_fusion), channel_id=1, source_target_pairs={{0,2},{1,5},{2,0},{3,7},{4,6},{5,1},{6,4},{7,3},{8,10},{9,13},{10,... | collective-permute-start | bytes 405512 | tf_op jit(solution)/shard_map/ppermute | solution.py:31
  14.1 5.1 %copy-start.1 = (f32[4096]{0:T(1024)S(1)}, f32[4096]{0:T(1024)}, u32[]{:S(2)}) copy-start(f32[4096]{0:T(1024)} %param.14) | copy-start | bytes 49156
  14.2 5.1 %collective-permute-start.6 = (bf16[16,4224]{1,0:T(8,128)(2,1)S(1)}, bf16[16,4224]{1,0:T(8,128)(2,1)S(1)}, u32[]{:S(2)}, u32[]{:S(2)}) collective-permute-start(bf16[16,4224]{1,0:T(8,128)(2,1)S(1)} %add_convert_fusion.mine_ref), channel_id=1, source_target_pairs={{0,4},{1,3},{2,6},{3,1},{4,0},{5,7},{6,2},{7,5},{8,12},{9,11},{10,... | collective-permute-start | bytes 405512 | tf_op jit(solution)/shard_map/ppermute | solution.py:31
  21.0 4.2 %collective-permute-start.8 = (bf16[2,4096]{1,0:T(2,128)(2,1)S(1)}, bf16[2,4096]{1,0:T(2,128)(2,1)S(1)}, u32[]{:S(2)}, u32[]{:S(2)}) collective-permute-start(bf16[2,4096]{1,0:T(2,128)(2,1)S(1)} %get-tuple-element.54), channel_id=1, source_target_pairs={{0,7},{1,6},{2,5},{3,4},{4,3},{5,2},{6,1},{7,0},{8,15},{9,14},{10,... | collective-permute-start | bytes 49160 | tf_op jit(solution)/shard_map/ppermute | solution.py:31
  22.7 3.7 %collective-permute-start.10 = (bf16[2,4096]{1,0:T(2,128)(2,1)S(1)}, bf16[2,4096]{1,0:T(2,128)(2,1)S(1)}, u32[]{:S(2)}, u32[]{:S(2)}) collective-permute-start(bf16[2,4096]{1,0:T(2,128)(2,1)S(1)} %get-tuple-element.55), channel_id=1, source_target_pairs={{0,2},{1,5},{2,0},{3,7},{4,6},{5,1},{6,4},{7,3},{8,10},{9,13},{10,... | collective-permute-start | bytes 49160 | tf_op jit(solution)/shard_map/ppermute | solution.py:31
  23.2 3.7 %collective-permute-start.11 = (bf16[2,4096]{1,0:T(2,128)(2,1)S(1)}, bf16[2,4096]{1,0:T(2,128)(2,1)S(1)}, u32[]{:S(2)}, u32[]{:S(2)}) collective-permute-start(bf16[2,4096]{1,0:T(2,128)(2,1)S(1)} %get-tuple-element.56), channel_id=1, source_target_pairs={{0,4},{1,3},{2,6},{3,1},{4,0},{5,7},{6,2},{7,5},{8,12},{9,11},{10,... | collective-permute-start | bytes 49160 | tf_op jit(solution)/shard_map/ppermute | solution.py:31
  25.2 1.8 %collective-permute-start.9 = (bf16[2,4096]{1,0:T(2,128)(2,1)S(1)}, bf16[2,4096]{1,0:T(2,128)(2,1)S(1)}, u32[]{:S(2)}, u32[]{:S(2)}) collective-permute-start(bf16[2,4096]{1,0:T(2,128)(2,1)S(1)} %collective-permute-done.8), channel_id=1, source_target_pairs={{0,1},{1,0},{2,3},{3,2},{4,5},{5,4},{6,7},{7,6},{8,9},{9,8},{10,11... | collective-permute-start | bytes 49160 | tf_op jit(solution)/shard_map/ppermute | solution.py:21

commit v7 on v6

--- a/solution.py
+++ b/solution.py
@@ -9,6 +9,7 @@
 
 CAP = 2
 LANES = 128
+CHUNKS = 4
 VMEM_LIMIT = 24 * 1024 * 1024
 
 
@@ -47,7 +48,7 @@
         masks += [(low, high), (high, low)]
         got += [mine, swap(mine, "tp", 1)]
     masks.append((size // 2, size // 2))
-    got.append(swap_by_core(x, "ctx", masks[-1], across=1))
+    got.append(swap_by_core(x, "ctx", masks[-1]))
     return masks, got
 
 
@@ -60,7 +61,7 @@
         kernel,
         out_shape=[kept(shape, dtype) for shape, dtype in outs],
         in_specs=[pl.BlockSpec(memory_space=where)] * len(args),
-        out_specs=[pl.BlockSpec(memory_space=pltpu.VMEM)] * len(outs),
+        out_specs=[pl.BlockSpec(memory_space=pltpu.HBM if kept is pltpu.HBM else pltpu.VMEM)] * len(outs),
         scratch_shapes=scratch,
         compiler_params=pltpu.CompilerParams(vmem_limit_bytes=VMEM_LIMIT),
         cost_estimate=pl.CostEstimate(flops=flops, bytes_accessed=read, transcendentals=0),
@@ -84,14 +85,33 @@
         kv_ref[n * span : (n + 1) * span, :] = kept.astype(kv_ref.dtype)
 
 
-def route_kernel(live, blocks, *refs):
-    ins, (q_ref, note_ref, mix_ref), held, sems = refs[:3], refs[3:6], refs[6:9], refs[9]
+def allow(masks, blocks, rows, out_ref):
+    heads_rows, keys = out_ref.shape
+    count = blocks * rows
+    span = keys // len(masks)
+    n_tp = lax.axis_size("tp")
+    ctx, core = lax.axis_index("ctx"), lax.axis_index("tp")
+    lane = lax.broadcasted_iota(jnp.int32, (1, keys), 1)
+    start = jnp.zeros_like(lane)
+    for j, (even, odd) in enumerate(masks):
+        block = ctx ^ jnp.where(core == 0, even, odd)
+        start = jnp.where(lane // span == j, block * span, start)
+    key_pos = start + lane % span
+    row = lax.broadcasted_iota(jnp.int32, (heads_rows, 1), 0) % count
+    query_pos = ((ctx * blocks + row // rows) * n_tp + core) * rows + row % rows
+    allowed = key_pos <= query_pos
+    out_ref[...] = jnp.where(allowed, 0.0, -1e30)
+
+
+def route_kernel(live, blocks, masks, *refs):
+    ins, (q_ref, note_ref, mix_ref, allowed_ref), held, sems = refs[:3], refs[3:7], refs[7:10], refs[10]
     copies = [pltpu.make_async_copy(i, h, sems.at[n]) for n, (i, h) in enumerate(zip(ins, held))]
     for copy in copies:
         copy.start()
     query_ref, routes_ref, weight_ref = held
     heads = query_ref.shape[1]
     mine = lax.axis_index("exp")
+    allow(masks, blocks, routes_ref.shape[0], allowed_ref)
     for copy in copies:
         copy.wait()
     q_ref[...] = jnp.concatenate([query_ref[:, h, :] for h in range(heads)], axis=0)
@@ -117,31 +137,19 @@
     ).astype(note_ref.dtype)
 
 
-def attend_kernel(masks, blocks, q_ref, *refs):
+def attend_kernel(q_ref, allowed_ref, *refs):
     kv_refs, out_ref = refs[:-1], refs[-1]
     count = out_ref.shape[0]
     heads = q_ref.shape[0] // count
     head_dim = q_ref.shape[1]
     span = kv_refs[0].shape[0] // 2
-    rows = count // blocks
-    n_tp = lax.axis_size("tp")
-    ctx, core = lax.axis_index("ctx"), lax.axis_index("tp")
     key = jnp.concatenate([r[:span, :] for r in kv_refs], axis=0)
     value = jnp.concatenate([r[span:, :] for r in kv_refs], axis=0)
     score = lax.dot_general(
         q_ref[...], key, (((1,), (1,)), ((), ())), preferred_element_type=jnp.float32
     ) * (head_dim ** (-0.5))
-    lane = lax.broadcasted_iota(jnp.int32, (1, len(kv_refs) * span), 1)
-    start = jnp.zeros_like(lane)
-    for j, (even, odd) in enumerate(masks):
-        block = ctx ^ jnp.where(core == 0, even, odd)
-        start = jnp.where(lane // span == j, block * span, start)
-    key_pos = start + lane % span
-    row = lax.broadcasted_iota(jnp.int32, (heads * count, 1), 0) % count
-    query_pos = ((ctx * blocks + row // rows) * n_tp + core) * rows + row % rows
-    allowed = key_pos <= query_pos
-    score = jnp.where(allowed, score, -1e30)
-    prob = jnp.where(allowed, jnp.exp(score - jnp.max(score, axis=1, keepdims=True)), 0.0)
+    score = score + allowed_ref[...]
+    prob = jnp.exp(score - jnp.max(score, axis=1, keepdims=True))
     total = jnp.sum(prob, axis=1, keepdims=True)
     mixed = jnp.dot(prob.astype(jnp.bfloat16), value, preferred_element_type=jnp.float32) / total
     mixed = mixed.astype(jnp.bfloat16)
@@ -167,32 +175,21 @@
     copies[2].wait()
 
 
-def hidden_units(x, wide_ref, down_ref):
+def hidden_units(x, inverse, wide_ref, down_ref):
     units = down_ref.shape[0]
-    both = jnp.dot(x, wide_ref[...], preferred_element_type=jnp.float32)
+    both = jnp.dot(x, wide_ref[...], preferred_element_type=jnp.float32) * inverse
     hidden = silu_mul(both[:, :units], both[:, units:]).astype(jnp.bfloat16)
     return jnp.dot(hidden, down_ref[...], preferred_element_type=jnp.float32)
 
 
-def experts_kernel(blocks, live, masks, mine_ref, other_ref, gain_ref, *refs):
+def experts_kernel(blocks, live, masks, parts, *refs):
+    part_refs, gain_ref, refs = refs[:parts], refs[parts], refs[parts + 1 :]
     weights, own_ref, outs = refs[:4], refs[4], refs[5:]
-    count, width = mine_ref.shape[0], own_ref.shape[1]
+    count, width = part_refs[0].shape[0], own_ref.shape[1]
     rows = count // blocks
     mine = lax.axis_index("exp")
-    summed = (mine_ref[:, :width].astype(jnp.float32) + other_ref[:, :width].astype(jnp.float32)).astype(
-        jnp.bfloat16
-    )
-    shape = (rows, count)
-    own = (
-        lax.broadcasted_iota(jnp.int32, shape, 0) + mine * rows
-        == lax.broadcasted_iota(jnp.int32, shape, 1)
-    )
-    own = own.astype(jnp.float32).astype(jnp.bfloat16)
-    own_ref[...] = jnp.dot(own, summed, preferred_element_type=jnp.float32)
-    state = summed.astype(jnp.float32)
-    note = mine_ref[:, width:] + other_ref[:, width:]
-    inverse = lax.rsqrt(jnp.mean(state * state, axis=1, keepdims=True) + 1e-06)
-    normed = (state * inverse * gain_ref[...]).astype(jnp.bfloat16)
+    summed = sum(r[:, :width].astype(jnp.float32) for r in part_refs).astype(jnp.bfloat16)
+    note = functools.reduce(lambda x, y: x + y, [r[:, width:] for r in part_refs])
     expert = lax.rem(mine, live)
     slots = blocks * CAP
     shape = (slots, note.shape[1])
@@ -213,27 +210,48 @@
     for i, (even, odd) in enumerate(masks):
         mask = jnp.where(place == i, jnp.where(core == 0, even, odd), mask)
     same = mask == (lax.broadcasted_iota(jnp.int32, shape, 1) // rows) ^ mine
-    pick = jnp.where(same, pick, 0.0).astype(jnp.bfloat16)
-    x = jnp.dot(pick, normed, preferred_element_type=jnp.float32).astype(jnp.bfloat16)
-    result = hidden_units(x, *weights[:2]) + hidden_units(x, *weights[2:])
+    pick = jnp.where(same, pick, 0.0)
+    shape = (rows, count)
+    own = (
+        lax.broadcasted_iota(jnp.int32, shape, 0) + mine * rows
+        == lax.broadcasted_iota(jnp.int32, shape, 1)
+    )
+    pick = jnp.concatenate([pick, own.astype(jnp.float32)], axis=0).astype(jnp.bfloat16)
+    picked = jnp.dot(pick, summed, preferred_element_type=jnp.float32)
+    own_ref[...] = picked[slots:]
+    state = picked[:slots]
+    inverse = lax.rsqrt(jnp.mean(state * state, axis=1, keepdims=True) + 1e-06)
+    x = (state * gain_ref[...]).astype(jnp.bfloat16)
+    result = hidden_units(x, inverse, *weights[:2]) + hidden_units(x, inverse, *weights[2:])
     for m, out_ref in enumerate(outs):
         out_ref[...] = result[m * CAP : (m + 1) * CAP].astype(out_ref.dtype)
 
 
 def combine_kernel(live, masks, mix_ref, own_ref, *refs):
-    back_refs, out_ref = refs[:-1], refs[-1]
-    mine = lax.axis_index("exp")
+    back_refs, (out_hbm, held_ref, sems) = refs[:-3], refs[-3:]
+    mine, core = lax.axis_index("exp"), lax.axis_index("tp")
     mix = mix_ref[...]
     lane = lax.broadcasted_iota(jnp.int32, mix.shape, 1)
-    total = own_ref[...]
-    core = lax.axis_index("tp")
-    for (even, odd), back_ref in zip(masks, back_refs):
+    shares = []
+    for even, odd in masks:
         expert = lax.rem(mine ^ jnp.where(core == 0, even, odd), live)
-        back = back_ref[...].astype(jnp.float32)
         for s in range(CAP):
-            share = jnp.sum(jnp.where(lane == expert * CAP + s, mix, 0.0), axis=1, keepdims=True)
-            total = total + share * back[s : s + 1]
-    out_ref[...] = total.astype(out_ref.dtype)
+            wanted = lane == expert * CAP + s
+            shares.append(jnp.sum(jnp.where(wanted, mix, 0.0), axis=1, keepdims=True))
+    width = out_hbm.shape[1] // CHUNKS
+    copies = []
+    for n in range(CHUNKS):
+        at = slice(n * width, (n + 1) * width)
+        total = own_ref[:, at]
+        for m, back_ref in enumerate(back_refs):
+            back = back_ref[:, at].astype(jnp.float32)
+            for s in range(CAP):
+                total = total + shares[m * CAP + s] * back[s : s + 1]
+        held_ref[:, at] = total.astype(held_ref.dtype)
+        copies.append(pltpu.make_async_copy(held_ref.at[:, at], out_hbm.at[:, at], sems.at[n]))
+        copies[-1].start()
+    for copy in copies:
+        copy.wait()
 
 
 def on_device(
@@ -260,12 +278,13 @@
     small = (queries.reshape(count, heads, head_dim), routes, route_weight)
     got[1], *tied = lax.optimization_barrier((got[1], *weights, *small))
     moved = [swap(w, "tp", 1) for w in tied[:3]]
-    query, note, mix = call(
-        functools.partial(route_kernel, live, blocks),
+    query, note, mix, allowed = call(
+        functools.partial(route_kernel, live, blocks, masks),
         [
             ((heads * count, head_dim), jnp.bfloat16),
             ((count, note_width), jnp.bfloat16),
             ((rows, note_width), jnp.float32),
+            ((heads * count, len(got) * keys.shape[0]), jnp.float32),
         ],
         *far(tied[3:]),
         where=pltpu.HBM,
@@ -273,10 +292,12 @@
         name="route",
     )
     (mixed,) = call(
-        functools.partial(attend_kernel, masks, blocks),
+        attend_kernel,
         [((count, heads * head_dim), jnp.bfloat16)],
         query,
+        allowed,
         *got,
+        flops=10**10,
         name="attend",
     )
     term = jnp.dot(mixed, out_weight, preferred_element_type=jnp.float32).astype(jnp.bfloat16)
@@ -293,23 +314,24 @@
         name="load",
     )
     steps = [1 << i for i in range(n_exp.bit_length() - 1)]
-    for i, step in enumerate(steps):
-        other = swap_by_core(summed, "exp", (step, steps[-1 - i]))
-        if i < len(steps) - 1:
-            summed = (summed.astype(jnp.float32) + other.astype(jnp.float32)).astype(jnp.bfloat16)
-            if i == 0:
-                summed, *tied = lax.optimization_barrier((summed, *weights, *moved[:2]))
-                weights, moved[:2] = tied[:2], tied[2:]
+    for at in range(0, len(steps), 2):
+        pair = steps[at : at + 2]
+        low, high = pair[0], pair[-1]
+        masks = [(low | high,) * 2, (low, high), (high, low)] if len(pair) == 2 else [(low, low)]
+        others = [swap_by_core(summed, "exp", m) for m in masks]
+        if at + 2 < len(steps):
+            summed = sum(o.astype(jnp.float32) for o in others) + summed.astype(jnp.float32)
+            summed = summed.astype(jnp.bfloat16)
     (wide,) = call(
         turn, [((width, 2 * units), w_down.dtype)], *moved[:2], read=4 * w_down.size, name="turn"
     )
     masks = by_distance(n_exp)
     slots = blocks * CAP
     own, *results = call(
-        functools.partial(experts_kernel, blocks, live, masks),
+        functools.partial(experts_kernel, blocks, live, masks, 1 + len(others)),
         [((rows, width), jnp.float32)] + [((CAP, width), jnp.bfloat16)] * n_exp,
+        *others,
         summed,
-        other,
         norm_gain.reshape(1, width),
         *weights,
         wide,
@@ -329,7 +351,8 @@
         mix,
         own,
         *back,
-        kept=jax.ShapeDtypeStruct,
+        kept=pltpu.HBM,
+        scratch=[pltpu.VMEM((rows, width), jnp.bfloat16), pltpu.SemaphoreType.DMA((CHUNKS,))],
         name="combine",
     )
     return out

time: 28 us -> 27.6 us (0.986)
  waiting for transfers between devices: 7.04 us -> 5.58 us
  starting transfers between devices: 11.7 us -> 12.8 us
    ppermute x7 -> x8, starting transfers between devices: 10.1 us -> 11.8 us  [swap_by_core(): return lax.ppermute(x, (axis, 'tp'), pairs)]
    ppermute x7 -> x8, waiting for transfers between devices: 7.03 us -> 5.57 us  [swap_by_core(): return lax.ppermute(x, (axis, 'tp'), pairs)]
    ppermute x5, starting transfers between devices: 1.62 us -> 1.02 us  [swap(): return lax.ppermute(x, axis, [(i, i ^ mask) for i in range(size)])]
  transfers between devices with their start and end apart: 12 -> 13, of which waited for: 6 -> 5; matrix products, arithmetic and copies ran while one was open for 2% -> 2% of each run, Pallas kernels for 17% -> 18%
where the time goes in v7:
time: 27.6 us; the launch traced here: 27.3 us
  starting transfers between devices  12.8 us (46%)
  Pallas kernels  8.43 us (31%)
  waiting for transfers between devices  5.58 us (20%)
  matrix products  0.4 us (1%)
    ppermute x8, starting transfers between devices, swap_by_core(): return lax.ppermute(x, (axis, 'tp'), pairs)  11.8 us
    pallas_call x7, Pallas kernels, call(): pl.pallas_call(kernel, out_shape=[kept(shape, dtype) for shape, dtype in...  8.43 us
    ppermute x8, waiting for transfers between devices, swap_by_core(): return lax.ppermute(x, (axis, 'tp'), pairs)  5.57 us
    ppermute x5, starting transfers between devices, swap(): return lax.ppermute(x, axis, [(i, i ^ mask) for i in range(size)])  1.02 us
  transfers between devices with their start and end apart: 13, of which 5 were waited for; matrix products, arithmetic and copies ran while one was open for 2% of the time, Pallas kernels for 18%

profile of v7, /device:TPU:0, one launch (start us, length us, event | category | flops | bytes accessed | tf_op | source)
XLA Modules:
  0.0 27.3 jit_solution(17836196319374041151)
XLA Ops:
  0.0 1.0 %open.1.refs_0_ = bf16[64,128]{1,0:T(8,128)(2,1)S(1)} custom-call(bf16[32,4,128]{2,1,0:T(4,128)(2,1)} %key_hbm.1, bf16[32,4,128]{2,1,0:T(4,128)(2,1)} %value_hbm.1), custom_call_target="tpu_custom_call" | custom-call | tf_op jit(solution)/shard_map/open/pallas_call | solution.py:60
  1.0 3.1 %collective-permute-start = (bf16[64,128]{1,0:T(8,128)(2,1)S(1)}, bf16[64,128]{1,0:T(8,128)(2,1)S(1)}, u32[]{:S(2)}, u32[]{:S(2)}) collective-permute-start(bf16[64,128]{1,0:T(8,128)(2,1)S(1)} %open.1.refs_0_), channel_id=1, source_target_pairs={{0,8},{1,25},{8,0},{9,17},{16,24},{17,9},{24,16},{25,1},{2,10},{3,... | collective-permute-start | bytes 49160 | tf_op jit(solution)/shard_map/ppermute | solution.py:32
  4.1 2.6 %collective-permute-start.2 = (bf16[64,128]{1,0:T(8,128)(2,1)S(1)}, bf16[64,128]{1,0:T(8,128)(2,1)S(1)}, u32[]{:S(2)}, u32[]{:S(2)}) collective-permute-start(bf16[64,128]{1,0:T(8,128)(2,1)S(1)} %open.1.refs_0_), channel_id=1, source_target_pairs={{0,16},{1,17},{8,24},{9,25},{16,0},{17,1},{24,8},{25,9},{2,18},{3,... | collective-permute-start | bytes 49160 | tf_op jit(solution)/shard_map/ppermute | solution.py:32
  6.7 0.0 collective-permute-done.refs_1_
  6.7 0.1 collective-permute-start.1
  6.8 0.4 %collective-permute-start.6 = (bf16[192,4096]{1,0:T(8,128)(2,1)}, bf16[192,4096]{1,0:T(8,128)(2,1)S(1)}, u32[]{:S(2)}, u32[]{:S(2)}) collective-permute-start(bf16[192,4096]{1,0:T(8,128)(2,1)} %bitcast.12), channel_id=1, source_target_pairs={{0,1},{1,0},{2,3},{3,2},{4,5},{5,4},{6,7},{7,6},{8,9},{9,8},{10,11... | collective-permute-start | bytes 4718600 | tf_op jit(solution)/shard_map/ppermute | solution.py:22
  7.2 0.1 collective-permute-start.7
  7.4 0.4 %collective-permute-start.8 = (bf16[192,4096]{1,0:T(8,128)(2,1)}, bf16[192,4096]{1,0:T(8,128)(2,1)S(1)}, u32[]{:S(2)}, u32[]{:S(2)}) collective-permute-start(bf16[192,4096]{1,0:T(8,128)(2,1)} %bitcast.16), channel_id=1, source_target_pairs={{0,1},{1,0},{2,3},{3,2},{4,5},{5,4},{6,7},{7,6},{8,9},{9,8},{10,11... | collective-permute-start | bytes 4718600 | tf_op jit(solution)/shard_map/ppermute | solution.py:22
  7.8 0.8 %route.1 = (bf16[32,128]{1,0:T(8,128)(2,1)S(1)}, bf16[16,128]{1,0:T(8,128)(2,1)S(1)}, f32[4,128]{1,0:T(4,128)S(1)}, f32[32,128]{1,0:T(8,128)S(1)}) custom-call(bf16[16,2,128]{2,1,0:T(2,128)(2,1)} %bitcast.18, s32[4,8]{1,0:T(4,128)} %refs_1_, f32[4,8]{1,0:T(4,128)} %refs_2_), custom_call_target="tpu_custom_call" | custom-call | tf_op jit(solution)/shard_map/route/pallas_call | solution.py:60
  8.6 0.2 collective-permute-done.2.refs_3_
  8.9 0.0 collective-permute-done.1.refs_2_
  8.9 0.3 %attend.1 = bf16[16,256]{1,0:T(8,128)(2,1)S(1)} custom-call(bf16[32,128]{1,0:T(8,128)(2,1)S(1)} %get-tuple-element.31.q_ref, f32[32,128]{1,0:T(8,128)S(1)} %get-tuple-element.32.allowed_ref, bf16[64,128]{1,0:T(8,128)(2,1)S(1)} %open.1.refs_0_, bf16[64,128]{1,0:T(8,128)(2,1)S(1)} %collective-permute-done.refs_1_, ...), custom_call_target="tpu_custom_call" | custom-call | flops 10000000000 | tf_op jit(solution)/shard_map/attend/pallas_call | solution.py:60
  9.2 0.4 %convolution_convert_fusion = bf16[16,4096]{1,0:T(8,128)(2,1)S(1)} fusion(bf16[16,256]{1,0:T(8,128)(2,1)S(1)} %attend.1, bf16[256,4096]{1,0:T(8,128)(2,1)S(1)} %copy-done), kind=kOutput, calls=%fused_computation | convolution fusion | flops 33619968 | bytes 2236416 | tf_op jit(solution)/shard_map/dot_general | solution.py:303
  9.6 1.6 %collective-permute-start.5 = (bf16[16,4224]{1,0:T(8,128)(2,1)S(1)}, bf16[16,4224]{1,0:T(8,128)(2,1)S(1)}, u32[]{:S(2)}, u32[]{:S(2)}) collective-permute-start(bf16[16,4224]{1,0:T(8,128)(2,1)S(1)} %pad_maximum_fusion.refs_3_), channel_id=1, source_target_pairs={{0,4},{1,3},{2,6},{3,1},{4,0},{5,7},{6,2},{7,5},{8,12},{9,11},{10,... | collective-permute-start | bytes 405512 | tf_op jit(solution)/shard_map/ppermute | solution.py:32
  11.2 1.5 %collective-permute-start.4 = (bf16[16,4224]{1,0:T(8,128)(2,1)S(1)}, bf16[16,4224]{1,0:T(8,128)(2,1)S(1)}, u32[]{:S(2)}, u32[]{:S(2)}) collective-permute-start(bf16[16,4224]{1,0:T(8,128)(2,1)S(1)} %pad_maximum_fusion.refs_3_), channel_id=1, source_target_pairs={{0,2},{1,5},{2,0},{3,7},{4,6},{5,1},{6,4},{7,3},{8,10},{9,13},{10,... | collective-permute-start | bytes 405512 | tf_op jit(solution)/shard_map/ppermute | solution.py:32
  12.7 0.5 %collective-permute-start.3 = (bf16[16,4224]{1,0:T(8,128)(2,1)S(1)}, bf16[16,4224]{1,0:T(8,128)(2,1)S(1)}, u32[]{:S(2)}, u32[]{:S(2)}) collective-permute-start(bf16[16,4224]{1,0:T(8,128)(2,1)S(1)} %pad_maximum_fusion.refs_3_), channel_id=1, source_target_pairs={{0,6},{1,7},{2,4},{3,5},{4,2},{5,3},{6,0},{7,1},{8,14},{9,15},{10,... | collective-permute-start | bytes 405512 | tf_op jit(solution)/shard_map/ppermute | solution.py:32
  13.2 2.8 %load.1 = (bf16[4096,384]{1,0:T(8,128)(2,1)S(1)}, bf16[192,4096]{1,0:T(8,128)(2,1)S(1)}) custom-call(bf16[192,4096]{1,0:T(8,128)(2,1)} %bitcast.13, bf16[192,4096]{1,0:T(8,128)(2,1)} %bitcast.15, bf16[192,4096]{1,0:T(8,128)(2,1)} %bitcast.17), custom_call_target="tpu_custom_call" | custom-call | bytes 4718592 | tf_op jit(solution)/shard_map/load/pallas_call | solution.py:60
  16.0 0.0 copy-start.1
  16.0 0.9 %turn.1.refs_7_ = bf16[4096,384]{1,0:T(8,128)(2,1)S(1)} custom-call(bf16[192,4096]{1,0:T(8,128)(2,1)S(1)} %collective-permute-done.6.gate_ref, bf16[192,4096]{1,0:T(8,128)(2,1)S(1)} %collective-permute-done.7.up_ref), custom_call_target="tpu_custom_call" | custom-call | bytes 3145728 | tf_op jit(solution)/shard_map/turn/pallas_call | solution.py:60
  16.9 0.0 collective-permute-done.5.refs_2_
  16.9 0.5 %collective-permute-done.4.refs_1_ = bf16[16,4224]{1,0:T(8,128)(2,1)S(1)} collective-permute-done((bf16[16,4224]{1,0:T(8,128)(2,1)S(1)}, bf16[16,4224]{1,0:T(8,128)(2,1)S(1)}, u32[]{:S(2)}, u32[]{:S(2)}) %collective-permute-start.4) | collective-permute-done | bytes 135200 | tf_op jit(solution)/shard_map/ppermute | solution.py:32
  17.4 2.0 %collective-permute-done.3.refs_0_ = bf16[16,4224]{1,0:T(8,128)(2,1)S(1)} collective-permute-done((bf16[16,4224]{1,0:T(8,128)(2,1)S(1)}, bf16[16,4224]{1,0:T(8,128)(2,1)S(1)}, u32[]{:S(2)}, u32[]{:S(2)}) %collective-permute-start.3) | collective-permute-done | bytes 135200 | tf_op jit(solution)/shard_map/ppermute | solution.py:32
  19.4 0.0 collective-permute-done.8.refs_8_
  19.4 1.7 %experts.1 = (f32[4,4096]{1,0:T(4,128)S(1)}, bf16[2,4096]{1,0:T(2,128)(2,1)S(1)}, bf16[2,4096]{1,0:T(2,128)(2,1)S(1)}, bf16[2,4096]{1,0:T(2,128)(2,1)S(1)}, bf16[2,4096]{1,0:T(2,128)(2,1)S(1)}) custom-call(bf16[16,4224]{1,0:T(8,128)(2,1)S(1)} %collective-permute-done.3.refs_0_, bf16[16,4224]{1,0:T(8,128)(2,1)S(1)} %collective-permute-done.4.refs_1_, ...), custom_call_target="tpu_custom_call" | custom-call | flops 75497472 | bytes 9437184 | tf_op jit(solution)/shard_map/experts/pallas_call | solution.py:60
  21.1 0.1 collective-permute-start.9
  21.2 1.6 %collective-permute-start.11 = (bf16[2,4096]{1,0:T(2,128)(2,1)S(1)}, bf16[2,4096]{1,0:T(2,128)(2,1)S(1)}, u32[]{:S(2)}, u32[]{:S(2)}) collective-permute-start(bf16[2,4096]{1,0:T(2,128)(2,1)S(1)} %get-tuple-element.47), channel_id=1, source_target_pairs={{0,2},{1,5},{2,0},{3,7},{4,6},{5,1},{6,4},{7,3},{8,10},{9,13},{10,... | collective-permute-start | bytes 49160 | tf_op jit(solution)/shard_map/ppermute | solution.py:32
  22.8 0.9 %collective-permute-start.12 = (bf16[2,4096]{1,0:T(2,128)(2,1)S(1)}, bf16[2,4096]{1,0:T(2,128)(2,1)S(1)}, u32[]{:S(2)}, u32[]{:S(2)}) collective-permute-start(bf16[2,4096]{1,0:T(2,128)(2,1)S(1)} %get-tuple-element.48), channel_id=1, source_target_pairs={{0,4},{1,3},{2,6},{3,1},{4,0},{5,7},{6,2},{7,5},{8,12},{9,11},{10,... | collective-permute-start | bytes 49160 | tf_op jit(solution)/shard_map/ppermute | solution.py:32
  23.7 1.6 %collective-permute-done.9 = bf16[2,4096]{1,0:T(2,128)(2,1)S(1)} collective-permute-done((bf16[2,4096]{1,0:T(2,128)(2,1)S(1)}, bf16[2,4096]{1,0:T(2,128)(2,1)S(1)}, u32[]{:S(2)}, u32[]{:S(2)}) %collective-permute-start.9) | collective-permute-done | bytes 16416 | tf_op jit(solution)/shard_map/ppermute | solution.py:32
  25.3 0.0 collective-permute-done.11.refs_2_
  25.3 1.2 %collective-permute-done.12.refs_3_ = bf16[2,4096]{1,0:T(2,128)(2,1)S(1)} collective-permute-done((bf16[2,4096]{1,0:T(2,128)(2,1)S(1)}, bf16[2,4096]{1,0:T(2,128)(2,1)S(1)}, u32[]{:S(2)}, u32[]{:S(2)}) %collective-permute-start.12) | collective-permute-done | bytes 16416 | tf_op jit(solution)/shard_map/ppermute | solution.py:32
  26.5 0.0 collective-permute-done.10.refs_1_
  26.5 0.8 %combine.1 = bf16[4,4096]{1,0:T(4,128)(2,1)} custom-call(f32[4,128]{1,0:T(4,128)S(1)} %get-tuple-element.30.mix_ref, f32[4,4096]{1,0:T(4,128)S(1)} %get-tuple-element.44.own_ref, bf16[2,4096]{1,0:T(2,128)(2,1)S(1)} %get-tuple-element.45.refs_0_, bf16[2,4096]{1,0:T(2,128)(2,1)S(1)} %collective-permute-done.10.refs_1_, ...), custom_call_target="tpu_custom_call" | custom-call | tf_op jit(solution)/shard_map/combine/pallas_call | solution.py:60
  (7 shorter events, 0.0 us)
Async XLA Ops:
  0.0 9.2 %copy-start = (bf16[256,4096]{1,0:T(8,128)(2,1)S(1)}, bf16[256,4096]{1,0:T(8,128)(2,1)}, u32[]{:S(2)}) copy-start(bf16[256,4096]{1,0:T(8,128)(2,1)} %param.13) | copy-start | bytes 6291460
  1.0 5.7 %collective-permute-start = (bf16[64,128]{1,0:T(8,128)(2,1)S(1)}, bf16[64,128]{1,0:T(8,128)(2,1)S(1)}, u32[]{:S(2)}, u32[]{:S(2)}) collective-permute-start(bf16[64,128]{1,0:T(8,128)(2,1)S(1)} %open.1.refs_0_), channel_id=1, source_target_pairs={{0,8},{1,25},{8,0},{9,17},{16,24},{17,9},{24,16},{25,1},{2,10},{3,... | collective-permute-start | bytes 49160 | tf_op jit(solution)/shard_map/ppermute | solution.py:32
  4.1 4.7 %collective-permute-start.2 = (bf16[64,128]{1,0:T(8,128)(2,1)S(1)}, bf16[64,128]{1,0:T(8,128)(2,1)S(1)}, u32[]{:S(2)}, u32[]{:S(2)}) collective-permute-start(bf16[64,128]{1,0:T(8,128)(2,1)S(1)} %open.1.refs_0_), channel_id=1, source_target_pairs={{0,16},{1,17},{8,24},{9,25},{16,0},{17,1},{24,8},{25,9},{2,18},{3,... | collective-permute-start | bytes 49160 | tf_op jit(solution)/shard_map/ppermute | solution.py:32
  6.7 2.1 %collective-permute-start.1 = (bf16[64,128]{1,0:T(8,128)(2,1)S(1)}, bf16[64,128]{1,0:T(8,128)(2,1)S(1)}, u32[]{:S(2)}, u32[]{:S(2)}) collective-permute-start(bf16[64,128]{1,0:T(8,128)(2,1)S(1)} %collective-permute-done.refs_1_), channel_id=1, source_target_pairs={{0,1},{1,0},{2,3},{3,2},{4,5},{5,4},{6,7},{7,6},{8,9},{9,8},{10,11... | collective-permute-start | bytes 49160 | tf_op jit(solution)/shard_map/ppermute | solution.py:22
  6.8 5.9 %collective-permute-start.6 = (bf16[192,4096]{1,0:T(8,128)(2,1)}, bf16[192,4096]{1,0:T(8,128)(2,1)S(1)}, u32[]{:S(2)}, u32[]{:S(2)}) collective-permute-start(bf16[192,4096]{1,0:T(8,128)(2,1)} %bitcast.12), channel_id=1, source_target_pairs={{0,1},{1,0},{2,3},{3,2},{4,5},{5,4},{6,7},{7,6},{8,9},{9,8},{10,11... | collective-permute-start | bytes 4718600 | tf_op jit(solution)/shard_map/ppermute | solution.py:22
  7.2 8.7 %collective-permute-start.7 = (bf16[192,4096]{1,0:T(8,128)(2,1)}, bf16[192,4096]{1,0:T(8,128)(2,1)S(1)}, u32[]{:S(2)}, u32[]{:S(2)}) collective-permute-start(bf16[192,4096]{1,0:T(8,128)(2,1)} %bitcast.14), channel_id=1, source_target_pairs={{0,1},{1,0},{2,3},{3,2},{4,5},{5,4},{6,7},{7,6},{8,9},{9,8},{10,11... | collective-permute-start | bytes 4718600 | tf_op jit(solution)/shard_map/ppermute | solution.py:22
  7.4 12.0 %collective-permute-start.8 = (bf16[192,4096]{1,0:T(8,128)(2,1)}, bf16[192,4096]{1,0:T(8,128)(2,1)S(1)}, u32[]{:S(2)}, u32[]{:S(2)}) collective-permute-start(bf16[192,4096]{1,0:T(8,128)(2,1)} %bitcast.16), channel_id=1, source_target_pairs={{0,1},{1,0},{2,3},{3,2},{4,5},{5,4},{6,7},{7,6},{8,9},{9,8},{10,11... | collective-permute-start | bytes 4718600 | tf_op jit(solution)/shard_map/ppermute | solution.py:22
  9.6 7.2 %collective-permute-start.5 = (bf16[16,4224]{1,0:T(8,128)(2,1)S(1)}, bf16[16,4224]{1,0:T(8,128)(2,1)S(1)}, u32[]{:S(2)}, u32[]{:S(2)}) collective-permute-start(bf16[16,4224]{1,0:T(8,128)(2,1)S(1)} %pad_maximum_fusion.refs_3_), channel_id=1, source_target_pairs={{0,4},{1,3},{2,6},{3,1},{4,0},{5,7},{6,2},{7,5},{8,12},{9,11},{10,... | collective-permute-start | bytes 405512 | tf_op jit(solution)/shard_map/ppermute | solution.py:32
  11.2 6.2 %collective-permute-start.4 = (bf16[16,4224]{1,0:T(8,128)(2,1)S(1)}, bf16[16,4224]{1,0:T(8,128)(2,1)S(1)}, u32[]{:S(2)}, u32[]{:S(2)}) collective-permute-start(bf16[16,4224]{1,0:T(8,128)(2,1)S(1)} %pad_maximum_fusion.refs_3_), channel_id=1, source_target_pairs={{0,2},{1,5},{2,0},{3,7},{4,6},{5,1},{6,4},{7,3},{8,10},{9,13},{10,... | collective-permute-start | bytes 405512 | tf_op jit(solution)/shard_map/ppermute | solution.py:32
  12.7 6.7 %collective-permute-start.3 = (bf16[16,4224]{1,0:T(8,128)(2,1)S(1)}, bf16[16,4224]{1,0:T(8,128)(2,1)S(1)}, u32[]{:S(2)}, u32[]{:S(2)}) collective-permute-start(bf16[16,4224]{1,0:T(8,128)(2,1)S(1)} %pad_maximum_fusion.refs_3_), channel_id=1, source_target_pairs={{0,6},{1,7},{2,4},{3,5},{4,2},{5,3},{6,0},{7,1},{8,14},{9,15},{10,... | collective-permute-start | bytes 405512 | tf_op jit(solution)/shard_map/ppermute | solution.py:32
  16.0 3.4 %copy-start.1 = (f32[4096]{0:T(1024)S(1)}, f32[4096]{0:T(1024)}, u32[]{:S(2)}) copy-start(f32[4096]{0:T(1024)} %param.14) | copy-start | bytes 49156
  21.1 4.1 %collective-permute-start.9 = (bf16[2,4096]{1,0:T(2,128)(2,1)S(1)}, bf16[2,4096]{1,0:T(2,128)(2,1)S(1)}, u32[]{:S(2)}, u32[]{:S(2)}) collective-permute-start(bf16[2,4096]{1,0:T(2,128)(2,1)S(1)} %get-tuple-element.46), channel_id=1, source_target_pairs={{0,7},{1,6},{2,5},{3,4},{4,3},{5,2},{6,1},{7,0},{8,15},{9,14},{10,... | collective-permute-start | bytes 49160 | tf_op jit(solution)/shard_map/ppermute | solution.py:32
  21.2 4.1 %collective-permute-start.11 = (bf16[2,4096]{1,0:T(2,128)(2,1)S(1)}, bf16[2,4096]{1,0:T(2,128)(2,1)S(1)}, u32[]{:S(2)}, u32[]{:S(2)}) collective-permute-start(bf16[2,4096]{1,0:T(2,128)(2,1)S(1)} %get-tuple-element.47), channel_id=1, source_target_pairs={{0,2},{1,5},{2,0},{3,7},{4,6},{5,1},{6,4},{7,3},{8,10},{9,13},{10,... | collective-permute-start | bytes 49160 | tf_op jit(solution)/shard_map/ppermute | solution.py:32
  22.8 3.7 %collective-permute-start.12 = (bf16[2,4096]{1,0:T(2,128)(2,1)S(1)}, bf16[2,4096]{1,0:T(2,128)(2,1)S(1)}, u32[]{:S(2)}, u32[]{:S(2)}) collective-permute-start(bf16[2,4096]{1,0:T(2,128)(2,1)S(1)} %get-tuple-element.48), channel_id=1, source_target_pairs={{0,4},{1,3},{2,6},{3,1},{4,0},{5,7},{6,2},{7,5},{8,12},{9,11},{10,... | collective-permute-start | bytes 49160 | tf_op jit(solution)/shard_map/ppermute | solution.py:32
  25.3 1.3 %collective-permute-start.10 = (bf16[2,4096]{1,0:T(2,128)(2,1)S(1)}, bf16[2,4096]{1,0:T(2,128)(2,1)S(1)}, u32[]{:S(2)}, u32[]{:S(2)}) collective-permute-start(bf16[2,4096]{1,0:T(2,128)(2,1)S(1)} %collective-permute-done.9), channel_id=1, source_target_pairs={{0,1},{1,0},{2,3},{3,2},{4,5},{5,4},{6,7},{7,6},{8,9},{9,8},{10,11... | collective-permute-start | bytes 49160 | tf_op jit(solution)/shard_map/ppermute | solution.py:22

commit v8 on v7

--- a/solution.py
+++ b/solution.py
@@ -35,7 +35,7 @@
 def by_distance(size):
     bits = size.bit_length() - 1
     mirror = [sum((m >> i & 1) << (bits - 1 - i) for i in range(bits)) for m in range(size)]
-    far_first = sorted(range(1, size), key=lambda m: -m.bit_count())
+    far_first = sorted(range(1, size), key=lambda m: (-m.bit_count(), -m))
     return [(0, 0)] + [(m, mirror[m]) for m in far_first]
 
 

time: 27.6 us -> 27.5 us (level)
  no operation moved by 1% of the time
where the time goes in v8:
time: 27.5 us; the launch traced here: 27.3 us
  starting transfers between devices  12.8 us (47%)
  Pallas kernels  8.43 us (31%)
  waiting for transfers between devices  5.54 us (20%)
  matrix products  0.4 us (1%)
    ppermute x8, starting transfers between devices, swap_by_core(): return lax.ppermute(x, (axis, 'tp'), pairs)  11.8 us
    pallas_call x7, Pallas kernels, call(): pl.pallas_call(kernel, out_shape=[kept(shape, dtype) for shape, dtype in...  8.43 us
    ppermute x8, waiting for transfers between devices, swap_by_core(): return lax.ppermute(x, (axis, 'tp'), pairs)  5.52 us
    ppermute x5, starting transfers between devices, swap(): return lax.ppermute(x, axis, [(i, i ^ mask) for i in range(size)])  1.02 us
  transfers between devices with their start and end apart: 13, of which 5 were waited for; matrix products, arithmetic and copies ran while one was open for 2% of the time, Pallas kernels for 18%

profile of v8, /device:TPU:0, one launch (start us, length us, event | category | flops | bytes accessed | tf_op | source)
XLA Modules:
  0.0 27.3 jit_solution(183638152785265207)
XLA Ops:
  0.0 1.0 %open.1.refs_0_ = bf16[64,128]{1,0:T(8,128)(2,1)S(1)} custom-call(bf16[32,4,128]{2,1,0:T(4,128)(2,1)} %key_hbm.1, bf16[32,4,128]{2,1,0:T(4,128)(2,1)} %value_hbm.1), custom_call_target="tpu_custom_call" | custom-call | tf_op jit(solution)/shard_map/open/pallas_call | solution.py:60
  1.0 3.1 %collective-permute-start = (bf16[64,128]{1,0:T(8,128)(2,1)S(1)}, bf16[64,128]{1,0:T(8,128)(2,1)S(1)}, u32[]{:S(2)}, u32[]{:S(2)}) collective-permute-start(bf16[64,128]{1,0:T(8,128)(2,1)S(1)} %open.1.refs_0_), channel_id=1, source_target_pairs={{0,8},{1,25},{8,0},{9,17},{16,24},{17,9},{24,16},{25,1},{2,10},{3,... | collective-permute-start | bytes 49160 | tf_op jit(solution)/shard_map/ppermute | solution.py:32
  4.1 2.6 %collective-permute-start.2 = (bf16[64,128]{1,0:T(8,128)(2,1)S(1)}, bf16[64,128]{1,0:T(8,128)(2,1)S(1)}, u32[]{:S(2)}, u32[]{:S(2)}) collective-permute-start(bf16[64,128]{1,0:T(8,128)(2,1)S(1)} %open.1.refs_0_), channel_id=1, source_target_pairs={{0,16},{1,17},{8,24},{9,25},{16,0},{17,1},{24,8},{25,9},{2,18},{3,... | collective-permute-start | bytes 49160 | tf_op jit(solution)/shard_map/ppermute | solution.py:32
  6.7 0.0 collective-permute-done.refs_1_
  6.7 0.1 collective-permute-start.1
  6.8 0.4 %collective-permute-start.6 = (bf16[192,4096]{1,0:T(8,128)(2,1)}, bf16[192,4096]{1,0:T(8,128)(2,1)S(1)}, u32[]{:S(2)}, u32[]{:S(2)}) collective-permute-start(bf16[192,4096]{1,0:T(8,128)(2,1)} %bitcast.12), channel_id=1, source_target_pairs={{0,1},{1,0},{2,3},{3,2},{4,5},{5,4},{6,7},{7,6},{8,9},{9,8},{10,11... | collective-permute-start | bytes 4718600 | tf_op jit(solution)/shard_map/ppermute | solution.py:22
  7.2 0.1 collective-permute-start.7
  7.4 0.4 %collective-permute-start.8 = (bf16[192,4096]{1,0:T(8,128)(2,1)}, bf16[192,4096]{1,0:T(8,128)(2,1)S(1)}, u32[]{:S(2)}, u32[]{:S(2)}) collective-permute-start(bf16[192,4096]{1,0:T(8,128)(2,1)} %bitcast.16), channel_id=1, source_target_pairs={{0,1},{1,0},{2,3},{3,2},{4,5},{5,4},{6,7},{7,6},{8,9},{9,8},{10,11... | collective-permute-start | bytes 4718600 | tf_op jit(solution)/shard_map/ppermute | solution.py:22
  7.8 0.8 %route.1 = (bf16[32,128]{1,0:T(8,128)(2,1)S(1)}, bf16[16,128]{1,0:T(8,128)(2,1)S(1)}, f32[4,128]{1,0:T(4,128)S(1)}, f32[32,128]{1,0:T(8,128)S(1)}) custom-call(bf16[16,2,128]{2,1,0:T(2,128)(2,1)} %bitcast.18, s32[4,8]{1,0:T(4,128)} %refs_1_, f32[4,8]{1,0:T(4,128)} %refs_2_), custom_call_target="tpu_custom_call" | custom-call | tf_op jit(solution)/shard_map/route/pallas_call | solution.py:60
  8.6 0.2 collective-permute-done.2.refs_3_
  8.9 0.0 collective-permute-done.1.refs_2_
  8.9 0.3 %attend.1 = bf16[16,256]{1,0:T(8,128)(2,1)S(1)} custom-call(bf16[32,128]{1,0:T(8,128)(2,1)S(1)} %get-tuple-element.31.q_ref, f32[32,128]{1,0:T(8,128)S(1)} %get-tuple-element.32.allowed_ref, bf16[64,128]{1,0:T(8,128)(2,1)S(1)} %open.1.refs_0_, bf16[64,128]{1,0:T(8,128)(2,1)S(1)} %collective-permute-done.refs_1_, ...), custom_call_target="tpu_custom_call" | custom-call | flops 10000000000 | tf_op jit(solution)/shard_map/attend/pallas_call | solution.py:60
  9.2 0.4 %convolution_convert_fusion = bf16[16,4096]{1,0:T(8,128)(2,1)S(1)} fusion(bf16[16,256]{1,0:T(8,128)(2,1)S(1)} %attend.1, bf16[256,4096]{1,0:T(8,128)(2,1)S(1)} %copy-done), kind=kOutput, calls=%fused_computation | convolution fusion | flops 33619968 | bytes 2236416 | tf_op jit(solution)/shard_map/dot_general | solution.py:303
  9.6 1.6 %collective-permute-start.5 = (bf16[16,4224]{1,0:T(8,128)(2,1)S(1)}, bf16[16,4224]{1,0:T(8,128)(2,1)S(1)}, u32[]{:S(2)}, u32[]{:S(2)}) collective-permute-start(bf16[16,4224]{1,0:T(8,128)(2,1)S(1)} %pad_maximum_fusion.refs_3_), channel_id=1, source_target_pairs={{0,4},{1,3},{2,6},{3,1},{4,0},{5,7},{6,2},{7,5},{8,12},{9,11},{10,... | collective-permute-start | bytes 405512 | tf_op jit(solution)/shard_map/ppermute | solution.py:32
  11.2 1.5 %collective-permute-start.4 = (bf16[16,4224]{1,0:T(8,128)(2,1)S(1)}, bf16[16,4224]{1,0:T(8,128)(2,1)S(1)}, u32[]{:S(2)}, u32[]{:S(2)}) collective-permute-start(bf16[16,4224]{1,0:T(8,128)(2,1)S(1)} %pad_maximum_fusion.refs_3_), channel_id=1, source_target_pairs={{0,2},{1,5},{2,0},{3,7},{4,6},{5,1},{6,4},{7,3},{8,10},{9,13},{10,... | collective-permute-start | bytes 405512 | tf_op jit(solution)/shard_map/ppermute | solution.py:32
  12.7 0.0 collective-permute-done.6.gate_ref
  12.7 0.5 %collective-permute-start.3 = (bf16[16,4224]{1,0:T(8,128)(2,1)S(1)}, bf16[16,4224]{1,0:T(8,128)(2,1)S(1)}, u32[]{:S(2)}, u32[]{:S(2)}) collective-permute-start(bf16[16,4224]{1,0:T(8,128)(2,1)S(1)} %pad_maximum_fusion.refs_3_), channel_id=1, source_target_pairs={{0,6},{1,7},{2,4},{3,5},{4,2},{5,3},{6,0},{7,1},{8,14},{9,15},{10,... | collective-permute-start | bytes 405512 | tf_op jit(solution)/shard_map/ppermute | solution.py:32
  13.2 2.8 %load.1 = (bf16[4096,384]{1,0:T(8,128)(2,1)S(1)}, bf16[192,4096]{1,0:T(8,128)(2,1)S(1)}) custom-call(bf16[192,4096]{1,0:T(8,128)(2,1)} %bitcast.13, bf16[192,4096]{1,0:T(8,128)(2,1)} %bitcast.15, bf16[192,4096]{1,0:T(8,128)(2,1)} %bitcast.17), custom_call_target="tpu_custom_call" | custom-call | bytes 4718592 | tf_op jit(solution)/shard_map/load/pallas_call | solution.py:60
  16.0 0.0 copy-start.1
  16.0 0.0 collective-permute-done.7.up_ref
  16.0 0.9 %turn.1.refs_7_ = bf16[4096,384]{1,0:T(8,128)(2,1)S(1)} custom-call(bf16[192,4096]{1,0:T(8,128)(2,1)S(1)} %collective-permute-done.6.gate_ref, bf16[192,4096]{1,0:T(8,128)(2,1)S(1)} %collective-permute-done.7.up_ref), custom_call_target="tpu_custom_call" | custom-call | bytes 3145728 | tf_op jit(solution)/shard_map/turn/pallas_call | solution.py:60
  16.9 0.5 %collective-permute-done.4.refs_1_ = bf16[16,4224]{1,0:T(8,128)(2,1)S(1)} collective-permute-done((bf16[16,4224]{1,0:T(8,128)(2,1)S(1)}, bf16[16,4224]{1,0:T(8,128)(2,1)S(1)}, u32[]{:S(2)}, u32[]{:S(2)}) %collective-permute-start.4) | collective-permute-done | bytes 135200 | tf_op jit(solution)/shard_map/ppermute | solution.py:32
  17.4 2.0 %collective-permute-done.3.refs_0_ = bf16[16,4224]{1,0:T(8,128)(2,1)S(1)} collective-permute-done((bf16[16,4224]{1,0:T(8,128)(2,1)S(1)}, bf16[16,4224]{1,0:T(8,128)(2,1)S(1)}, u32[]{:S(2)}, u32[]{:S(2)}) %collective-permute-start.3) | collective-permute-done | bytes 135200 | tf_op jit(solution)/shard_map/ppermute | solution.py:32
  19.4 0.0 collective-permute-done.8.refs_8_
  19.4 1.7 %experts.1 = (f32[4,4096]{1,0:T(4,128)S(1)}, bf16[2,4096]{1,0:T(2,128)(2,1)S(1)}, bf16[2,4096]{1,0:T(2,128)(2,1)S(1)}, bf16[2,4096]{1,0:T(2,128)(2,1)S(1)}, bf16[2,4096]{1,0:T(2,128)(2,1)S(1)}) custom-call(bf16[16,4224]{1,0:T(8,128)(2,1)S(1)} %collective-permute-done.3.refs_0_, bf16[16,4224]{1,0:T(8,128)(2,1)S(1)} %collective-permute-done.4.refs_1_, ...), custom_call_target="tpu_custom_call" | custom-call | flops 75497472 | bytes 9437184 | tf_op jit(solution)/shard_map/experts/pallas_call | solution.py:60
  21.1 0.1 collective-permute-start.9
  21.2 1.5 %collective-permute-start.11 = (bf16[2,4096]{1,0:T(2,128)(2,1)S(1)}, bf16[2,4096]{1,0:T(2,128)(2,1)S(1)}, u32[]{:S(2)}, u32[]{:S(2)}) collective-permute-start(bf16[2,4096]{1,0:T(2,128)(2,1)S(1)} %get-tuple-element.47), channel_id=1, source_target_pairs={{0,4},{1,3},{2,6},{3,1},{4,0},{5,7},{6,2},{7,5},{8,12},{9,11},{10,... | collective-permute-start | bytes 49160 | tf_op jit(solution)/shard_map/ppermute | solution.py:32
  22.7 1.0 %collective-permute-start.12 = (bf16[2,4096]{1,0:T(2,128)(2,1)S(1)}, bf16[2,4096]{1,0:T(2,128)(2,1)S(1)}, u32[]{:S(2)}, u32[]{:S(2)}) collective-permute-start(bf16[2,4096]{1,0:T(2,128)(2,1)S(1)} %get-tuple-element.48), channel_id=1, source_target_pairs={{0,2},{1,5},{2,0},{3,7},{4,6},{5,1},{6,4},{7,3},{8,10},{9,13},{10,... | collective-permute-start | bytes 49160 | tf_op jit(solution)/shard_map/ppermute | solution.py:32
  23.7 1.6 %collective-permute-done.9 = bf16[2,4096]{1,0:T(2,128)(2,1)S(1)} collective-permute-done((bf16[2,4096]{1,0:T(2,128)(2,1)S(1)}, bf16[2,4096]{1,0:T(2,128)(2,1)S(1)}, u32[]{:S(2)}, u32[]{:S(2)}) %collective-permute-start.9) | collective-permute-done | bytes 16416 | tf_op jit(solution)/shard_map/ppermute | solution.py:32
  25.3 1.2 %collective-permute-done.12.refs_3_ = bf16[2,4096]{1,0:T(2,128)(2,1)S(1)} collective-permute-done((bf16[2,4096]{1,0:T(2,128)(2,1)S(1)}, bf16[2,4096]{1,0:T(2,128)(2,1)S(1)}, u32[]{:S(2)}, u32[]{:S(2)}) %collective-permute-start.12) | collective-permute-done | bytes 16416 | tf_op jit(solution)/shard_map/ppermute | solution.py:32
  26.5 0.0 collective-permute-done.10.refs_1_
  26.5 0.8 %combine.1 = bf16[4,4096]{1,0:T(4,128)(2,1)} custom-call(f32[4,128]{1,0:T(4,128)S(1)} %get-tuple-element.30.mix_ref, f32[4,4096]{1,0:T(4,128)S(1)} %get-tuple-element.44.own_ref, bf16[2,4096]{1,0:T(2,128)(2,1)S(1)} %get-tuple-element.45.refs_0_, bf16[2,4096]{1,0:T(2,128)(2,1)S(1)} %collective-permute-done.10.refs_1_, ...), custom_call_target="tpu_custom_call" | custom-call | tf_op jit(solution)/shard_map/combine/pallas_call | solution.py:60
  (7 shorter events, 0.0 us)
Async XLA Ops:
  0.0 9.2 %copy-start = (bf16[256,4096]{1,0:T(8,128)(2,1)S(1)}, bf16[256,4096]{1,0:T(8,128)(2,1)}, u32[]{:S(2)}) copy-start(bf16[256,4096]{1,0:T(8,128)(2,1)} %param.13) | copy-start | bytes 6291460
  1.0 5.7 %collective-permute-start = (bf16[64,128]{1,0:T(8,128)(2,1)S(1)}, bf16[64,128]{1,0:T(8,128)(2,1)S(1)}, u32[]{:S(2)}, u32[]{:S(2)}) collective-permute-start(bf16[64,128]{1,0:T(8,128)(2,1)S(1)} %open.1.refs_0_), channel_id=1, source_target_pairs={{0,8},{1,25},{8,0},{9,17},{16,24},{17,9},{24,16},{25,1},{2,10},{3,... | collective-permute-start | bytes 49160 | tf_op jit(solution)/shard_map/ppermute | solution.py:32
  4.1 4.7 %collective-permute-start.2 = (bf16[64,128]{1,0:T(8,128)(2,1)S(1)}, bf16[64,128]{1,0:T(8,128)(2,1)S(1)}, u32[]{:S(2)}, u32[]{:S(2)}) collective-permute-start(bf16[64,128]{1,0:T(8,128)(2,1)S(1)} %open.1.refs_0_), channel_id=1, source_target_pairs={{0,16},{1,17},{8,24},{9,25},{16,0},{17,1},{24,8},{25,9},{2,18},{3,... | collective-permute-start | bytes 49160 | tf_op jit(solution)/shard_map/ppermute | solution.py:32
  6.7 2.1 %collective-permute-start.1 = (bf16[64,128]{1,0:T(8,128)(2,1)S(1)}, bf16[64,128]{1,0:T(8,128)(2,1)S(1)}, u32[]{:S(2)}, u32[]{:S(2)}) collective-permute-start(bf16[64,128]{1,0:T(8,128)(2,1)S(1)} %collective-permute-done.refs_1_), channel_id=1, source_target_pairs={{0,1},{1,0},{2,3},{3,2},{4,5},{5,4},{6,7},{7,6},{8,9},{9,8},{10,11... | collective-permute-start | bytes 49160 | tf_op jit(solution)/shard_map/ppermute | solution.py:22
  6.8 5.9 %collective-permute-start.6 = (bf16[192,4096]{1,0:T(8,128)(2,1)}, bf16[192,4096]{1,0:T(8,128)(2,1)S(1)}, u32[]{:S(2)}, u32[]{:S(2)}) collective-permute-start(bf16[192,4096]{1,0:T(8,128)(2,1)} %bitcast.12), channel_id=1, source_target_pairs={{0,1},{1,0},{2,3},{3,2},{4,5},{5,4},{6,7},{7,6},{8,9},{9,8},{10,11... | collective-permute-start | bytes 4718600 | tf_op jit(solution)/shard_map/ppermute | solution.py:22
  7.2 8.7 %collective-permute-start.7 = (bf16[192,4096]{1,0:T(8,128)(2,1)}, bf16[192,4096]{1,0:T(8,128)(2,1)S(1)}, u32[]{:S(2)}, u32[]{:S(2)}) collective-permute-start(bf16[192,4096]{1,0:T(8,128)(2,1)} %bitcast.14), channel_id=1, source_target_pairs={{0,1},{1,0},{2,3},{3,2},{4,5},{5,4},{6,7},{7,6},{8,9},{9,8},{10,11... | collective-permute-start | bytes 4718600 | tf_op jit(solution)/shard_map/ppermute | solution.py:22
  7.4 12.0 %collective-permute-start.8 = (bf16[192,4096]{1,0:T(8,128)(2,1)}, bf16[192,4096]{1,0:T(8,128)(2,1)S(1)}, u32[]{:S(2)}, u32[]{:S(2)}) collective-permute-start(bf16[192,4096]{1,0:T(8,128)(2,1)} %bitcast.16), channel_id=1, source_target_pairs={{0,1},{1,0},{2,3},{3,2},{4,5},{5,4},{6,7},{7,6},{8,9},{9,8},{10,11... | collective-permute-start | bytes 4718600 | tf_op jit(solution)/shard_map/ppermute | solution.py:22
  9.6 7.2 %collective-permute-start.5 = (bf16[16,4224]{1,0:T(8,128)(2,1)S(1)}, bf16[16,4224]{1,0:T(8,128)(2,1)S(1)}, u32[]{:S(2)}, u32[]{:S(2)}) collective-permute-start(bf16[16,4224]{1,0:T(8,128)(2,1)S(1)} %pad_maximum_fusion.refs_3_), channel_id=1, source_target_pairs={{0,4},{1,3},{2,6},{3,1},{4,0},{5,7},{6,2},{7,5},{8,12},{9,11},{10,... | collective-permute-start | bytes 405512 | tf_op jit(solution)/shard_map/ppermute | solution.py:32
  11.2 6.2 %collective-permute-start.4 = (bf16[16,4224]{1,0:T(8,128)(2,1)S(1)}, bf16[16,4224]{1,0:T(8,128)(2,1)S(1)}, u32[]{:S(2)}, u32[]{:S(2)}) collective-permute-start(bf16[16,4224]{1,0:T(8,128)(2,1)S(1)} %pad_maximum_fusion.refs_3_), channel_id=1, source_target_pairs={{0,2},{1,5},{2,0},{3,7},{4,6},{5,1},{6,4},{7,3},{8,10},{9,13},{10,... | collective-permute-start | bytes 405512 | tf_op jit(solution)/shard_map/ppermute | solution.py:32
  12.7 6.7 %collective-permute-start.3 = (bf16[16,4224]{1,0:T(8,128)(2,1)S(1)}, bf16[16,4224]{1,0:T(8,128)(2,1)S(1)}, u32[]{:S(2)}, u32[]{:S(2)}) collective-permute-start(bf16[16,4224]{1,0:T(8,128)(2,1)S(1)} %pad_maximum_fusion.refs_3_), channel_id=1, source_target_pairs={{0,6},{1,7},{2,4},{3,5},{4,2},{5,3},{6,0},{7,1},{8,14},{9,15},{10,... | collective-permute-start | bytes 405512 | tf_op jit(solution)/shard_map/ppermute | solution.py:32
  16.0 3.4 %copy-start.1 = (f32[4096]{0:T(1024)S(1)}, f32[4096]{0:T(1024)}, u32[]{:S(2)}) copy-start(f32[4096]{0:T(1024)} %param.14) | copy-start | bytes 49156
  21.1 4.1 %collective-permute-start.9 = (bf16[2,4096]{1,0:T(2,128)(2,1)S(1)}, bf16[2,4096]{1,0:T(2,128)(2,1)S(1)}, u32[]{:S(2)}, u32[]{:S(2)}) collective-permute-start(bf16[2,4096]{1,0:T(2,128)(2,1)S(1)} %get-tuple-element.46), channel_id=1, source_target_pairs={{0,7},{1,6},{2,5},{3,4},{4,3},{5,2},{6,1},{7,0},{8,15},{9,14},{10,... | collective-permute-start | bytes 49160 | tf_op jit(solution)/shard_map/ppermute | solution.py:32
  21.2 4.1 %collective-permute-start.11 = (bf16[2,4096]{1,0:T(2,128)(2,1)S(1)}, bf16[2,4096]{1,0:T(2,128)(2,1)S(1)}, u32[]{:S(2)}, u32[]{:S(2)}) collective-permute-start(bf16[2,4096]{1,0:T(2,128)(2,1)S(1)} %get-tuple-element.47), channel_id=1, source_target_pairs={{0,4},{1,3},{2,6},{3,1},{4,0},{5,7},{6,2},{7,5},{8,12},{9,11},{10,... | collective-permute-start | bytes 49160 | tf_op jit(solution)/shard_map/ppermute | solution.py:32
  22.7 3.7 %collective-permute-start.12 = (bf16[2,4096]{1,0:T(2,128)(2,1)S(1)}, bf16[2,4096]{1,0:T(2,128)(2,1)S(1)}, u32[]{:S(2)}, u32[]{:S(2)}) collective-permute-start(bf16[2,4096]{1,0:T(2,128)(2,1)S(1)} %get-tuple-element.48), channel_id=1, source_target_pairs={{0,2},{1,5},{2,0},{3,7},{4,6},{5,1},{6,4},{7,3},{8,10},{9,13},{10,... | collective-permute-start | bytes 49160 | tf_op jit(solution)/shard_map/ppermute | solution.py:32
  25.3 1.2 %collective-permute-start.10 = (bf16[2,4096]{1,0:T(2,128)(2,1)S(1)}, bf16[2,4096]{1,0:T(2,128)(2,1)S(1)}, u32[]{:S(2)}, u32[]{:S(2)}) collective-permute-start(bf16[2,4096]{1,0:T(2,128)(2,1)S(1)} %collective-permute-done.9), channel_id=1, source_target_pairs={{0,1},{1,0},{2,3},{3,2},{4,5},{5,4},{6,7},{7,6},{8,9},{9,8},{10,11... | collective-permute-start | bytes 49160 | tf_op jit(solution)/shard_map/ppermute | solution.py:22

commit v9 on v8

--- a/solution.py
+++ b/solution.py
@@ -33,10 +33,8 @@
 
 
 def by_distance(size):
-    bits = size.bit_length() - 1
-    mirror = [sum((m >> i & 1) << (bits - 1 - i) for i in range(bits)) for m in range(size)]
     far_first = sorted(range(1, size), key=lambda m: (-m.bit_count(), -m))
-    return [(0, 0)] + [(m, mirror[m]) for m in far_first]
+    return [(0, 0)] + [(m, m) for m in far_first]
 
 
 def gather_ctx(x):

time: 27.5 us -> 27.5 us (level)
  no operation moved by 1% of the time
where the time goes in v9:
time: 27.5 us; the launch traced here: 27.3 us
  starting transfers between devices  12.8 us (47%)
  Pallas kernels  8.42 us (31%)
  waiting for transfers between devices  5.54 us (20%)
  matrix products  0.4 us (1%)
    ppermute x8, starting transfers between devices, swap_by_core(): return lax.ppermute(x, (axis, 'tp'), pairs)  11.8 us
    pallas_call x7, Pallas kernels, call(): pl.pallas_call(kernel, out_shape=[kept(shape, dtype) for shape, dtype in...  8.42 us
    ppermute x8, waiting for transfers between devices, swap_by_core(): return lax.ppermute(x, (axis, 'tp'), pairs)  5.53 us
    ppermute x5, starting transfers between devices, swap(): return lax.ppermute(x, axis, [(i, i ^ mask) for i in range(size)])  1.02 us
  transfers between devices with their start and end apart: 13, of which 5 were waited for; matrix products, arithmetic and copies ran while one was open for 2% of the time, Pallas kernels for 18%

profile of v9, /device:TPU:0, one launch (start us, length us, event | category | flops | bytes accessed | tf_op | source)
XLA Modules:
  0.0 27.3 jit_solution(13934654071746634307)
XLA Ops:
  0.0 1.0 %open.1.refs_0_ = bf16[64,128]{1,0:T(8,128)(2,1)S(1)} custom-call(bf16[32,4,128]{2,1,0:T(4,128)(2,1)} %key_hbm.1, bf16[32,4,128]{2,1,0:T(4,128)(2,1)} %value_hbm.1), custom_call_target="tpu_custom_call" | custom-call | tf_op jit(solution)/shard_map/open/pallas_call | solution.py:58
  1.0 3.1 %collective-permute-start = (bf16[64,128]{1,0:T(8,128)(2,1)S(1)}, bf16[64,128]{1,0:T(8,128)(2,1)S(1)}, u32[]{:S(2)}, u32[]{:S(2)}) collective-permute-start(bf16[64,128]{1,0:T(8,128)(2,1)S(1)} %open.1.refs_0_), channel_id=1, source_target_pairs={{0,8},{1,25},{8,0},{9,17},{16,24},{17,9},{24,16},{25,1},{2,10},{3,... | collective-permute-start | bytes 49160 | tf_op jit(solution)/shard_map/ppermute | solution.py:32
  4.1 2.6 %collective-permute-start.2 = (bf16[64,128]{1,0:T(8,128)(2,1)S(1)}, bf16[64,128]{1,0:T(8,128)(2,1)S(1)}, u32[]{:S(2)}, u32[]{:S(2)}) collective-permute-start(bf16[64,128]{1,0:T(8,128)(2,1)S(1)} %open.1.refs_0_), channel_id=1, source_target_pairs={{0,16},{1,17},{8,24},{9,25},{16,0},{17,1},{24,8},{25,9},{2,18},{3,... | collective-permute-start | bytes 49160 | tf_op jit(solution)/shard_map/ppermute | solution.py:32
  6.7 0.0 collective-permute-done.refs_1_
  6.7 0.1 collective-permute-start.1
  6.8 0.4 %collective-permute-start.6 = (bf16[192,4096]{1,0:T(8,128)(2,1)}, bf16[192,4096]{1,0:T(8,128)(2,1)S(1)}, u32[]{:S(2)}, u32[]{:S(2)}) collective-permute-start(bf16[192,4096]{1,0:T(8,128)(2,1)} %bitcast.12), channel_id=1, source_target_pairs={{0,1},{1,0},{2,3},{3,2},{4,5},{5,4},{6,7},{7,6},{8,9},{9,8},{10,11... | collective-permute-start | bytes 4718600 | tf_op jit(solution)/shard_map/ppermute | solution.py:22
  7.2 0.1 collective-permute-start.7
  7.4 0.4 %collective-permute-start.8 = (bf16[192,4096]{1,0:T(8,128)(2,1)}, bf16[192,4096]{1,0:T(8,128)(2,1)S(1)}, u32[]{:S(2)}, u32[]{:S(2)}) collective-permute-start(bf16[192,4096]{1,0:T(8,128)(2,1)} %bitcast.16), channel_id=1, source_target_pairs={{0,1},{1,0},{2,3},{3,2},{4,5},{5,4},{6,7},{7,6},{8,9},{9,8},{10,11... | collective-permute-start | bytes 4718600 | tf_op jit(solution)/shard_map/ppermute | solution.py:22
  7.8 0.8 %route.1 = (bf16[32,128]{1,0:T(8,128)(2,1)S(1)}, bf16[16,128]{1,0:T(8,128)(2,1)S(1)}, f32[4,128]{1,0:T(4,128)S(1)}, f32[32,128]{1,0:T(8,128)S(1)}) custom-call(bf16[16,2,128]{2,1,0:T(2,128)(2,1)} %bitcast.18, s32[4,8]{1,0:T(4,128)} %refs_1_, f32[4,8]{1,0:T(4,128)} %refs_2_), custom_call_target="tpu_custom_call" | custom-call | tf_op jit(solution)/shard_map/route/pallas_call | solution.py:58
  8.6 0.2 collective-permute-done.2.refs_3_
  8.9 0.0 collective-permute-done.1.refs_2_
  8.9 0.3 %attend.1 = bf16[16,256]{1,0:T(8,128)(2,1)S(1)} custom-call(bf16[32,128]{1,0:T(8,128)(2,1)S(1)} %get-tuple-element.31.q_ref, f32[32,128]{1,0:T(8,128)S(1)} %get-tuple-element.32.allowed_ref, bf16[64,128]{1,0:T(8,128)(2,1)S(1)} %open.1.refs_0_, bf16[64,128]{1,0:T(8,128)(2,1)S(1)} %collective-permute-done.refs_1_, ...), custom_call_target="tpu_custom_call" | custom-call | flops 10000000000 | tf_op jit(solution)/shard_map/attend/pallas_call | solution.py:58
  9.2 0.4 %convolution_convert_fusion = bf16[16,4096]{1,0:T(8,128)(2,1)S(1)} fusion(bf16[16,256]{1,0:T(8,128)(2,1)S(1)} %attend.1, bf16[256,4096]{1,0:T(8,128)(2,1)S(1)} %copy-done), kind=kOutput, calls=%fused_computation | convolution fusion | flops 33619968 | bytes 2236416 | tf_op jit(solution)/shard_map/dot_general | solution.py:301
  9.6 1.6 %collective-permute-start.5 = (bf16[16,4224]{1,0:T(8,128)(2,1)S(1)}, bf16[16,4224]{1,0:T(8,128)(2,1)S(1)}, u32[]{:S(2)}, u32[]{:S(2)}) collective-permute-start(bf16[16,4224]{1,0:T(8,128)(2,1)S(1)} %pad_maximum_fusion.refs_3_), channel_id=1, source_target_pairs={{0,4},{1,3},{2,6},{3,1},{4,0},{5,7},{6,2},{7,5},{8,12},{9,11},{10,... | collective-permute-start | bytes 405512 | tf_op jit(solution)/shard_map/ppermute | solution.py:32
  11.2 1.5 %collective-permute-start.4 = (bf16[16,4224]{1,0:T(8,128)(2,1)S(1)}, bf16[16,4224]{1,0:T(8,128)(2,1)S(1)}, u32[]{:S(2)}, u32[]{:S(2)}) collective-permute-start(bf16[16,4224]{1,0:T(8,128)(2,1)S(1)} %pad_maximum_fusion.refs_3_), channel_id=1, source_target_pairs={{0,2},{1,5},{2,0},{3,7},{4,6},{5,1},{6,4},{7,3},{8,10},{9,13},{10,... | collective-permute-start | bytes 405512 | tf_op jit(solution)/shard_map/ppermute | solution.py:32
  12.7 0.0 collective-permute-done.6.gate_ref
  12.7 0.5 %collective-permute-start.3 = (bf16[16,4224]{1,0:T(8,128)(2,1)S(1)}, bf16[16,4224]{1,0:T(8,128)(2,1)S(1)}, u32[]{:S(2)}, u32[]{:S(2)}) collective-permute-start(bf16[16,4224]{1,0:T(8,128)(2,1)S(1)} %pad_maximum_fusion.refs_3_), channel_id=1, source_target_pairs={{0,6},{1,7},{2,4},{3,5},{4,2},{5,3},{6,0},{7,1},{8,14},{9,15},{10,... | collective-permute-start | bytes 405512 | tf_op jit(solution)/shard_map/ppermute | solution.py:32
  13.2 2.8 %load.1 = (bf16[4096,384]{1,0:T(8,128)(2,1)S(1)}, bf16[192,4096]{1,0:T(8,128)(2,1)S(1)}) custom-call(bf16[192,4096]{1,0:T(8,128)(2,1)} %bitcast.13, bf16[192,4096]{1,0:T(8,128)(2,1)} %bitcast.15, bf16[192,4096]{1,0:T(8,128)(2,1)} %bitcast.17), custom_call_target="tpu_custom_call" | custom-call | bytes 4718592 | tf_op jit(solution)/shard_map/load/pallas_call | solution.py:58
  16.0 0.0 copy-start.1
  16.0 0.0 collective-permute-done.7.up_ref
  16.0 0.9 %turn.1.refs_7_ = bf16[4096,384]{1,0:T(8,128)(2,1)S(1)} custom-call(bf16[192,4096]{1,0:T(8,128)(2,1)S(1)} %collective-permute-done.6.gate_ref, bf16[192,4096]{1,0:T(8,128)(2,1)S(1)} %collective-permute-done.7.up_ref), custom_call_target="tpu_custom_call" | custom-call | bytes 3145728 | tf_op jit(solution)/shard_map/turn/pallas_call | solution.py:58
  16.9 0.5 %collective-permute-done.4.refs_1_ = bf16[16,4224]{1,0:T(8,128)(2,1)S(1)} collective-permute-done((bf16[16,4224]{1,0:T(8,128)(2,1)S(1)}, bf16[16,4224]{1,0:T(8,128)(2,1)S(1)}, u32[]{:S(2)}, u32[]{:S(2)}) %collective-permute-start.4) | collective-permute-done | bytes 135200 | tf_op jit(solution)/shard_map/ppermute | solution.py:32
  17.4 2.0 %collective-permute-done.3.refs_0_ = bf16[16,4224]{1,0:T(8,128)(2,1)S(1)} collective-permute-done((bf16[16,4224]{1,0:T(8,128)(2,1)S(1)}, bf16[16,4224]{1,0:T(8,128)(2,1)S(1)}, u32[]{:S(2)}, u32[]{:S(2)}) %collective-permute-start.3) | collective-permute-done | bytes 135200 | tf_op jit(solution)/shard_map/ppermute | solution.py:32
  19.4 0.0 collective-permute-done.8.refs_8_
  19.4 1.7 %experts.1 = (f32[4,4096]{1,0:T(4,128)S(1)}, bf16[2,4096]{1,0:T(2,128)(2,1)S(1)}, bf16[2,4096]{1,0:T(2,128)(2,1)S(1)}, bf16[2,4096]{1,0:T(2,128)(2,1)S(1)}, bf16[2,4096]{1,0:T(2,128)(2,1)S(1)}) custom-call(bf16[16,4224]{1,0:T(8,128)(2,1)S(1)} %collective-permute-done.3.refs_0_, bf16[16,4224]{1,0:T(8,128)(2,1)S(1)} %collective-permute-done.4.refs_1_, ...), custom_call_target="tpu_custom_call" | custom-call | flops 75497472 | bytes 9437184 | tf_op jit(solution)/shard_map/experts/pallas_call | solution.py:58
  21.1 0.1 collective-permute-start.9
  21.2 1.5 %collective-permute-start.11 = (bf16[2,4096]{1,0:T(2,128)(2,1)S(1)}, bf16[2,4096]{1,0:T(2,128)(2,1)S(1)}, u32[]{:S(2)}, u32[]{:S(2)}) collective-permute-start(bf16[2,4096]{1,0:T(2,128)(2,1)S(1)} %get-tuple-element.47), channel_id=1, source_target_pairs={{0,4},{1,5},{2,6},{3,7},{4,0},{5,1},{6,2},{7,3},{8,12},{9,13},{10,... | collective-permute-start | bytes 49160 | tf_op jit(solution)/shard_map/ppermute | solution.py:32
  22.7 1.0 %collective-permute-start.12 = (bf16[2,4096]{1,0:T(2,128)(2,1)S(1)}, bf16[2,4096]{1,0:T(2,128)(2,1)S(1)}, u32[]{:S(2)}, u32[]{:S(2)}) collective-permute-start(bf16[2,4096]{1,0:T(2,128)(2,1)S(1)} %get-tuple-element.48), channel_id=1, source_target_pairs={{0,2},{1,3},{2,0},{3,1},{4,6},{5,7},{6,4},{7,5},{8,10},{9,11},{10,... | collective-permute-start | bytes 49160 | tf_op jit(solution)/shard_map/ppermute | solution.py:32
  23.7 1.6 %collective-permute-done.9 = bf16[2,4096]{1,0:T(2,128)(2,1)S(1)} collective-permute-done((bf16[2,4096]{1,0:T(2,128)(2,1)S(1)}, bf16[2,4096]{1,0:T(2,128)(2,1)S(1)}, u32[]{:S(2)}, u32[]{:S(2)}) %collective-permute-start.9) | collective-permute-done | bytes 16416 | tf_op jit(solution)/shard_map/ppermute | solution.py:32
  25.2 0.0 collective-permute-start.10
  25.3 1.2 %collective-permute-done.12.refs_3_ = bf16[2,4096]{1,0:T(2,128)(2,1)S(1)} collective-permute-done((bf16[2,4096]{1,0:T(2,128)(2,1)S(1)}, bf16[2,4096]{1,0:T(2,128)(2,1)S(1)}, u32[]{:S(2)}, u32[]{:S(2)}) %collective-permute-start.12) | collective-permute-done | bytes 16416 | tf_op jit(solution)/shard_map/ppermute | solution.py:32
  26.5 0.8 %combine.1 = bf16[4,4096]{1,0:T(4,128)(2,1)} custom-call(f32[4,128]{1,0:T(4,128)S(1)} %get-tuple-element.30.mix_ref, f32[4,4096]{1,0:T(4,128)S(1)} %get-tuple-element.44.own_ref, bf16[2,4096]{1,0:T(2,128)(2,1)S(1)} %get-tuple-element.45.refs_0_, bf16[2,4096]{1,0:T(2,128)(2,1)S(1)} %collective-permute-done.10.refs_1_, ...), custom_call_target="tpu_custom_call" | custom-call | tf_op jit(solution)/shard_map/combine/pallas_call | solution.py:58
  (7 shorter events, 0.0 us)
Async XLA Ops:
  0.0 9.2 %copy-start = (bf16[256,4096]{1,0:T(8,128)(2,1)S(1)}, bf16[256,4096]{1,0:T(8,128)(2,1)}, u32[]{:S(2)}) copy-start(bf16[256,4096]{1,0:T(8,128)(2,1)} %param.13) | copy-start | bytes 6291460
  1.0 5.7 %collective-permute-start = (bf16[64,128]{1,0:T(8,128)(2,1)S(1)}, bf16[64,128]{1,0:T(8,128)(2,1)S(1)}, u32[]{:S(2)}, u32[]{:S(2)}) collective-permute-start(bf16[64,128]{1,0:T(8,128)(2,1)S(1)} %open.1.refs_0_), channel_id=1, source_target_pairs={{0,8},{1,25},{8,0},{9,17},{16,24},{17,9},{24,16},{25,1},{2,10},{3,... | collective-permute-start | bytes 49160 | tf_op jit(solution)/shard_map/ppermute | solution.py:32
  4.1 4.7 %collective-permute-start.2 = (bf16[64,128]{1,0:T(8,128)(2,1)S(1)}, bf16[64,128]{1,0:T(8,128)(2,1)S(1)}, u32[]{:S(2)}, u32[]{:S(2)}) collective-permute-start(bf16[64,128]{1,0:T(8,128)(2,1)S(1)} %open.1.refs_0_), channel_id=1, source_target_pairs={{0,16},{1,17},{8,24},{9,25},{16,0},{17,1},{24,8},{25,9},{2,18},{3,... | collective-permute-start | bytes 49160 | tf_op jit(solution)/shard_map/ppermute | solution.py:32
  6.7 2.1 %collective-permute-start.1 = (bf16[64,128]{1,0:T(8,128)(2,1)S(1)}, bf16[64,128]{1,0:T(8,128)(2,1)S(1)}, u32[]{:S(2)}, u32[]{:S(2)}) collective-permute-start(bf16[64,128]{1,0:T(8,128)(2,1)S(1)} %collective-permute-done.refs_1_), channel_id=1, source_target_pairs={{0,1},{1,0},{2,3},{3,2},{4,5},{5,4},{6,7},{7,6},{8,9},{9,8},{10,11... | collective-permute-start | bytes 49160 | tf_op jit(solution)/shard_map/ppermute | solution.py:22
  6.8 5.9 %collective-permute-start.6 = (bf16[192,4096]{1,0:T(8,128)(2,1)}, bf16[192,4096]{1,0:T(8,128)(2,1)S(1)}, u32[]{:S(2)}, u32[]{:S(2)}) collective-permute-start(bf16[192,4096]{1,0:T(8,128)(2,1)} %bitcast.12), channel_id=1, source_target_pairs={{0,1},{1,0},{2,3},{3,2},{4,5},{5,4},{6,7},{7,6},{8,9},{9,8},{10,11... | collective-permute-start | bytes 4718600 | tf_op jit(solution)/shard_map/ppermute | solution.py:22
  7.2 8.7 %collective-permute-start.7 = (bf16[192,4096]{1,0:T(8,128)(2,1)}, bf16[192,4096]{1,0:T(8,128)(2,1)S(1)}, u32[]{:S(2)}, u32[]{:S(2)}) collective-permute-start(bf16[192,4096]{1,0:T(8,128)(2,1)} %bitcast.14), channel_id=1, source_target_pairs={{0,1},{1,0},{2,3},{3,2},{4,5},{5,4},{6,7},{7,6},{8,9},{9,8},{10,11... | collective-permute-start | bytes 4718600 | tf_op jit(solution)/shard_map/ppermute | solution.py:22
  7.4 12.0 %collective-permute-start.8 = (bf16[192,4096]{1,0:T(8,128)(2,1)}, bf16[192,4096]{1,0:T(8,128)(2,1)S(1)}, u32[]{:S(2)}, u32[]{:S(2)}) collective-permute-start(bf16[192,4096]{1,0:T(8,128)(2,1)} %bitcast.16), channel_id=1, source_target_pairs={{0,1},{1,0},{2,3},{3,2},{4,5},{5,4},{6,7},{7,6},{8,9},{9,8},{10,11... | collective-permute-start | bytes 4718600 | tf_op jit(solution)/shard_map/ppermute | solution.py:22
  9.6 7.2 %collective-permute-start.5 = (bf16[16,4224]{1,0:T(8,128)(2,1)S(1)}, bf16[16,4224]{1,0:T(8,128)(2,1)S(1)}, u32[]{:S(2)}, u32[]{:S(2)}) collective-permute-start(bf16[16,4224]{1,0:T(8,128)(2,1)S(1)} %pad_maximum_fusion.refs_3_), channel_id=1, source_target_pairs={{0,4},{1,3},{2,6},{3,1},{4,0},{5,7},{6,2},{7,5},{8,12},{9,11},{10,... | collective-permute-start | bytes 405512 | tf_op jit(solution)/shard_map/ppermute | solution.py:32
  11.2 6.2 %collective-permute-start.4 = (bf16[16,4224]{1,0:T(8,128)(2,1)S(1)}, bf16[16,4224]{1,0:T(8,128)(2,1)S(1)}, u32[]{:S(2)}, u32[]{:S(2)}) collective-permute-start(bf16[16,4224]{1,0:T(8,128)(2,1)S(1)} %pad_maximum_fusion.refs_3_), channel_id=1, source_target_pairs={{0,2},{1,5},{2,0},{3,7},{4,6},{5,1},{6,4},{7,3},{8,10},{9,13},{10,... | collective-permute-start | bytes 405512 | tf_op jit(solution)/shard_map/ppermute | solution.py:32
  12.7 6.7 %collective-permute-start.3 = (bf16[16,4224]{1,0:T(8,128)(2,1)S(1)}, bf16[16,4224]{1,0:T(8,128)(2,1)S(1)}, u32[]{:S(2)}, u32[]{:S(2)}) collective-permute-start(bf16[16,4224]{1,0:T(8,128)(2,1)S(1)} %pad_maximum_fusion.refs_3_), channel_id=1, source_target_pairs={{0,6},{1,7},{2,4},{3,5},{4,2},{5,3},{6,0},{7,1},{8,14},{9,15},{10,... | collective-permute-start | bytes 405512 | tf_op jit(solution)/shard_map/ppermute | solution.py:32
  16.0 3.4 %copy-start.1 = (f32[4096]{0:T(1024)S(1)}, f32[4096]{0:T(1024)}, u32[]{:S(2)}) copy-start(f32[4096]{0:T(1024)} %param.14) | copy-start | bytes 49156
  21.1 4.1 %collective-permute-start.9 = (bf16[2,4096]{1,0:T(2,128)(2,1)S(1)}, bf16[2,4096]{1,0:T(2,128)(2,1)S(1)}, u32[]{:S(2)}, u32[]{:S(2)}) collective-permute-start(bf16[2,4096]{1,0:T(2,128)(2,1)S(1)} %get-tuple-element.46), channel_id=1, source_target_pairs={{0,7},{1,6},{2,5},{3,4},{4,3},{5,2},{6,1},{7,0},{8,15},{9,14},{10,... | collective-permute-start | bytes 49160 | tf_op jit(solution)/shard_map/ppermute | solution.py:32
  21.2 4.1 %collective-permute-start.11 = (bf16[2,4096]{1,0:T(2,128)(2,1)S(1)}, bf16[2,4096]{1,0:T(2,128)(2,1)S(1)}, u32[]{:S(2)}, u32[]{:S(2)}) collective-permute-start(bf16[2,4096]{1,0:T(2,128)(2,1)S(1)} %get-tuple-element.47), channel_id=1, source_target_pairs={{0,4},{1,5},{2,6},{3,7},{4,0},{5,1},{6,2},{7,3},{8,12},{9,13},{10,... | collective-permute-start | bytes 49160 | tf_op jit(solution)/shard_map/ppermute | solution.py:32
  22.7 3.7 %collective-permute-start.12 = (bf16[2,4096]{1,0:T(2,128)(2,1)S(1)}, bf16[2,4096]{1,0:T(2,128)(2,1)S(1)}, u32[]{:S(2)}, u32[]{:S(2)}) collective-permute-start(bf16[2,4096]{1,0:T(2,128)(2,1)S(1)} %get-tuple-element.48), channel_id=1, source_target_pairs={{0,2},{1,3},{2,0},{3,1},{4,6},{5,7},{6,4},{7,5},{8,10},{9,11},{10,... | collective-permute-start | bytes 49160 | tf_op jit(solution)/shard_map/ppermute | solution.py:32
  25.2 1.2 %collective-permute-start.10 = (bf16[2,4096]{1,0:T(2,128)(2,1)S(1)}, bf16[2,4096]{1,0:T(2,128)(2,1)S(1)}, u32[]{:S(2)}, u32[]{:S(2)}) collective-permute-start(bf16[2,4096]{1,0:T(2,128)(2,1)S(1)} %collective-permute-done.9), channel_id=1, source_target_pairs={{0,1},{1,0},{2,3},{3,2},{4,5},{5,4},{6,7},{7,6},{8,9},{9,8},{10,11... | collective-permute-start | bytes 49160 | tf_op jit(solution)/shard_map/ppermute | solution.py:22
